TPU v7x, 512 devices: a whole 4x8x8 slice. The times are simulated.
512 devices in a mesh: shot: 32 (over y_lo, x, core), pair: 16 (over y_hi, z).
Axes of the slice: x: 4, y: 8 (y_hi: 2, y_lo: 4; y = y_hi * 4 + y_lo), z: 8, core: 2. Of those that a mesh axis runs over, the one named last changes fastest.
Arguments:
- spectra: bfloat16 [2, 512, 128, 1024], P(None, 'shot', None, 'pair'), may hold values from -6 to 6
- shot_weight: float32 [512], P('shot'), may hold values from 0.5 to 2
Outputs:
- virtual_gather: bfloat16 [2, 128, 1024, 1024], P(None, 'shot', 'pair')
All inputs are finite; a program needn't handle non-finite values.
Results may differ from a plain program's by a relative error of at most 0.0054.
Values may be sent and summed in bfloat16 or wider, within the bound.
No kernel may reach another device: no remote copies, remote signals or barrier semaphores. Data moves between devices by JAX's collectives and lax.ppermute only.
A program may use at most 64 MiB of HBM per device.

v0:
```python
import jax
import jax.numpy as jnp
from jax import lax
from jax.sharding import PartitionSpec as P


def gram_block(row_data, column_data, factor):
    swapped = jnp.stack([-row_data[1], row_data[0]])
    left_side = jnp.stack([row_data, swapped])
    product = jnp.einsum(
        "ocsfa,csfb->ofab", left_side, column_data, preferred_element_type=jnp.float32
    )
    return product * factor


def shards(spectra, shot_weight):
    scaled = (spectra.astype(jnp.float32) * shot_weight[None, :, None, None]).astype(jnp.bfloat16)
    by_freq = lax.all_to_all(scaled, "shot", split_axis=2, concat_axis=1, tiled=True)
    total_shots = by_freq.shape[1]
    factor = total_shots ** (-0.5)
    local_bins = by_freq.shape[2]
    row_width = by_freq.shape[3]
    gathered = lax.all_gather(by_freq, "pair", axis=3, tiled=True)
    device_count = lax.axis_size("pair")
    own_index = lax.axis_index("pair")

    def one_tile(tile_index):
        columns = lax.dynamic_slice_in_dim(gathered, tile_index * row_width, row_width, 3)
        return lax.cond(
            tile_index >= own_index,
            lambda: gram_block(by_freq, columns, factor).astype(jnp.bfloat16),
            lambda: jnp.zeros((2, local_bins, row_width, row_width), jnp.bfloat16),
        )

    tiles = lax.map(one_tile, jnp.arange(device_count, dtype=jnp.int32))
    received = lax.all_to_all(tiles, "pair", split_axis=0, concat_axis=0, tiled=True)
    mirrored = jnp.stack(
        [jnp.swapaxes(received[:, 0], 2, 3), -jnp.swapaxes(received[:, 1], 2, 3)], axis=1
    )
    below_diag = (jnp.arange(device_count, dtype=jnp.int32) < own_index)[:, None, None, None, None]
    merged = jnp.where(below_diag, mirrored, tiles)
    return merged.transpose(1, 2, 3, 0, 4).reshape(
        2, local_bins, row_width, device_count * row_width
    )


def solution(mesh):
    return jax.shard_map(
        shards,
        mesh=mesh,
        in_specs=(P(None, "shot", None, "pair"), P("shot")),
        out_specs=P(None, "shot", "pair", None),
        check_vma=False,
    )
```

profile of v0, /device:TPU:16, one launch (start us, length us, event | category | flops | bytes accessed | tf_op | source)
XLA Modules:
  0.0 356.7 jit_solution(6008609927738838939)
XLA Ops:
  6.5 1.2 multiply_convert_fusion
  7.8 1.6 copy.33
  9.4 0.7 reshape.12
  10.1 23.1 %all_to_all.23 = bf16[32,2,4096]{2,1,0:T(2,128)(2,1)S(1)} all-to-all(bf16[32,2,4096]{2,1,0:T(2,128)(2,1)S(1)} %reshape.12), channel_id=1, replica_groups=mesh['shot'=32,'pair'=16] {'shot'}, dimensions={0} | all-to-all | bytes 1048576 | tf_op jit(solution)/shard_map/all_to_all | solution.py:18
  33.2 0.7 reshape.13
  34.1 1.3 copy.36
  35.8 194.2 %all-gather.2.cloned.1.call-done = bf16[2,512,4,1024]{1,2,0,3:T(4,128)(2,1)} async-done(((bf16[2,512,4,64]{1,2,0,3:T(4,128)(2,1)}), bf16[2,512,4,1024]{1,2,0,3:T(4,128)(2,1)}) %all-gather.2.cloned.1.call-update) | async-done | bytes 8388624 | tf_op jit(solution)/shard_map/all_gather | solution.py:23
  230.0 9.5 %copy.38 = bf16[2,512,4,1024]{1,3,0,2:T(8,128)(2,1)} copy(bf16[2,512,4,1024]{1,2,0,3:T(4,128)(2,1)} %all-gather.2.cloned.1.call-done) | data formatting | bytes 16777216 | tf_op jit(solution)/shard_map/while | solution.py:35
  239.5 56.6 %while.10 = (s32[]{:T(128)}, bf16[16,2,4,64,64]{4,3,1,2,0:T(8,128)(2,1)S(1)}, s32[16]{0:T(128)S(1)}, s32[]{:T(128)}, bf16[2,512,4,64]{1,3,0,2:T(8,128)(2,1)S(1)}, /*index=5*/bf16[2,512,4,1024]{1,3,0,2:T(8,128)(2,1)}, s32[]{:T(128)}) while((s32[]{:T(128)}, bf16[16,2,4,64,64]{4,3,1,2,0:T(8,128)(2,1)S(1)}, s32[16]{0:T(128)S(1)}, s32[]{:T(128)}, ...), condition=%wide.region_3.4_spmd, body=%wide.region_0.3_spmd.sunk | while | flops 68091904 | bytes 3997893 | solution.py:35
  240.7 2.2 conditional.2
  241.5 1.5 fusion.2
  243.1 0.6 dynamic_slice.17
  244.3 2.2 conditional.2
  245.1 1.5 fusion.2
  246.6 0.6 dynamic_slice.17
  247.8 2.2 conditional.2
  248.6 1.5 fusion.2
  250.1 0.6 dynamic_slice.17
  251.4 2.2 conditional.2
  252.1 1.5 fusion.2
  253.7 0.6 dynamic_slice.17
  254.9 2.2 conditional.2
  255.7 1.5 fusion.2
  257.2 0.6 dynamic_slice.17
  258.4 2.2 conditional.2
  259.2 1.5 fusion.2
  260.7 0.6 dynamic_slice.17
  262.0 2.2 conditional.2
  262.8 1.5 fusion.2
  264.3 0.6 dynamic_slice.17
  265.5 2.2 conditional.2
  266.3 1.5 fusion.2
  267.8 0.6 dynamic_slice.17
  269.1 2.2 conditional.2
  269.8 1.5 fusion.2
  271.4 0.6 dynamic_slice.17
  272.6 2.2 conditional.2
  273.4 1.5 fusion.2
  274.9 0.6 dynamic_slice.17
  276.1 2.2 conditional.2
  276.9 1.5 fusion.2
  278.4 0.6 dynamic_slice.17
  279.7 2.2 conditional.2
  280.5 1.5 fusion.2
  282.0 0.6 dynamic_slice.17
  283.2 2.2 conditional.2
  284.0 1.5 fusion.2
  285.5 0.6 dynamic_slice.17
  286.8 2.2 conditional.2
  287.5 1.5 fusion.2
  289.1 0.6 dynamic_slice.17
  290.3 2.2 conditional.2
  291.1 1.5 fusion.2
  292.6 0.6 dynamic_slice.17
  293.8 2.2 conditional.2
  294.6 1.5 fusion.2
  296.1 2.6 copy.39
  298.7 4.6 %reshape.14 = bf16[16,2,16384]{2,1,0:T(2,128)(2,1)} reshape(bf16[16,2,4,64,64]{4,3,2,1,0:T(8,128)(2,1)} %bitcast.54) | data formatting | bytes 2097152
  303.4 4.5 %all-to-all-start.1 = ((bf16[16,2,16384]{2,1,0:T(2,128)(2,1)}), bf16[16,2,16384]{2,1,0:T(2,128)(2,1)}, u32[]{:S(2)}, u32[]{:S(2)}) async-start(bf16[16,2,16384]{2,1,0:T(2,128)(2,1)} %reshape.14), calls=%async_computation.1 | async-start | bytes 2097152 | tf_op jit(solution)/shard_map/all_to_all | solution.py:36
  307.9 31.3 %all-to-all-done.1 = bf16[16,2,16384]{2,1,0:T(2,128)(2,1)} async-done(((bf16[16,2,16384]{2,1,0:T(2,128)(2,1)}), bf16[16,2,16384]{2,1,0:T(2,128)(2,1)}, u32[]{:S(2)}, u32[]{:S(2)}) %all-to-all-start.1) | async-done | bytes 1048608 | tf_op jit(solution)/shard_map/all_to_all | solution.py:36
  339.2 4.7 %reshape.15 = bf16[16,2,4,64,64]{4,3,2,1,0:T(8,128)(2,1)} reshape(bf16[16,2,16384]{2,1,0:T(2,128)(2,1)} %all-to-all-done.1) | data formatting | bytes 2097152
  343.9 1.7 slice_bitcast_fusion
  346.2 1.4 copy.42
  347.6 2.3 reshape.9
  (59 shorter events, 3.5 us)
Async XLA Ops:
  6.5 223.5 %all-gather.2.cloned.1.call-start = ((), (), s32[]{:S(2)}) async-start(), calls=%async_computation.2 | async-start | bytes 8912896 | tf_op jit(solution)/shard_map/all_gather | solution.py:23
  35.8 203.7 %copy-start = (bf16[16,2,4,64,64]{4,3,1,2,0:T(8,128)(2,1)S(1)}, bf16[16,2,4,64,64]{4,3,1,2,0:T(8,128)(2,1)}, u32[]{:S(2)}) copy-start(bf16[16,2,4,64,64]{4,3,1,2,0:T(8,128)(2,1)} %custom-call) | copy-start | bytes 3145732
  303.4 35.8 %all-to-all-start.1 = ((bf16[16,2,16384]{2,1,0:T(2,128)(2,1)}), bf16[16,2,16384]{2,1,0:T(2,128)(2,1)}, u32[]{:S(2)}, u32[]{:S(2)}) async-start(bf16[16,2,16384]{2,1,0:T(2,128)(2,1)} %reshape.14), calls=%async_computation.1 | async-start | bytes 2097152 | tf_op jit(solution)/shard_map/all_to_all | solution.py:36
Sparse Core Ops, SparseCore 0:
  35.6 194.4 all-gather.1
where the time goes:
time: 358 us; the launch traced here: 357 us
  waiting for transfers between devices  226 us (63%)
  local copies, waits for them, and re-layouts  39.7 us (11%)
  matrix products  23.5 us (7%)
  blocking collectives  23.1 us (6%)
  loops' own time  21.9 us (6%)
  between operations  13.5 us (4%)
  other arithmetic  4.96 us (1%)
  starting transfers between devices  4.54 us (1%)
    all_gather x1, waiting for transfers between devices, shards(): gathered = lax.all_gather(by_freq, 'pair', axis=3, tiled=True)  194 us
    all_to_all x1, waiting for transfers between devices, shards(): lax.all_to_all(tiles, 'pair', split_axis=0, concat_axis=0, tiled=True)  31.3 us
    dot_general x16, matrix products, gram_block(): jnp.einsum('ocsfa,csfb->ofab', left_side, column_data, preferred_element_...  23.5 us
    all_to_all x1, blocking collectives, shards(): lax.all_to_all(scaled, 'shot', split_axis=2, concat_axis=1, tiled=True)  23.1 us
    while x3, local copies, waits for them, and re-layouts, shards(): tiles = lax.map(one_tile, jnp.arange(device_count, dtype=jnp.int32))  12.4 us
    another operation x16, loops' own time, one_tile(): lax.cond(tile_index >= own_index, lambda: gram_block(by_freq, columns, fa...  11 us
    another operation x1, loops' own time, shards(): tiles = lax.map(one_tile, jnp.arange(device_count, dtype=jnp.int32))  10.9 us
    unnamed x6, local copies, waits for them, and re-layouts  10.7 us
  transfers between devices with their start and end apart: 2, of which 2 were waited for; matrix products, arithmetic and copies ran while one was open for 0% of the time, Pallas kernels for 0%

commit v1 on v0

v1 whole, which is shorter than its diff:
```python
import functools

import jax
import jax.numpy as jnp
from jax import lax
from jax.experimental import pallas as pl
from jax.experimental.pallas import tpu as pltpu
from jax.sharding import Mesh, PartitionSpec as P

VMEM = pltpu.MemorySpace.VMEM
SMEM = pltpu.MemorySpace.SMEM
PARAMS = pltpu.CompilerParams(vmem_limit_bytes=32 * 1024 * 1024)


def vmem_call(body, out_shape, in_spaces, scratch=(), flops=0, nbytes=0):
    outs = out_shape if isinstance(out_shape, (list, tuple)) else (out_shape,)
    specs = [pl.BlockSpec(memory_space=VMEM) for _ in outs]
    return pl.pallas_call(
        body,
        out_shape=out_shape,
        in_specs=[pl.BlockSpec(memory_space=s) for s in in_spaces],
        out_specs=specs if isinstance(out_shape, (list, tuple)) else specs[0],
        scratch_shapes=list(scratch),
        compiler_params=PARAMS,
        cost_estimate=pl.CostEstimate(flops=flops, bytes_accessed=nbytes, transcendentals=0),
    )


def scale_kernel(weight_ref, x_ref, out_ref, turned):
    _, shots, chans, bins = x_ref.shape
    planes, depth = turned.shape[0], turned.shape[1]
    for s in range(shots):
        block = x_ref[:, s].reshape(2 * chans, bins).astype(jnp.float32) * weight_ref[s]
        block = block.astype(jnp.bfloat16).astype(jnp.float32)
        turned[:, :, s, :] = block.T.reshape(planes, depth, 2 * chans)
    for z in range(depth):
        out_ref[z] = turned[:, z].astype(jnp.bfloat16)


def split_parts(first, second):
    half = first.shape[1] // 2
    p = jnp.concatenate([first[:, :half], second[:, :half]], axis=1)
    q = jnp.concatenate([first[:, half:], second[:, half:]], axis=1)
    return p, q


def fill_right(right, load, k_rows, factor=None):
    width = right.shape[1] // 2
    for h in range(2):
        base = 2 * h * k_rows
        for j in range(width // 128):
            p, q = load(h, j)
            cols = slice(j * 128, (j + 1) * 128)
            icols = slice(width + j * 128, width + (j + 1) * 128)
            right[base:base + k_rows, cols] = p
            right[base:base + k_rows, icols] = q
            right[base + k_rows:base + 2 * k_rows, cols] = q
            right[base + k_rows:base + 2 * k_rows, icols] = -p


def multiply(left_ref, right, out_ref, factor):
    rows = left_ref.shape[0]
    step = 256
    for r in range(rows // step):
        acc = jnp.dot(
            left_ref[r * step:(r + 1) * step, :], right[...], preferred_element_type=jnp.float32
        )
        out_ref[r * step:(r + 1) * step, :] = (acc * factor).astype(jnp.bfloat16)


def own_kernel(factor, core_ref, a_ref, b_ref, out_ref, left_ref, right):
    depth, k_rows, _ = a_ref.shape
    for h, ref in enumerate((a_ref, b_ref)):
        base = 2 * h * k_rows
        for j in range(depth // 2):
            p, q = split_parts(ref[2 * j], ref[2 * j + 1])
            rows = slice(j * 128, (j + 1) * 128)
            left_ref[rows, base:base + k_rows] = p.T
            left_ref[rows, base + k_rows:base + 2 * k_rows] = q.T
    first = core_ref[0] * (depth // 2)

    def load(h, j):
        ref = (a_ref, b_ref)[h]
        return split_parts(ref[first + 2 * j], ref[first + 2 * j + 1])

    fill_right(right, load, k_rows)
    multiply(left_ref, right, out_ref, factor)


def cross_kernel(factor, core_ref, left_ref, y_ref, out_ref, right):
    _, _, k_rows, _ = y_ref.shape
    core = core_ref[0]

    def load(h, j):
        k_half = core if h == 0 else 1 - core
        return split_parts(y_ref[k_half, 2 * j], y_ref[k_half, 2 * j + 1])

    fill_right(right, load, k_rows)
    multiply(left_ref, right, out_ref, factor)


def assemble_kernel(yh_ref, own_ref, cross_ref, out_ref):
    width = own_ref.shape[3] // 2

    def place(ref, half):
        for part in range(2):
            for quarter in range(2):
                at = (2 * half + quarter) * width
                out_ref[part, :, :, at:at + width] = ref[quarter, :, :, part * width:(part + 1) * width]

    @pl.when(yh_ref[0] == 0)
    def _():
        place(own_ref, 0)
        place(cross_ref, 1)

    @pl.when(yh_ref[0] != 0)
    def _():
        place(own_ref, 1)
        place(cross_ref, 0)


SWAP = [(0, 1), (1, 0)]


def shards(spectra, shot_weight):
    _, shots, bins, chans = spectra.shape
    depth = lax.axis_size("z")
    planes = lax.axis_size("y") * lax.axis_size("x")
    cores = lax.axis_size("c")
    factor = (shots * planes * cores) ** (-0.5)
    core = lax.axis_index("c").astype(jnp.int32).reshape(1)
    yh = lax.axis_index("yh").astype(jnp.int32).reshape(1)
    lanes = 2 * chans
    k_rows = planes * shots
    rows = depth * chans
    width = 2 * (rows // 2)

    turned = jnp.swapaxes(spectra, 2, 3)
    scaled = vmem_call(
        scale_kernel,
        jax.ShapeDtypeStruct((depth, planes, shots, lanes), jnp.bfloat16),
        [SMEM, VMEM],
        [pltpu.VMEM((planes, depth, shots, lanes), jnp.float32)],
        nbytes=2 * spectra.size * 2,
    )(shot_weight, turned)
    scaled = scaled.reshape(bins, shots, lanes)
    mine = lax.all_to_all(scaled, ("z", "y", "x"), 0, 0, tiled=True)
    far = lax.ppermute(mine, "yh", SWAP)
    near = lax.ppermute(mine, "c", SWAP)

    flops = 2 * rows * 4 * k_rows * width
    own, left = vmem_call(
        functools.partial(own_kernel, factor),
        (
            jax.ShapeDtypeStruct((rows, width), jnp.bfloat16),
            jax.ShapeDtypeStruct((rows, 4 * k_rows), jnp.bfloat16),
        ),
        [SMEM, VMEM, VMEM],
        [pltpu.VMEM((4 * k_rows, width), jnp.bfloat16)],
        flops=flops,
        nbytes=4 * rows * width * 2,
    )(core, mine.reshape(depth, k_rows, lanes), near.reshape(depth, k_rows, lanes))
    own = lax.all_to_all(own, "z", 0, 0, tiled=True)
    own = lax.all_to_all(own, "c", 0, 0, tiled=True)

    far = lax.all_to_all(far, "c", 0, 0, tiled=True)
    cross = vmem_call(
        functools.partial(cross_kernel, factor),
        jax.ShapeDtypeStruct((rows, width), jnp.bfloat16),
        [SMEM, VMEM, VMEM],
        [pltpu.VMEM((4 * k_rows, width), jnp.bfloat16)],
        flops=flops,
        nbytes=4 * rows * width * 2,
    )(core, left, far.reshape(cores, depth // 2, k_rows, lanes))
    cross = lax.all_to_all(cross, "z", 0, 0, tiled=True)
    cross = lax.all_to_all(cross, "c", 0, 0, tiled=True)

    per = depth // cores
    shape = (cores, per, chans, width)
    return vmem_call(
        assemble_kernel,
        jax.ShapeDtypeStruct((2, per, chans, 2 * rows), jnp.bfloat16),
        [SMEM, VMEM, VMEM],
        nbytes=4 * rows * width * 2,
    )(yh, own.reshape(shape), cross.reshape(shape))


def solution(mesh):
    fine = Mesh(mesh.devices.reshape(4, 4, 2, 2, 8), ("y", "x", "c", "yh", "z"))
    shot, pair = ("y", "x", "c"), ("yh", "z")
    return jax.shard_map(
        shards,
        mesh=fine,
        in_specs=(P(None, shot, None, pair), P(shot)),
        out_specs=P(None, shot, pair, None),
        check_vma=False,
    )
```

time: 358 us -> 132 us (0.37)
  the two profiles are of different devices: /device:TPU:16 before, /device:TPU:1 now
where the time goes in v1:
time: 132 us
  blocking collectives  70.9 us (54%)
  waiting for transfers between devices  41.5 us (31%)
  starting transfers between devices  12.2 us (9%)
  Pallas kernels  5.44 us (4%)
  local copies, waits for them, and re-layouts  1.7 us (1%)
    all_to_all x1, blocking collectives, shards(): mine = lax.all_to_all(scaled, ('z', 'y', 'x'), 0, 0, tiled=True)  37.5 us
    ppermute x1, waiting for transfers between devices, shards(): far = lax.ppermute(mine, 'yh', SWAP)  23.6 us
    all_to_all x1, blocking collectives, shards(): cross = lax.all_to_all(cross, 'z', 0, 0, tiled=True)  20.4 us
    all_to_all x1, waiting for transfers between devices, shards(): own = lax.all_to_all(own, 'z', 0, 0, tiled=True)  17.9 us
    ppermute x1, starting transfers between devices, shards(): far = lax.ppermute(mine, 'yh', SWAP)  4.76 us
    all_to_all x1, blocking collectives, shards(): far = lax.all_to_all(far, 'c', 0, 0, tiled=True)  4.56 us
    all_to_all x1, blocking collectives, shards(): cross = lax.all_to_all(cross, 'c', 0, 0, tiled=True)  4.25 us
    all_to_all x1, blocking collectives, shards(): own = lax.all_to_all(own, 'c', 0, 0, tiled=True)  4.25 us
  transfers between devices with their start and end apart: 3, of which 2 were waited for; matrix products, arithmetic and copies ran while one was open for 0% of the time, Pallas kernels for 2%

profile of v1, /device:TPU:1, one launch (start us, length us, event | category | flops | bytes accessed | tf_op | source)
XLA Modules:
  0.0 131.8 jit_solution(11426851945656755996)
XLA Ops:
  0.0 0.0 copy-start.1
  0.0 0.7 copy-done.1
  0.7 0.0 copy-start
  0.7 1.0 copy-done
  1.7 1.3 shard_map.28
  3.0 37.5 %all_to_all.46 = bf16[128,16,128]{2,1,0:T(8,128)(2,1)S(1)} all-to-all(bf16[128,16,128]{2,1,0:T(8,128)(2,1)S(1)} %bitcast.17), channel_id=1, replica_groups=mesh['y'=4,'x'=4,'c'=2,'yh'=2,'z'=8] {'z','y','x'}, dimensions={0} | all-to-all | bytes 1048576 | tf_op jit(solution)/shard_map/all_to_all | solution.py:147
  40.5 3.9 %collective-permute-start = (bf16[128,16,128]{2,1,0:T(8,128)(2,1)S(1)}, bf16[128,16,128]{2,1,0:T(8,128)(2,1)S(1)}, u32[]{:S(2)}, u32[]{:S(2)}) collective-permute-start(bf16[128,16,128]{2,1,0:T(8,128)(2,1)S(1)} %all_to_all.46), channel_id=1, source_target_pairs={{0,16},{16,0},{1,17},{17,1},{2,18},{18,2},{3,19},{19,3},{4,20},{20... | collective-permute-start | bytes 1572872 | tf_op jit(solution)/shard_map/ppermute | solution.py:149
  44.4 4.8 %collective-permute-start.1 = (bf16[128,16,128]{2,1,0:T(8,128)(2,1)S(1)}, bf16[128,16,128]{2,1,0:T(8,128)(2,1)S(1)}, u32[]{:S(2)}, u32[]{:S(2)}) collective-permute-start(bf16[128,16,128]{2,1,0:T(8,128)(2,1)S(1)} %all_to_all.46), channel_id=1, source_target_pairs={{0,8},{8,0},{1,9},{9,1},{2,10},{10,2},{3,11},{11,3},{4,12},{12,4},... | collective-permute-start | bytes 1572872 | tf_op jit(solution)/shard_map/ppermute | solution.py:148
  49.2 0.0 collective-permute-done
  49.2 2.2 %shard_map.29 = (bf16[512,512]{1,0:T(8,128)(2,1)}, bf16[512,1024]{1,0:T(8,128)(2,1)S(1)}) custom-call(s32[1]{0:T(128)} %bitcast.1.core_ref, bf16[8,256,128]{2,1,0:T(8,128)(2,1)S(1)} %bitcast.18, bf16[8,256,128]{2,1,0:T(8,128)(2,1)S(1)} %bitcast.20), custom_call_target="tpu_custom_call" | custom-call | flops 536870912 | bytes 2097152 | tf_op jit(solution)/shard_map/pallas_call | solution.py:152
  51.4 23.6 %collective-permute-done.1 = bf16[128,16,128]{2,1,0:T(8,128)(2,1)S(1)} collective-permute-done((bf16[128,16,128]{2,1,0:T(8,128)(2,1)S(1)}, bf16[128,16,128]{2,1,0:T(8,128)(2,1)S(1)}, u32[]{:S(2)}, u32[]{:S(2)}) %collective-permute-start.1) | collective-permute-done | bytes 524320 | tf_op jit(solution)/shard_map/ppermute | solution.py:148
  75.0 4.6 %all_to_all.47 = bf16[128,16,128]{2,1,0:T(8,128)(2,1)S(1)} all-to-all(bf16[128,16,128]{2,1,0:T(8,128)(2,1)S(1)} %collective-permute-done.1), channel_id=1, replica_groups=mesh['y'=4,'x'=4,'c'=2,'yh'=2,'z'=8] {'c'}, dimensions={0} | all-to-all | bytes 1048576 | tf_op jit(solution)/shard_map/all_to_all | solution.py:166
  79.5 0.9 shard_map.30
  80.4 20.4 %all_to_all.48 = bf16[8,64,512]{2,1,0:T(8,128)(2,1)S(1)} all-to-all(bf16[8,64,512]{2,1,0:T(8,128)(2,1)S(1)} %bitcast.15), channel_id=1, replica_groups=mesh['y'=4,'x'=4,'c'=2,'yh'=2,'z'=8] {'z'}, dimensions={0} | all-to-all | bytes 1048576 | tf_op jit(solution)/shard_map/all_to_all | solution.py:175
  100.8 4.2 %all_to_all.49 = bf16[2,256,512]{2,1,0:T(8,128)(2,1)S(1)} all-to-all(bf16[2,256,512]{2,1,0:T(8,128)(2,1)S(1)} %bitcast.22), channel_id=1, replica_groups=mesh['y'=4,'x'=4,'c'=2,'yh'=2,'z'=8] {'c'}, dimensions={0} | all-to-all | bytes 1048576 | tf_op jit(solution)/shard_map/all_to_all | solution.py:176
  105.0 3.5 %all-to-all-start.1 = ((bf16[8,64,512]{2,1,0:T(8,128)(2,1)}), bf16[8,64,512]{2,1,0:T(8,128)(2,1)S(1)}, u32[]{:S(2)}, u32[]{:S(2)}) async-start(bf16[8,64,512]{2,1,0:T(8,128)(2,1)} %bitcast.6), calls=%async_computation.1 | async-start | bytes 1048576 | tf_op jit(solution)/shard_map/all_to_all | solution.py:163
  108.5 17.9 %all-to-all-done.1 = bf16[8,64,512]{2,1,0:T(8,128)(2,1)S(1)} async-done(((bf16[8,64,512]{2,1,0:T(8,128)(2,1)}), bf16[8,64,512]{2,1,0:T(8,128)(2,1)S(1)}, u32[]{:S(2)}, u32[]{:S(2)}) %all-to-all-start.1) | async-done | bytes 524320 | tf_op jit(solution)/shard_map/all_to_all | solution.py:163
  126.5 4.2 %all_to_all.50 = bf16[2,256,512]{2,1,0:T(8,128)(2,1)S(1)} all-to-all(bf16[2,256,512]{2,1,0:T(8,128)(2,1)S(1)} %bitcast.21), channel_id=1, replica_groups=mesh['y'=4,'x'=4,'c'=2,'yh'=2,'z'=8] {'c'}, dimensions={0} | all-to-all | bytes 1048576 | tf_op jit(solution)/shard_map/all_to_all | solution.py:164
  130.7 1.1 shard_map.31
Async XLA Ops:
  0.0 0.7 copy-start.1
  0.7 1.0 copy-start
  40.5 8.7 %collective-permute-start = (bf16[128,16,128]{2,1,0:T(8,128)(2,1)S(1)}, bf16[128,16,128]{2,1,0:T(8,128)(2,1)S(1)}, u32[]{:S(2)}, u32[]{:S(2)}) collective-permute-start(bf16[128,16,128]{2,1,0:T(8,128)(2,1)S(1)} %all_to_all.46), channel_id=1, source_target_pairs={{0,16},{16,0},{1,17},{17,1},{2,18},{18,2},{3,19},{19,3},{4,20},{20... | collective-permute-start | bytes 1572872 | tf_op jit(solution)/shard_map/ppermute | solution.py:149
  44.4 30.6 %collective-permute-start.1 = (bf16[128,16,128]{2,1,0:T(8,128)(2,1)S(1)}, bf16[128,16,128]{2,1,0:T(8,128)(2,1)S(1)}, u32[]{:S(2)}, u32[]{:S(2)}) collective-permute-start(bf16[128,16,128]{2,1,0:T(8,128)(2,1)S(1)} %all_to_all.46), channel_id=1, source_target_pairs={{0,8},{8,0},{1,9},{9,1},{2,10},{10,2},{3,11},{11,3},{4,12},{12,4},... | collective-permute-start | bytes 1572872 | tf_op jit(solution)/shard_map/ppermute | solution.py:148
  105.0 21.4 %all-to-all-start.1 = ((bf16[8,64,512]{2,1,0:T(8,128)(2,1)}), bf16[8,64,512]{2,1,0:T(8,128)(2,1)S(1)}, u32[]{:S(2)}, u32[]{:S(2)}) async-start(bf16[8,64,512]{2,1,0:T(8,128)(2,1)} %bitcast.6), calls=%async_computation.1 | async-start | bytes 1048576 | tf_op jit(solution)/shard_map/all_to_all | solution.py:163

commit v2 on v1

--- a/solution.py
+++ b/solution.py
@@ -87,36 +87,36 @@
     multiply(left_ref, right, out_ref, factor)
 
 
-def cross_kernel(factor, core_ref, left_ref, y_ref, out_ref, right):
-    _, _, k_rows, _ = y_ref.shape
-    core = core_ref[0]
+def cross_kernel(factor, core_ref, left_ref, y_ref, y_other_ref, out_ref, right):
+    depth, k_rows, _ = y_ref.shape
+    first = core_ref[0] * (depth // 2)
 
     def load(h, j):
-        k_half = core if h == 0 else 1 - core
-        return split_parts(y_ref[k_half, 2 * j], y_ref[k_half, 2 * j + 1])
+        ref = (y_ref, y_other_ref)[h]
+        return split_parts(ref[first + 2 * j], ref[first + 2 * j + 1])
 
     fill_right(right, load, k_rows)
     multiply(left_ref, right, out_ref, factor)
 
 
-def assemble_kernel(yh_ref, own_ref, cross_ref, out_ref):
-    width = own_ref.shape[3] // 2
+def assemble_kernel(yh_ref, core_ref, own_ref, own_other_ref, cross_ref, cross_other_ref, out_ref):
+    width = own_ref.shape[2] // 2
+    bins = own_ref.shape[0] // 2
 
-    def place(ref, half):
+    def place(ref, core, at):
+        mine = slice(core * bins, (core + 1) * bins)
         for part in range(2):
-            for quarter in range(2):
-                at = (2 * half + quarter) * width
-                out_ref[part, :, :, at:at + width] = ref[quarter, :, :, part * width:(part + 1) * width]
+            out_ref[part, :, :, at * width:(at + 1) * width] = ref[mine, :, part * width:(part + 1) * width]
 
-    @pl.when(yh_ref[0] == 0)
-    def _():
-        place(own_ref, 0)
-        place(cross_ref, 1)
+    for yh in range(2):
+        for core in range(2):
 
-    @pl.when(yh_ref[0] != 0)
-    def _():
-        place(own_ref, 1)
-        place(cross_ref, 0)
+            @pl.when(jnp.logical_and(yh_ref[0] == yh, core_ref[0] == core))
+            def _(yh=yh, core=core):
+                place(own_ref, core, 2 * yh + core)
+                place(own_other_ref, core, 2 * yh + 1 - core)
+                place(cross_ref, core, 2 * (1 - yh) + core)
+                place(cross_other_ref, core, 2 * (1 - yh) + 1 - core)
 
 
 SWAP = [(0, 1), (1, 0)]
@@ -160,29 +160,28 @@
         flops=flops,
         nbytes=4 * rows * width * 2,
     )(core, mine.reshape(depth, k_rows, lanes), near.reshape(depth, k_rows, lanes))
-    own = lax.all_to_all(own, "z", 0, 0, tiled=True)
-    own = lax.all_to_all(own, "c", 0, 0, tiled=True)
+    own = lax.all_to_all(own.reshape(depth, chans, width), "z", 0, 0, tiled=True)
 
-    far = lax.all_to_all(far, "c", 0, 0, tiled=True)
+    far_other = lax.ppermute(far, "c", SWAP)
+    own, far, far_other = lax.optimization_barrier((own, far, far_other))
+    own_other = lax.ppermute(own, "c", SWAP)
     cross = vmem_call(
         functools.partial(cross_kernel, factor),
         jax.ShapeDtypeStruct((rows, width), jnp.bfloat16),
-        [SMEM, VMEM, VMEM],
+        [SMEM, VMEM, VMEM, VMEM],
         [pltpu.VMEM((4 * k_rows, width), jnp.bfloat16)],
         flops=flops,
         nbytes=4 * rows * width * 2,
-    )(core, left, far.reshape(cores, depth // 2, k_rows, lanes))
-    cross = lax.all_to_all(cross, "z", 0, 0, tiled=True)
-    cross = lax.all_to_all(cross, "c", 0, 0, tiled=True)
+    )(core, left, far.reshape(depth, k_rows, lanes), far_other.reshape(depth, k_rows, lanes))
+    cross = lax.all_to_all(cross.reshape(depth, chans, width), "z", 0, 0, tiled=True)
+    cross_other = lax.ppermute(cross, "c", SWAP)
 
-    per = depth // cores
-    shape = (cores, per, chans, width)
     return vmem_call(
         assemble_kernel,
-        jax.ShapeDtypeStruct((2, per, chans, 2 * rows), jnp.bfloat16),
-        [SMEM, VMEM, VMEM],
+        jax.ShapeDtypeStruct((2, depth // cores, chans, 2 * rows), jnp.bfloat16),
+        [SMEM, SMEM, VMEM, VMEM, VMEM, VMEM],
         nbytes=4 * rows * width * 2,
-    )(yh, own.reshape(shape), cross.reshape(shape))
+    )(yh, core, own, own_other, cross, cross_other)
 
 
 def solution(mesh):

time: 132 us -> 108 us (0.82)
  blocking collectives: 70.9 us -> 37.5 us
  starting transfers between devices: 12.2 us -> 23 us
  waiting for transfers between devices: 41.5 us -> 38.8 us
    all_to_all x4 -> x0, blocking collectives: 33.4 us -> none  [the longest x1 20.4 us: shards(): cross = lax.all_to_all(cross, 'z', 0, 0, tiled=True)]
    ppermute x0 -> x3, starting transfers between devices: none -> 7.35 us  [the longest x1 2.69 us: shards(): far_other = lax.ppermute(far, 'c', SWAP)]
    ppermute x1, waiting for transfers between devices: 23.6 us -> 20.1 us  [shards(): far = lax.ppermute(mine, 'yh', SWAP)]
    all_to_all x1 -> x2, starting transfers between devices: 3.49 us -> 6.99 us  [the longest x1 3.49 us: shards(): lax.all_to_all(own.reshape(depth, chans, width), 'z', 0, 0, tiled=True)]
    ppermute x0 -> x3, waiting for transfers between devices: none -> 3.02 us  [the longest x1 1.51 us: shards(): far_other = lax.ppermute(far, 'c', SWAP)]
    all_to_all x1 -> x2, waiting for transfers between devices: 17.9 us -> 15.6 us  [the longest x1 15.6 us: shards(): lax.all_to_all(cross.reshape(depth, chans, width), 'z', 0, 0, tiled=True)]
  transfers between devices with their start and end apart: 3 -> 7, of which waited for: 2 -> 4; matrix products, arithmetic and copies ran while one was open for 0% -> 0% of each run, Pallas kernels for 2% -> 2%
where the time goes in v2:
time: 108 us; the launch traced here: 107 us
  waiting for transfers between devices  38.8 us (36%)
  blocking collectives  37.5 us (35%)
  starting transfers between devices  23 us (21%)
  Pallas kernels  6.24 us (6%)
  local copies, waits for them, and re-layouts  1.7 us (2%)
    all_to_all x1, blocking collectives, shards(): mine = lax.all_to_all(scaled, ('z', 'y', 'x'), 0, 0, tiled=True)  37.5 us
    ppermute x1, waiting for transfers between devices, shards(): far = lax.ppermute(mine, 'yh', SWAP)  20.1 us
    all_to_all x1, waiting for transfers between devices, shards(): lax.all_to_all(cross.reshape(depth, chans, width), 'z', 0, 0, tiled=True)  15.6 us
    ppermute x1, starting transfers between devices, shards(): far = lax.ppermute(mine, 'yh', SWAP)  4.76 us
    ppermute x1, starting transfers between devices, shards(): near = lax.ppermute(mine, 'c', SWAP)  3.92 us
    all_to_all x1, starting transfers between devices, shards(): lax.all_to_all(own.reshape(depth, chans, width), 'z', 0, 0, tiled=True)  3.49 us
    all_to_all x1, starting transfers between devices, shards(): lax.all_to_all(cross.reshape(depth, chans, width), 'z', 0, 0, tiled=True)  3.49 us
    ppermute x1, starting transfers between devices, shards(): far_other = lax.ppermute(far, 'c', SWAP)  2.69 us
  transfers between devices with their start and end apart: 7, of which 4 were waited for; matrix products, arithmetic and copies ran while one was open for 0% of the time, Pallas kernels for 2%

profile of v2, /device:TPU:1, one launch (start us, length us, event | category | flops | bytes accessed | tf_op | source)
XLA Modules:
  0.0 107.3 jit_solution(15891600527290723713)
XLA Ops:
  0.0 0.0 copy-start.1
  0.0 0.7 copy-done.1
  0.7 0.0 copy-start
  0.7 1.0 copy-done
  1.7 1.3 %shard_map.28 = bf16[8,16,16,128]{3,2,1,0:T(8,128)(2,1)S(1)} custom-call(f32[16]{0:T(128)S(1)} %copy-done.1, bf16[2,16,64,128]{3,2,1,0:T(8,128)(2,1)S(1)} %bitcast.12), custom_call_target="tpu_custom_call" | custom-call | bytes 1048576 | tf_op jit(solution)/shard_map/pallas_call | solution.py:139
  3.0 37.5 %all_to_all.15 = bf16[128,16,128]{2,1,0:T(8,128)(2,1)S(1)} all-to-all(bf16[128,16,128]{2,1,0:T(8,128)(2,1)S(1)} %bitcast.10), channel_id=1, replica_groups=mesh['y'=4,'x'=4,'c'=2,'yh'=2,'z'=8] {'z','y','x'}, dimensions={0} | all-to-all | bytes 1048576 | tf_op jit(solution)/shard_map/all_to_all | solution.py:147
  40.5 3.9 %collective-permute-start = (bf16[128,16,128]{2,1,0:T(8,128)(2,1)S(1)}, bf16[128,16,128]{2,1,0:T(8,128)(2,1)S(1)}, u32[]{:S(2)}, u32[]{:S(2)}) collective-permute-start(bf16[128,16,128]{2,1,0:T(8,128)(2,1)S(1)} %all_to_all.15), channel_id=1, source_target_pairs={{0,16},{16,0},{1,17},{17,1},{2,18},{18,2},{3,19},{19,3},{4,20},{20... | collective-permute-start | bytes 1572872 | tf_op jit(solution)/shard_map/ppermute | solution.py:149
  44.4 4.8 %collective-permute-start.1 = (bf16[128,16,128]{2,1,0:T(8,128)(2,1)S(1)}, bf16[128,16,128]{2,1,0:T(8,128)(2,1)S(1)}, u32[]{:S(2)}, u32[]{:S(2)}) collective-permute-start(bf16[128,16,128]{2,1,0:T(8,128)(2,1)S(1)} %all_to_all.15), channel_id=1, source_target_pairs={{0,8},{8,0},{1,9},{9,1},{2,10},{10,2},{3,11},{11,3},{4,12},{12,4},... | collective-permute-start | bytes 1572872 | tf_op jit(solution)/shard_map/ppermute | solution.py:148
  49.2 0.0 collective-permute-done
  49.2 2.2 %shard_map.29 = (bf16[512,512]{1,0:T(8,128)(2,1)}, bf16[512,1024]{1,0:T(8,128)(2,1)S(1)}) custom-call(s32[1]{0:T(128)} %bitcast.1.core_ref, bf16[8,256,128]{2,1,0:T(8,128)(2,1)S(1)} %bitcast.11, bf16[8,256,128]{2,1,0:T(8,128)(2,1)S(1)} %bitcast.15), custom_call_target="tpu_custom_call" | custom-call | flops 536870912 | bytes 2097152 | tf_op jit(solution)/shard_map/pallas_call | solution.py:152
  51.4 3.5 %all-to-all-start.1 = ((bf16[8,64,512]{2,1,0:T(8,128)(2,1)}), bf16[8,64,512]{2,1,0:T(8,128)(2,1)S(1)}, u32[]{:S(2)}, u32[]{:S(2)}) async-start(bf16[8,64,512]{2,1,0:T(8,128)(2,1)} %bitcast.6), calls=%async_computation.1 | async-start | bytes 1048576 | tf_op jit(solution)/shard_map/all_to_all | solution.py:163
  54.9 20.1 %collective-permute-done.1 = bf16[128,16,128]{2,1,0:T(8,128)(2,1)S(1)} collective-permute-done((bf16[128,16,128]{2,1,0:T(8,128)(2,1)S(1)}, bf16[128,16,128]{2,1,0:T(8,128)(2,1)S(1)}, u32[]{:S(2)}, u32[]{:S(2)}) %collective-permute-start.1) | collective-permute-done | bytes 524320 | tf_op jit(solution)/shard_map/ppermute | solution.py:148
  75.0 2.7 %collective-permute-start.2 = (bf16[128,16,128]{2,1,0:T(8,128)(2,1)S(1)}, bf16[128,16,128]{2,1,0:T(8,128)(2,1)S(1)}, u32[]{:S(2)}, u32[]{:S(2)}) collective-permute-start(bf16[128,16,128]{2,1,0:T(8,128)(2,1)S(1)} %collective-permute-done.1), channel_id=1, source_target_pairs={{0,16},{16,0},{1,17},{17,1},{2,18},{18,2},{3,19},{19,3},{4,20},{20... | collective-permute-start | bytes 1572872 | tf_op jit(solution)/shard_map/ppermute | solution.py:165
  77.7 1.5 %collective-permute-done.2 = bf16[128,16,128]{2,1,0:T(8,128)(2,1)S(1)} collective-permute-done((bf16[128,16,128]{2,1,0:T(8,128)(2,1)S(1)}, bf16[128,16,128]{2,1,0:T(8,128)(2,1)S(1)}, u32[]{:S(2)}, u32[]{:S(2)}) %collective-permute-start.2) | collective-permute-done | bytes 524320 | tf_op jit(solution)/shard_map/ppermute | solution.py:165
  79.2 0.0 all-to-all-done.1.own_ref
  79.2 1.7 %shard_map.30 = bf16[512,512]{1,0:T(8,128)(2,1)} custom-call(s32[1]{0:T(128)} %bitcast.1.core_ref, bf16[512,1024]{1,0:T(8,128)(2,1)S(1)} %get-tuple-element.12.left_ref, bf16[8,256,128]{2,1,0:T(8,128)(2,1)S(1)} %bitcast.13, bf16[8,256,128]{2,1,0:T(8,128)(2,1)S(1)} %bitcast.14), custom_call_target="tpu_custom_call" | custom-call | flops 536870912 | bytes 2097152 | tf_op jit(solution)/shard_map/pallas_call | solution.py:168
  80.8 3.5 %all-to-all-start.2 = ((bf16[8,64,512]{2,1,0:T(8,128)(2,1)}), bf16[8,64,512]{2,1,0:T(8,128)(2,1)S(1)}, u32[]{:S(2)}, u32[]{:S(2)}) async-start(bf16[8,64,512]{2,1,0:T(8,128)(2,1)} %bitcast.9), calls=%async_computation.2 | async-start | bytes 1048576 | tf_op jit(solution)/shard_map/all_to_all | solution.py:176
  84.3 2.3 %collective-permute-start.3 = (bf16[8,64,512]{2,1,0:T(8,128)(2,1)S(1)}, bf16[8,64,512]{2,1,0:T(8,128)(2,1)S(1)}, u32[]{:S(2)}, u32[]{:S(2)}) collective-permute-start(bf16[8,64,512]{2,1,0:T(8,128)(2,1)S(1)} %all-to-all-done.1.own_ref), channel_id=1, source_target_pairs={{0,16},{16,0},{1,17},{17,1},{2,18},{18,2},{3,19},{19,3},{4,20},{20... | collective-permute-start | bytes 1572872 | tf_op jit(solution)/shard_map/ppermute | solution.py:167
  86.6 15.6 %all-to-all-done.2.cross_ref = bf16[8,64,512]{2,1,0:T(8,128)(2,1)S(1)} async-done(((bf16[8,64,512]{2,1,0:T(8,128)(2,1)}), bf16[8,64,512]{2,1,0:T(8,128)(2,1)S(1)}, u32[]{:S(2)}, u32[]{:S(2)}) %all-to-all-start.2) | async-done | bytes 524320 | tf_op jit(solution)/shard_map/all_to_all | solution.py:176
  102.3 2.4 %collective-permute-start.4 = (bf16[8,64,512]{2,1,0:T(8,128)(2,1)S(1)}, bf16[8,64,512]{2,1,0:T(8,128)(2,1)S(1)}, u32[]{:S(2)}, u32[]{:S(2)}) collective-permute-start(bf16[8,64,512]{2,1,0:T(8,128)(2,1)S(1)} %all-to-all-done.2.cross_ref), channel_id=1, source_target_pairs={{0,16},{16,0},{1,17},{17,1},{2,18},{18,2},{3,19},{19,3},{4,20},{20... | collective-permute-start | bytes 1572872 | tf_op jit(solution)/shard_map/ppermute | solution.py:177
  104.7 0.0 collective-permute-done.3.own_other_ref
  104.7 1.5 %collective-permute-done.4.cross_other_ref = bf16[8,64,512]{2,1,0:T(8,128)(2,1)S(1)} collective-permute-done((bf16[8,64,512]{2,1,0:T(8,128)(2,1)S(1)}, bf16[8,64,512]{2,1,0:T(8,128)(2,1)S(1)}, u32[]{:S(2)}, u32[]{:S(2)}) %collective-permute-start.4) | collective-permute-done | bytes 524320 | tf_op jit(solution)/shard_map/ppermute | solution.py:177
  106.2 1.1 %shard_map.31 = bf16[2,4,64,1024]{3,2,1,0:T(8,128)(2,1)} custom-call(s32[1]{0:T(128)} %bitcast.yh_ref, s32[1]{0:T(128)} %bitcast.1.core_ref, bf16[8,64,512]{2,1,0:T(8,128)(2,1)S(1)} %all-to-all-done.1.own_ref, bf16[8,64,512]{2,1,0:T(8,128)(2,1)S(1)} %collective-permute-done.3.own_other_ref, bf16[8,64,512]{2,1,0:T(8,128)(2,1)S(1)} %all-to-all-done.2.cross_ref, ...), custom_call_target="tpu_custom_call" | custom-call | bytes 2097152 | tf_op jit(solution)/shard_map/pallas_call | solution.py:179
Async XLA Ops:
  0.0 0.7 copy-start.1
  0.7 1.0 copy-start
  40.5 8.7 %collective-permute-start = (bf16[128,16,128]{2,1,0:T(8,128)(2,1)S(1)}, bf16[128,16,128]{2,1,0:T(8,128)(2,1)S(1)}, u32[]{:S(2)}, u32[]{:S(2)}) collective-permute-start(bf16[128,16,128]{2,1,0:T(8,128)(2,1)S(1)} %all_to_all.15), channel_id=1, source_target_pairs={{0,16},{16,0},{1,17},{17,1},{2,18},{18,2},{3,19},{19,3},{4,20},{20... | collective-permute-start | bytes 1572872 | tf_op jit(solution)/shard_map/ppermute | solution.py:149
  44.4 30.6 %collective-permute-start.1 = (bf16[128,16,128]{2,1,0:T(8,128)(2,1)S(1)}, bf16[128,16,128]{2,1,0:T(8,128)(2,1)S(1)}, u32[]{:S(2)}, u32[]{:S(2)}) collective-permute-start(bf16[128,16,128]{2,1,0:T(8,128)(2,1)S(1)} %all_to_all.15), channel_id=1, source_target_pairs={{0,8},{8,0},{1,9},{9,1},{2,10},{10,2},{3,11},{11,3},{4,12},{12,4},... | collective-permute-start | bytes 1572872 | tf_op jit(solution)/shard_map/ppermute | solution.py:148
  51.4 27.8 %all-to-all-start.1 = ((bf16[8,64,512]{2,1,0:T(8,128)(2,1)}), bf16[8,64,512]{2,1,0:T(8,128)(2,1)S(1)}, u32[]{:S(2)}, u32[]{:S(2)}) async-start(bf16[8,64,512]{2,1,0:T(8,128)(2,1)} %bitcast.6), calls=%async_computation.1 | async-start | bytes 1048576 | tf_op jit(solution)/shard_map/all_to_all | solution.py:163
  75.0 4.2 %collective-permute-start.2 = (bf16[128,16,128]{2,1,0:T(8,128)(2,1)S(1)}, bf16[128,16,128]{2,1,0:T(8,128)(2,1)S(1)}, u32[]{:S(2)}, u32[]{:S(2)}) collective-permute-start(bf16[128,16,128]{2,1,0:T(8,128)(2,1)S(1)} %collective-permute-done.1), channel_id=1, source_target_pairs={{0,16},{16,0},{1,17},{17,1},{2,18},{18,2},{3,19},{19,3},{4,20},{20... | collective-permute-start | bytes 1572872 | tf_op jit(solution)/shard_map/ppermute | solution.py:165
  80.8 21.4 %all-to-all-start.2 = ((bf16[8,64,512]{2,1,0:T(8,128)(2,1)}), bf16[8,64,512]{2,1,0:T(8,128)(2,1)S(1)}, u32[]{:S(2)}, u32[]{:S(2)}) async-start(bf16[8,64,512]{2,1,0:T(8,128)(2,1)} %bitcast.9), calls=%async_computation.2 | async-start | bytes 1048576 | tf_op jit(solution)/shard_map/all_to_all | solution.py:176
  84.3 20.3 %collective-permute-start.3 = (bf16[8,64,512]{2,1,0:T(8,128)(2,1)S(1)}, bf16[8,64,512]{2,1,0:T(8,128)(2,1)S(1)}, u32[]{:S(2)}, u32[]{:S(2)}) collective-permute-start(bf16[8,64,512]{2,1,0:T(8,128)(2,1)S(1)} %all-to-all-done.1.own_ref), channel_id=1, source_target_pairs={{0,16},{16,0},{1,17},{17,1},{2,18},{18,2},{3,19},{19,3},{4,20},{20... | collective-permute-start | bytes 1572872 | tf_op jit(solution)/shard_map/ppermute | solution.py:167
  102.3 3.9 %collective-permute-start.4 = (bf16[8,64,512]{2,1,0:T(8,128)(2,1)S(1)}, bf16[8,64,512]{2,1,0:T(8,128)(2,1)S(1)}, u32[]{:S(2)}, u32[]{:S(2)}) collective-permute-start(bf16[8,64,512]{2,1,0:T(8,128)(2,1)S(1)} %all-to-all-done.2.cross_ref), channel_id=1, source_target_pairs={{0,16},{16,0},{1,17},{17,1},{2,18},{18,2},{3,19},{19,3},{4,20},{20... | collective-permute-start | bytes 1572872 | tf_op jit(solution)/shard_map/ppermute | solution.py:177

commit v3 on v2

--- a/solution.py
+++ b/solution.py
@@ -87,15 +87,17 @@
     multiply(left_ref, right, out_ref, factor)
 
 
-def cross_kernel(factor, core_ref, left_ref, y_ref, y_other_ref, out_ref, right):
-    depth, k_rows, _ = y_ref.shape
-    first = core_ref[0] * (depth // 2)
+def right_kernel(y_ref, y_other_ref, right):
+    k_rows = y_ref.shape[1]
 
     def load(h, j):
         ref = (y_ref, y_other_ref)[h]
-        return split_parts(ref[first + 2 * j], ref[first + 2 * j + 1])
+        return split_parts(ref[2 * j], ref[2 * j + 1])
 
     fill_right(right, load, k_rows)
+
+
+def cross_kernel(factor, left_ref, right, out_ref):
     multiply(left_ref, right, out_ref, factor)
 
 
@@ -145,8 +147,11 @@
     )(shot_weight, turned)
     scaled = scaled.reshape(bins, shots, lanes)
     mine = lax.all_to_all(scaled, ("z", "y", "x"), 0, 0, tiled=True)
-    far = lax.ppermute(mine, "yh", SWAP)
+    half = bins // cores
+    first = lax.axis_index("c") * half
+    far = lax.ppermute(lax.dynamic_slice_in_dim(mine, first, half), "yh", SWAP)
     near = lax.ppermute(mine, "c", SWAP)
+    far_other = lax.ppermute(lax.dynamic_slice_in_dim(near, first, half), "yh", SWAP)
 
     flops = 2 * rows * 4 * k_rows * width
     own, left = vmem_call(
@@ -161,18 +166,24 @@
         nbytes=4 * rows * width * 2,
     )(core, mine.reshape(depth, k_rows, lanes), near.reshape(depth, k_rows, lanes))
     own = lax.all_to_all(own.reshape(depth, chans, width), "z", 0, 0, tiled=True)
-
-    far_other = lax.ppermute(far, "c", SWAP)
-    own, far, far_other = lax.optimization_barrier((own, far, far_other))
+    right = vmem_call(
+        right_kernel,
+        jax.ShapeDtypeStruct((4 * k_rows, width), jnp.bfloat16),
+        [VMEM, VMEM],
+        flops=40 * flops,
+    )(
+        far.reshape(depth // cores, k_rows, lanes),
+        far_other.reshape(depth // cores, k_rows, lanes),
+    )
+    own, right = lax.optimization_barrier((own, right))
     own_other = lax.ppermute(own, "c", SWAP)
     cross = vmem_call(
         functools.partial(cross_kernel, factor),
         jax.ShapeDtypeStruct((rows, width), jnp.bfloat16),
-        [SMEM, VMEM, VMEM, VMEM],
-        [pltpu.VMEM((4 * k_rows, width), jnp.bfloat16)],
+        [VMEM, VMEM],
         flops=flops,
         nbytes=4 * rows * width * 2,
-    )(core, left, far.reshape(depth, k_rows, lanes), far_other.reshape(depth, k_rows, lanes))
+    )(left, right)
     cross = lax.all_to_all(cross.reshape(depth, chans, width), "z", 0, 0, tiled=True)
     cross_other = lax.ppermute(cross, "c", SWAP)
 

time: 108 us -> 106 us (0.981)
  waiting for transfers between devices: 38.8 us -> 34.6 us
  starting transfers between devices: 23 us -> 24.9 us
    ppermute x2, waiting for transfers between devices: 21.6 us -> 15.6 us  [the longest x1 10 us: shards(): far = lax.ppermute(lax.dynamic_slice_in_dim(mine, first, half), 'yh', SWAP)]
    all_to_all x1, waiting for transfers between devices: 0.01 us -> 2.03 us  [shards(): lax.all_to_all(own.reshape(depth, chans, width), 'z', 0, 0, tiled=True)]
    ppermute x2, starting transfers between devices: 7.45 us -> 9.19 us  [the longest x1 4.76 us: shards(): far = lax.ppermute(lax.dynamic_slice_in_dim(mine, first, half), 'yh', SWAP)]
  transfers between devices with their start and end apart: 7 -> 7, of which waited for: 4 -> 5; matrix products, arithmetic and copies ran while one was open for 0% -> 0% of each run, Pallas kernels for 2% -> 2%
where the time goes in v3:
time: 106 us; the launch traced here: 105 us
  blocking collectives  37.5 us (35%)
  waiting for transfers between devices  34.6 us (33%)
  starting transfers between devices  24.9 us (23%)
  Pallas kernels  6.3 us (6%)
  local copies, waits for them, and re-layouts  1.75 us (2%)
    all_to_all x1, blocking collectives, shards(): mine = lax.all_to_all(scaled, ('z', 'y', 'x'), 0, 0, tiled=True)  37.5 us
    all_to_all x1, waiting for transfers between devices, shards(): lax.all_to_all(cross.reshape(depth, chans, width), 'z', 0, 0, tiled=True)  15.5 us
    ppermute x1, waiting for transfers between devices, shards(): far = lax.ppermute(lax.dynamic_slice_in_dim(mine, first, half), 'yh', SWAP)  10 us
    ppermute x1, waiting for transfers between devices, shards(): lax.ppermute(lax.dynamic_slice_in_dim(near, first, half), 'yh', SWAP)  5.62 us
    ppermute x1, starting transfers between devices, shards(): far = lax.ppermute(lax.dynamic_slice_in_dim(mine, first, half), 'yh', SWAP)  4.76 us
    ppermute x1, starting transfers between devices, shards(): lax.ppermute(lax.dynamic_slice_in_dim(near, first, half), 'yh', SWAP)  4.43 us
    ppermute x1, starting transfers between devices, shards(): near = lax.ppermute(mine, 'c', SWAP)  3.92 us
    all_to_all x1, starting transfers between devices, shards(): lax.all_to_all(own.reshape(depth, chans, width), 'z', 0, 0, tiled=True)  3.49 us
  transfers between devices with their start and end apart: 7, of which 5 were waited for; matrix products, arithmetic and copies ran while one was open for 0% of the time, Pallas kernels for 2%

profile of v3, /device:TPU:1, one launch (start us, length us, event | category | flops | bytes accessed | tf_op | source)
XLA Modules:
  0.0 105.1 jit_solution(707825791621039918)
XLA Ops:
  0.0 0.0 copy-start.1
  0.0 0.7 copy-done.1
  0.7 0.0 copy-start
  0.7 1.0 copy-done
  1.7 1.3 %shard_map.28 = bf16[8,16,16,128]{3,2,1,0:T(8,128)(2,1)S(1)} custom-call(f32[16]{0:T(128)S(1)} %copy-done.1, bf16[2,16,64,128]{3,2,1,0:T(8,128)(2,1)S(1)} %bitcast.12), custom_call_target="tpu_custom_call" | custom-call | bytes 1048576 | tf_op jit(solution)/shard_map/pallas_call | solution.py:141
  3.0 37.5 %all_to_all.15 = bf16[128,16,128]{2,1,0:T(8,128)(2,1)S(1)} all-to-all(bf16[128,16,128]{2,1,0:T(8,128)(2,1)S(1)} %bitcast.10), channel_id=1, replica_groups=mesh['y'=4,'x'=4,'c'=2,'yh'=2,'z'=8] {'z','y','x'}, dimensions={0} | all-to-all | bytes 1048576 | tf_op jit(solution)/shard_map/all_to_all | solution.py:149
  40.5 3.9 %collective-permute-start = (bf16[128,16,128]{2,1,0:T(8,128)(2,1)S(1)}, bf16[128,16,128]{2,1,0:T(8,128)(2,1)S(1)}, u32[]{:S(2)}, u32[]{:S(2)}) collective-permute-start(bf16[128,16,128]{2,1,0:T(8,128)(2,1)S(1)} %all_to_all.15), channel_id=1, source_target_pairs={{0,16},{16,0},{1,17},{17,1},{2,18},{18,2},{3,19},{19,3},{4,20},{20... | collective-permute-start | bytes 1572872 | tf_op jit(solution)/shard_map/ppermute | solution.py:153
  44.4 4.8 %collective-permute-start.1 = (bf16[64,16,128]{2,1,0:T(8,128)(2,1)S(1)}, bf16[64,16,128]{2,1,0:T(8,128)(2,1)S(1)}, u32[]{:S(2)}, u32[]{:S(2)}) collective-permute-start(bf16[64,16,128]{2,1,0:T(8,128)(2,1)S(1)} %constant_dynamic-slice_fusion.1), channel_id=1, source_target_pairs={{0,8},{8,0},{1,9},{9,1},{2,10},{10,2},{3,11},{11,3},{4,12},{12,4},... | collective-permute-start | bytes 786440 | tf_op jit(solution)/shard_map/ppermute | solution.py:152
  49.2 0.0 collective-permute-done
  49.2 4.4 %collective-permute-start.2 = (bf16[64,16,128]{2,1,0:T(8,128)(2,1)S(1)}, bf16[64,16,128]{2,1,0:T(8,128)(2,1)S(1)}, u32[]{:S(2)}, u32[]{:S(2)}) collective-permute-start(bf16[64,16,128]{2,1,0:T(8,128)(2,1)S(1)} %constant_dynamic-slice_fusion), channel_id=1, source_target_pairs={{0,8},{8,0},{1,9},{9,1},{2,10},{10,2},{3,11},{11,3},{4,12},{12,4},... | collective-permute-start | bytes 786440 | tf_op jit(solution)/shard_map/ppermute | solution.py:154
  53.7 2.2 %shard_map.29 = (bf16[512,512]{1,0:T(8,128)(2,1)}, bf16[512,1024]{1,0:T(8,128)(2,1)S(1)}) custom-call(s32[1]{0:T(128)} %bitcast.1.core_ref, bf16[8,256,128]{2,1,0:T(8,128)(2,1)S(1)} %bitcast.11, bf16[8,256,128]{2,1,0:T(8,128)(2,1)S(1)} %bitcast.13), custom_call_target="tpu_custom_call" | custom-call | flops 536870912 | bytes 2097152 | tf_op jit(solution)/shard_map/pallas_call | solution.py:157
  55.9 3.5 %all-to-all-start.1 = ((bf16[8,64,512]{2,1,0:T(8,128)(2,1)}), bf16[8,64,512]{2,1,0:T(8,128)(2,1)S(1)}, u32[]{:S(2)}, u32[]{:S(2)}) async-start(bf16[8,64,512]{2,1,0:T(8,128)(2,1)} %bitcast.6), calls=%async_computation.1 | async-start | bytes 1048576 | tf_op jit(solution)/shard_map/all_to_all | solution.py:168
  59.4 10.0 %collective-permute-done.1 = bf16[64,16,128]{2,1,0:T(8,128)(2,1)S(1)} collective-permute-done((bf16[64,16,128]{2,1,0:T(8,128)(2,1)S(1)}, bf16[64,16,128]{2,1,0:T(8,128)(2,1)S(1)}, u32[]{:S(2)}, u32[]{:S(2)}) %collective-permute-start.1) | collective-permute-done | bytes 262176 | tf_op jit(solution)/shard_map/ppermute | solution.py:152
  69.4 5.6 %collective-permute-done.2 = bf16[64,16,128]{2,1,0:T(8,128)(2,1)S(1)} collective-permute-done((bf16[64,16,128]{2,1,0:T(8,128)(2,1)S(1)}, bf16[64,16,128]{2,1,0:T(8,128)(2,1)S(1)}, u32[]{:S(2)}, u32[]{:S(2)}) %collective-permute-start.2) | collective-permute-done | bytes 262176 | tf_op jit(solution)/shard_map/ppermute | solution.py:154
  75.0 0.2 shard_map.30.right
  75.2 2.0 %all-to-all-done.1.own_ref = bf16[8,64,512]{2,1,0:T(8,128)(2,1)S(1)} async-done(((bf16[8,64,512]{2,1,0:T(8,128)(2,1)}), bf16[8,64,512]{2,1,0:T(8,128)(2,1)S(1)}, u32[]{:S(2)}, u32[]{:S(2)}) %all-to-all-start.1) | async-done | bytes 524320 | tf_op jit(solution)/shard_map/all_to_all | solution.py:168
  77.2 1.5 %shard_map.31 = bf16[512,512]{1,0:T(8,128)(2,1)} custom-call(bf16[512,1024]{1,0:T(8,128)(2,1)S(1)} %get-tuple-element.11.left_ref, bf16[1024,512]{1,0:T(8,128)(2,1)S(1)} %shard_map.30.right), custom_call_target="tpu_custom_call" | custom-call | flops 536870912 | bytes 2097152 | tf_op jit(solution)/shard_map/pallas_call | solution.py:180
  78.7 3.5 %all-to-all-start.2 = ((bf16[8,64,512]{2,1,0:T(8,128)(2,1)}), bf16[8,64,512]{2,1,0:T(8,128)(2,1)S(1)}, u32[]{:S(2)}, u32[]{:S(2)}) async-start(bf16[8,64,512]{2,1,0:T(8,128)(2,1)} %bitcast.9), calls=%async_computation.2 | async-start | bytes 1048576 | tf_op jit(solution)/shard_map/all_to_all | solution.py:187
  82.3 2.4 %collective-permute-start.3 = (bf16[8,64,512]{2,1,0:T(8,128)(2,1)S(1)}, bf16[8,64,512]{2,1,0:T(8,128)(2,1)S(1)}, u32[]{:S(2)}, u32[]{:S(2)}) collective-permute-start(bf16[8,64,512]{2,1,0:T(8,128)(2,1)S(1)} %all-to-all-done.1.own_ref), channel_id=1, source_target_pairs={{0,16},{16,0},{1,17},{17,1},{2,18},{18,2},{3,19},{19,3},{4,20},{20... | collective-permute-start | bytes 1572872 | tf_op jit(solution)/shard_map/ppermute | solution.py:179
  84.7 15.5 %all-to-all-done.2.cross_ref = bf16[8,64,512]{2,1,0:T(8,128)(2,1)S(1)} async-done(((bf16[8,64,512]{2,1,0:T(8,128)(2,1)}), bf16[8,64,512]{2,1,0:T(8,128)(2,1)S(1)}, u32[]{:S(2)}, u32[]{:S(2)}) %all-to-all-start.2) | async-done | bytes 524320 | tf_op jit(solution)/shard_map/all_to_all | solution.py:187
  100.1 2.4 %collective-permute-start.4 = (bf16[8,64,512]{2,1,0:T(8,128)(2,1)S(1)}, bf16[8,64,512]{2,1,0:T(8,128)(2,1)S(1)}, u32[]{:S(2)}, u32[]{:S(2)}) collective-permute-start(bf16[8,64,512]{2,1,0:T(8,128)(2,1)S(1)} %all-to-all-done.2.cross_ref), channel_id=1, source_target_pairs={{0,16},{16,0},{1,17},{17,1},{2,18},{18,2},{3,19},{19,3},{4,20},{20... | collective-permute-start | bytes 1572872 | tf_op jit(solution)/shard_map/ppermute | solution.py:188
  102.5 0.0 collective-permute-done.3.own_other_ref
  102.5 1.5 %collective-permute-done.4.cross_other_ref = bf16[8,64,512]{2,1,0:T(8,128)(2,1)S(1)} collective-permute-done((bf16[8,64,512]{2,1,0:T(8,128)(2,1)S(1)}, bf16[8,64,512]{2,1,0:T(8,128)(2,1)S(1)}, u32[]{:S(2)}, u32[]{:S(2)}) %collective-permute-start.4) | collective-permute-done | bytes 524320 | tf_op jit(solution)/shard_map/ppermute | solution.py:188
  104.0 1.1 %shard_map.32 = bf16[2,4,64,1024]{3,2,1,0:T(8,128)(2,1)} custom-call(s32[1]{0:T(128)} %bitcast.yh_ref, s32[1]{0:T(128)} %bitcast.1.core_ref, bf16[8,64,512]{2,1,0:T(8,128)(2,1)S(1)} %all-to-all-done.1.own_ref, bf16[8,64,512]{2,1,0:T(8,128)(2,1)S(1)} %collective-permute-done.3.own_other_ref, bf16[8,64,512]{2,1,0:T(8,128)(2,1)S(1)} %all-to-all-done.2.cross_ref, ...), custom_call_target="tpu_custom_call" | custom-call | bytes 2097152 | tf_op jit(solution)/shard_map/pallas_call | solution.py:190
  (2 shorter events, 0.1 us)
Async XLA Ops:
  0.0 0.7 copy-start.1
  0.7 1.0 copy-start
  40.5 8.7 %collective-permute-start = (bf16[128,16,128]{2,1,0:T(8,128)(2,1)S(1)}, bf16[128,16,128]{2,1,0:T(8,128)(2,1)S(1)}, u32[]{:S(2)}, u32[]{:S(2)}) collective-permute-start(bf16[128,16,128]{2,1,0:T(8,128)(2,1)S(1)} %all_to_all.15), channel_id=1, source_target_pairs={{0,16},{16,0},{1,17},{17,1},{2,18},{18,2},{3,19},{19,3},{4,20},{20... | collective-permute-start | bytes 1572872 | tf_op jit(solution)/shard_map/ppermute | solution.py:153
  44.4 25.0 %collective-permute-start.1 = (bf16[64,16,128]{2,1,0:T(8,128)(2,1)S(1)}, bf16[64,16,128]{2,1,0:T(8,128)(2,1)S(1)}, u32[]{:S(2)}, u32[]{:S(2)}) collective-permute-start(bf16[64,16,128]{2,1,0:T(8,128)(2,1)S(1)} %constant_dynamic-slice_fusion.1), channel_id=1, source_target_pairs={{0,8},{8,0},{1,9},{9,1},{2,10},{10,2},{3,11},{11,3},{4,12},{12,4},... | collective-permute-start | bytes 786440 | tf_op jit(solution)/shard_map/ppermute | solution.py:152
  49.2 25.8 %collective-permute-start.2 = (bf16[64,16,128]{2,1,0:T(8,128)(2,1)S(1)}, bf16[64,16,128]{2,1,0:T(8,128)(2,1)S(1)}, u32[]{:S(2)}, u32[]{:S(2)}) collective-permute-start(bf16[64,16,128]{2,1,0:T(8,128)(2,1)S(1)} %constant_dynamic-slice_fusion), channel_id=1, source_target_pairs={{0,8},{8,0},{1,9},{9,1},{2,10},{10,2},{3,11},{11,3},{4,12},{12,4},... | collective-permute-start | bytes 786440 | tf_op jit(solution)/shard_map/ppermute | solution.py:154
  55.9 21.4 %all-to-all-start.1 = ((bf16[8,64,512]{2,1,0:T(8,128)(2,1)}), bf16[8,64,512]{2,1,0:T(8,128)(2,1)S(1)}, u32[]{:S(2)}, u32[]{:S(2)}) async-start(bf16[8,64,512]{2,1,0:T(8,128)(2,1)} %bitcast.6), calls=%async_computation.1 | async-start | bytes 1048576 | tf_op jit(solution)/shard_map/all_to_all | solution.py:168
  78.7 21.4 %all-to-all-start.2 = ((bf16[8,64,512]{2,1,0:T(8,128)(2,1)}), bf16[8,64,512]{2,1,0:T(8,128)(2,1)S(1)}, u32[]{:S(2)}, u32[]{:S(2)}) async-start(bf16[8,64,512]{2,1,0:T(8,128)(2,1)} %bitcast.9), calls=%async_computation.2 | async-start | bytes 1048576 | tf_op jit(solution)/shard_map/all_to_all | solution.py:187
  82.3 20.3 %collective-permute-start.3 = (bf16[8,64,512]{2,1,0:T(8,128)(2,1)S(1)}, bf16[8,64,512]{2,1,0:T(8,128)(2,1)S(1)}, u32[]{:S(2)}, u32[]{:S(2)}) collective-permute-start(bf16[8,64,512]{2,1,0:T(8,128)(2,1)S(1)} %all-to-all-done.1.own_ref), channel_id=1, source_target_pairs={{0,16},{16,0},{1,17},{17,1},{2,18},{18,2},{3,19},{19,3},{4,20},{20... | collective-permute-start | bytes 1572872 | tf_op jit(solution)/shard_map/ppermute | solution.py:179
  100.1 3.9 %collective-permute-start.4 = (bf16[8,64,512]{2,1,0:T(8,128)(2,1)S(1)}, bf16[8,64,512]{2,1,0:T(8,128)(2,1)S(1)}, u32[]{:S(2)}, u32[]{:S(2)}) collective-permute-start(bf16[8,64,512]{2,1,0:T(8,128)(2,1)S(1)} %all-to-all-done.2.cross_ref), channel_id=1, source_target_pairs={{0,16},{16,0},{1,17},{17,1},{2,18},{18,2},{3,19},{19,3},{4,20},{20... | collective-permute-start | bytes 1572872 | tf_op jit(solution)/shard_map/ppermute | solution.py:188

commit v4 on v2

v4 whole, which is shorter than its diff:
```python
import functools

import jax
import jax.numpy as jnp
from jax import lax
from jax.experimental import pallas as pl
from jax.experimental.pallas import tpu as pltpu
from jax.sharding import Mesh, PartitionSpec as P

VMEM = pltpu.MemorySpace.VMEM
SMEM = pltpu.MemorySpace.SMEM
HBM = pltpu.MemorySpace.HBM
STEPS = 4
PARAMS = pltpu.CompilerParams(vmem_limit_bytes=32 * 1024 * 1024)


def vmem_call(body, out_shape, in_spaces, scratch=(), flops=0, nbytes=0, params=PARAMS):
    outs = out_shape if isinstance(out_shape, (list, tuple)) else (out_shape,)
    specs = [pl.BlockSpec(memory_space=VMEM) for _ in outs]
    return pl.pallas_call(
        body,
        out_shape=out_shape,
        in_specs=[pl.BlockSpec(memory_space=s) for s in in_spaces],
        out_specs=specs if isinstance(out_shape, (list, tuple)) else specs[0],
        scratch_shapes=list(scratch),
        compiler_params=params,
        cost_estimate=pl.CostEstimate(flops=flops, bytes_accessed=nbytes, transcendentals=0),
    )


def scale_kernel(weight_hbm, x_hbm, out_ref, weight_ref, x_ref, turned, sems):
    _, shots, chans, bins = x_ref.shape
    planes, depth = turned.shape[0], turned.shape[1]
    step = shots // STEPS
    weight_copy = pltpu.make_async_copy(weight_hbm, weight_ref, sems.at[STEPS])
    weight_copy.start()
    copies = []
    for i in range(STEPS):
        some = pl.ds(i * step, step)
        copies.append(pltpu.make_async_copy(x_hbm.at[:, some], x_ref.at[:, some], sems.at[i]))
        copies[-1].start()
    weight_copy.wait()
    for s in range(shots):
        if s % step == 0:
            copies[s // step].wait()
        block = x_ref[:, s].reshape(2 * chans, bins).astype(jnp.float32) * weight_ref[s]
        block = block.astype(jnp.bfloat16).astype(jnp.float32)
        turned[:, :, s, :] = block.T.reshape(planes, depth, 2 * chans)
    for z in range(depth):
        out_ref[z] = turned[:, z].astype(jnp.bfloat16)


def split_parts(first, second):
    half = first.shape[1] // 2
    p = jnp.concatenate([first[:, :half], second[:, :half]], axis=1)
    q = jnp.concatenate([first[:, half:], second[:, half:]], axis=1)
    return p, q


def fill_right(right, base, load, k_rows):
    width = right.shape[1] // 2
    for j in range(width // 128):
        p, q = load(j)
        cols = slice(j * 128, (j + 1) * 128)
        icols = slice(width + j * 128, width + (j + 1) * 128)
        right[base:base + k_rows, cols] = p
        right[base:base + k_rows, icols] = q
        right[base + k_rows:base + 2 * k_rows, cols] = q
        right[base + k_rows:base + 2 * k_rows, icols] = -p


def multiply(left_ref, rights, out_ref, factor):
    rows = left_ref.shape[0]
    step = 256
    for r in range(rows // step):
        at, acc = 0, None
        for right in rights:
            depth = right.shape[0]
            term = jnp.dot(
                left_ref[r * step:(r + 1) * step, at:at + depth],
                right[...],
                preferred_element_type=jnp.float32,
            )
            acc = term if acc is None else acc + term
            at += depth
        out_ref[r * step:(r + 1) * step, :] = (acc * factor).astype(jnp.bfloat16)


def own_kernel(factor, core_ref, a_ref, b_ref, out_ref, left_ref, right):
    depth, k_rows, _ = a_ref.shape
    for h, ref in enumerate((a_ref, b_ref)):
        base = 2 * h * k_rows
        for j in range(depth // 2):
            p, q = split_parts(ref[2 * j], ref[2 * j + 1])
            rows = slice(j * 128, (j + 1) * 128)
            left_ref[rows, base:base + k_rows] = p.T
            left_ref[rows, base + k_rows:base + 2 * k_rows] = q.T
    first = core_ref[0] * (depth // 2)

    for h, ref in enumerate((a_ref, b_ref)):

        def load(j, ref=ref):
            return split_parts(ref[first + 2 * j], ref[first + 2 * j + 1])

        fill_right(right, 2 * h * k_rows, load, k_rows)
    multiply(left_ref, (right,), out_ref, factor)


def right_kernel(y_ref, right):
    fill_right(right, 0, lambda j: split_parts(y_ref[2 * j], y_ref[2 * j + 1]), y_ref.shape[1])


def cross_kernel(factor, left_ref, right_ref, right_other_ref, out_ref):
    multiply(left_ref, (right_ref, right_other_ref), out_ref, factor)


def place_kernel(pieces, half, yh_ref, core_ref, *refs):
    sources, out_hbm, sems = refs[:len(pieces)], refs[-2], refs[-1]
    core = core_ref[0]
    bins, width = out_hbm.shape[1], out_hbm.shape[3] // 4
    copies = []
    for n, (piece, source) in enumerate(zip(pieces, sources)):
        bins_at = core * bins if piece == 0 else 0
        column = (2 * ((yh_ref[0] + half) % 2) + (core + piece) % 2) * width
        for part in range(2):
            copies.append(
                pltpu.make_async_copy(
                    source.at[pl.ds(bins_at, bins), :, pl.ds(part * width, width)],
                    out_hbm.at[part, :, :, pl.ds(pl.multiple_of(column, width), width)],
                    sems.at[2 * n + part],
                )
            )
            copies[-1].start()
    for copy in copies:
        copy.wait()


def place(pieces, half, yh, core, sources, shape, out=None):
    extra = [] if out is None else [out]
    return pl.pallas_call(
        functools.partial(place_kernel, pieces, half),
        out_shape=jax.ShapeDtypeStruct(shape, jnp.bfloat16),
        in_specs=[pl.BlockSpec(memory_space=SMEM)] * 2
        + [pl.BlockSpec(memory_space=VMEM)] * len(sources)
        + [pl.BlockSpec(memory_space=HBM)] * len(extra),
        out_specs=pl.BlockSpec(memory_space=HBM),
        scratch_shapes=[pltpu.SemaphoreType.DMA((2 * len(sources),))],
        input_output_aliases={2 + len(sources): 0} if extra else {},
        compiler_params=PARAMS,
        cost_estimate=pl.CostEstimate(flops=0, bytes_accessed=2 ** 20, transcendentals=0),
    )(yh, core, *sources, *extra)


SWAP = [(0, 1), (1, 0)]


def shards(spectra, shot_weight):
    _, shots, bins, chans = spectra.shape
    depth = lax.axis_size("z")
    planes = lax.axis_size("y") * lax.axis_size("x")
    cores = lax.axis_size("c")
    factor = (shots * planes * cores) ** (-0.5)
    core = lax.axis_index("c").astype(jnp.int32).reshape(1)
    yh = lax.axis_index("yh").astype(jnp.int32).reshape(1)
    lanes = 2 * chans
    k_rows = planes * shots
    rows = depth * chans
    width = 2 * (rows // 2)

    turned = jnp.swapaxes(spectra, 2, 3)
    scaled = vmem_call(
        scale_kernel,
        jax.ShapeDtypeStruct((depth, planes, shots, lanes), jnp.bfloat16),
        [HBM, HBM],
        [
            pltpu.SMEM((shots,), jnp.float32),
            pltpu.VMEM((2, shots, chans, bins), jnp.bfloat16),
            pltpu.VMEM((planes, depth, shots, lanes), jnp.float32),
            pltpu.SemaphoreType.DMA((STEPS + 1,)),
        ],
        nbytes=2 * spectra.size * 2,
        params=pltpu.CompilerParams(vmem_limit_bytes=56 * 1024 * 1024),
    )(shot_weight, turned)
    scaled = scaled.reshape(bins, shots, lanes)
    mine = lax.all_to_all(scaled, ("z", "y", "x"), 0, 0, tiled=True)
    half = bins // cores
    first = lax.axis_index("c") * half
    far = lax.ppermute(lax.dynamic_slice_in_dim(mine, first, half), "yh", SWAP)
    near = lax.ppermute(mine, "c", SWAP)

    flops = 2 * rows * 4 * k_rows * width
    own, left = vmem_call(
        functools.partial(own_kernel, factor),
        (
            jax.ShapeDtypeStruct((rows, width), jnp.bfloat16),
            jax.ShapeDtypeStruct((rows, 4 * k_rows), jnp.bfloat16),
        ),
        [SMEM, VMEM, VMEM],
        [pltpu.VMEM((4 * k_rows, width), jnp.bfloat16)],
        flops=flops,
        nbytes=4 * rows * width * 2,
    )(core, mine.reshape(depth, k_rows, lanes), near.reshape(depth, k_rows, lanes))
    own, near = lax.optimization_barrier((own, near))
    far_other = lax.ppermute(lax.dynamic_slice_in_dim(near, first, half), "yh", SWAP)
    own = lax.all_to_all(own.reshape(depth, chans, width), "z", 0, 0, tiled=True)
    def right_of(part, weight):
        return vmem_call(
            right_kernel,
            jax.ShapeDtypeStruct((2 * k_rows, width), jnp.bfloat16),
            [VMEM],
            flops=weight * flops,
        )(part.reshape(depth // cores, k_rows, lanes))

    right, right_other = right_of(far, 15), right_of(far_other, 0)
    own, right, right_other = lax.optimization_barrier((own, right, right_other))
    per = depth // cores
    shape = (2, per, chans, 2 * rows)
    theirs = (1 - lax.axis_index("c")) * per
    own_other = lax.ppermute(lax.dynamic_slice_in_dim(own, theirs, per), "c", SWAP)
    cross = vmem_call(
        functools.partial(cross_kernel, factor),
        jax.ShapeDtypeStruct((rows, width), jnp.bfloat16),
        [VMEM, VMEM, VMEM],
        flops=flops,
        nbytes=4 * rows * width * 2,
    )(left, right, right_other)
    cross = lax.all_to_all(cross.reshape(depth, chans, width), "z", 0, 0, tiled=True)
    out = place((0, 1), 0, yh, core, (own, own_other), shape)
    out, cross = lax.optimization_barrier((out, cross))
    cross_other = lax.ppermute(lax.dynamic_slice_in_dim(cross, theirs, per), "c", SWAP)
    out = place((0,), 1, yh, core, (cross,), shape, out)
    return place((1,), 1, yh, core, (cross_other,), shape, out)


def solution(mesh):
    fine = Mesh(mesh.devices.reshape(4, 4, 2, 2, 8), ("y", "x", "c", "yh", "z"))
    shot, pair = ("y", "x", "c"), ("yh", "z")
    return jax.shard_map(
        shards,
        mesh=fine,
        in_specs=(P(None, shot, None, pair), P(shot)),
        out_specs=P(None, shot, pair, None),
        check_vma=False,
    )
```

time: 108 us -> 105 us (0.972)
  waiting for transfers between devices: 38.8 us -> 27.7 us
  starting transfers between devices: 23 us -> 30.2 us
  Pallas kernels: 6.24 us -> 8.93 us
  local copies, waits for them, and re-layouts: 1.7 us -> 0.09 us
    ppermute x4, waiting for transfers between devices: 23.1 us -> 11.6 us  [the longest x1 5.66 us: shards(): lax.ppermute(lax.dynamic_slice_in_dim(near, first, half), 'yh', SWAP)]
    all_to_all x1, starting transfers between devices: 3.49 us -> 8.16 us  [shards(): lax.all_to_all(cross.reshape(depth, chans, width), 'z', 0, 0, tiled=True)]
    all_to_all x1, waiting for transfers between devices: 0.01 us -> 3.13 us  [shards(): lax.all_to_all(own.reshape(depth, chans, width), 'z', 0, 0, tiled=True)]
    all_to_all x1, waiting for transfers between devices: 15.6 us -> 13 us  [shards(): lax.all_to_all(cross.reshape(depth, chans, width), 'z', 0, 0, tiled=True)]
    ppermute x4, starting transfers between devices: 12.1 us -> 14.6 us  [the longest x1 4.76 us: shards(): far = lax.ppermute(lax.dynamic_slice_in_dim(mine, first, half), 'yh', SWAP)]
    unnamed x4 -> x0, local copies, waits for them, and re-layouts: 1.7 us -> none
    pallas_call x1, Pallas kernels: 1.28 us -> 2.7 us  [shards(): vmem_call(scale_kernel, jax.ShapeDtypeStruct((depth, planes, shots, lanes...]
    pallas_call x1 -> x5, Pallas kernels: 1.12 us -> 2.52 us  [the longest x3 2.26 us: place(): pl.pallas_call(functools.partial(place_kernel, pieces, half), out_shape=j...]
  transfers between devices with their start and end apart: 7 -> 7, of which waited for: 4 -> 6; matrix products, arithmetic and copies ran while one was open for 0% -> 0% of each run, Pallas kernels for 2% -> 4%
where the time goes in v4:
time: 105 us
  blocking collectives  37.7 us (36%)
  starting transfers between devices  30.2 us (29%)
  waiting for transfers between devices  27.7 us (26%)
  Pallas kernels  8.93 us (9%)
    all_to_all x1, blocking collectives, shards(): mine = lax.all_to_all(scaled, ('z', 'y', 'x'), 0, 0, tiled=True)  37.7 us
    all_to_all x1, waiting for transfers between devices, shards(): lax.all_to_all(cross.reshape(depth, chans, width), 'z', 0, 0, tiled=True)  13 us
    all_to_all x1, starting transfers between devices, shards(): lax.all_to_all(cross.reshape(depth, chans, width), 'z', 0, 0, tiled=True)  8.16 us
    ppermute x1, waiting for transfers between devices, shards(): lax.ppermute(lax.dynamic_slice_in_dim(near, first, half), 'yh', SWAP)  5.66 us
    ppermute x1, starting transfers between devices, shards(): far = lax.ppermute(lax.dynamic_slice_in_dim(mine, first, half), 'yh', SWAP)  4.76 us
    ppermute x1, starting transfers between devices, shards(): lax.ppermute(lax.dynamic_slice_in_dim(near, first, half), 'yh', SWAP)  4.43 us
    ppermute x1, waiting for transfers between devices, shards(): far = lax.ppermute(lax.dynamic_slice_in_dim(mine, first, half), 'yh', SWAP)  4.4 us
    ppermute x1, starting transfers between devices, shards(): near = lax.ppermute(mine, 'c', SWAP)  3.92 us
  transfers between devices with their start and end apart: 7, of which 6 were waited for; matrix products, arithmetic and copies ran while one was open for 0% of the time, Pallas kernels for 4%

profile of v4, /device:TPU:1, one launch (start us, length us, event | category | flops | bytes accessed | tf_op | source)
XLA Modules:
  0.0 104.7 jit_solution(4482618830775690830)
XLA Ops:
  0.0 2.7 %shard_map.28 = bf16[8,16,16,128]{3,2,1,0:T(8,128)(2,1)} custom-call(f32[16]{0:T(128)} %weight_hbm.1, bf16[2,16,64,128]{3,2,1,0:T(8,128)(2,1)} %bitcast.15), custom_call_target="tpu_custom_call" | custom-call | bytes 1048576 | tf_op jit(solution)/shard_map/pallas_call | solution.py:171
  2.7 37.7 %all_to_all.15 = bf16[128,16,128]{2,1,0:T(8,128)(2,1)S(1)} all-to-all(bf16[128,16,128]{2,1,0:T(8,128)(2,1)} %bitcast.14), channel_id=1, replica_groups=mesh['y'=4,'x'=4,'c'=2,'yh'=2,'z'=8] {'z','y','x'}, dimensions={0} | all-to-all | bytes 1048576 | tf_op jit(solution)/shard_map/all_to_all | solution.py:185
  40.4 3.9 %collective-permute-start = (bf16[128,16,128]{2,1,0:T(8,128)(2,1)S(1)}, bf16[128,16,128]{2,1,0:T(8,128)(2,1)S(1)}, u32[]{:S(2)}, u32[]{:S(2)}) collective-permute-start(bf16[128,16,128]{2,1,0:T(8,128)(2,1)S(1)} %all_to_all.15), channel_id=1, source_target_pairs={{0,16},{16,0},{1,17},{17,1},{2,18},{18,2},{3,19},{19,3},{4,20},{20... | collective-permute-start | bytes 1572872 | tf_op jit(solution)/shard_map/ppermute | solution.py:189
  44.4 4.8 %collective-permute-start.1 = (bf16[64,16,128]{2,1,0:T(8,128)(2,1)S(1)}, bf16[64,16,128]{2,1,0:T(8,128)(2,1)S(1)}, u32[]{:S(2)}, u32[]{:S(2)}) collective-permute-start(bf16[64,16,128]{2,1,0:T(8,128)(2,1)S(1)} %constant_dynamic-slice_fusion.3), channel_id=1, source_target_pairs={{0,8},{8,0},{1,9},{9,1},{2,10},{10,2},{3,11},{11,3},{4,12},{12,4},... | collective-permute-start | bytes 786440 | tf_op jit(solution)/shard_map/ppermute | solution.py:188
  49.1 0.0 collective-permute-done
  49.1 2.2 %shard_map.29 = (bf16[512,512]{1,0:T(8,128)(2,1)}, bf16[512,1024]{1,0:T(8,128)(2,1)S(1)}) custom-call(s32[1]{0:T(128)} %bitcast.1.core_ref, bf16[8,256,128]{2,1,0:T(8,128)(2,1)S(1)} %bitcast.10, bf16[8,256,128]{2,1,0:T(8,128)(2,1)S(1)} %bitcast.12), custom_call_target="tpu_custom_call" | custom-call | flops 536870912 | bytes 2097152 | tf_op jit(solution)/shard_map/pallas_call | solution.py:192
  51.3 3.5 %all-to-all-start.1 = ((bf16[8,64,512]{2,1,0:T(8,128)(2,1)}), bf16[8,64,512]{2,1,0:T(8,128)(2,1)S(1)}, u32[]{:S(2)}, u32[]{:S(2)}) async-start(bf16[8,64,512]{2,1,0:T(8,128)(2,1)} %bitcast.6), calls=%async_computation.1 | async-start | bytes 1048576 | tf_op jit(solution)/shard_map/all_to_all | solution.py:205
  54.9 4.4 %collective-permute-start.2 = (bf16[64,16,128]{2,1,0:T(8,128)(2,1)S(1)}, bf16[64,16,128]{2,1,0:T(8,128)(2,1)S(1)}, u32[]{:S(2)}, u32[]{:S(2)}) collective-permute-start(bf16[64,16,128]{2,1,0:T(8,128)(2,1)S(1)} %constant_dynamic-slice_fusion.2), channel_id=1, source_target_pairs={{0,8},{8,0},{1,9},{9,1},{2,10},{10,2},{3,11},{11,3},{4,12},{12,4},... | collective-permute-start | bytes 786440 | tf_op jit(solution)/shard_map/ppermute | solution.py:204
  59.3 4.4 %collective-permute-done.1 = bf16[64,16,128]{2,1,0:T(8,128)(2,1)S(1)} collective-permute-done((bf16[64,16,128]{2,1,0:T(8,128)(2,1)S(1)}, bf16[64,16,128]{2,1,0:T(8,128)(2,1)S(1)}, u32[]{:S(2)}, u32[]{:S(2)}) %collective-permute-start.1) | collective-permute-done | bytes 262176 | tf_op jit(solution)/shard_map/ppermute | solution.py:188
  63.7 0.1 shard_map.30.right_ref
  63.8 5.7 %collective-permute-done.2 = bf16[64,16,128]{2,1,0:T(8,128)(2,1)S(1)} collective-permute-done((bf16[64,16,128]{2,1,0:T(8,128)(2,1)S(1)}, bf16[64,16,128]{2,1,0:T(8,128)(2,1)S(1)}, u32[]{:S(2)}, u32[]{:S(2)}) %collective-permute-start.2) | collective-permute-done | bytes 262176 | tf_op jit(solution)/shard_map/ppermute | solution.py:204
  69.5 0.1 shard_map.31.right_other_ref
  69.6 3.1 %all-to-all-done.1.refs_0_ = bf16[8,64,512]{2,1,0:T(8,128)(2,1)S(1)} async-done(((bf16[8,64,512]{2,1,0:T(8,128)(2,1)}), bf16[8,64,512]{2,1,0:T(8,128)(2,1)S(1)}, u32[]{:S(2)}, u32[]{:S(2)}) %all-to-all-start.1) | async-done | bytes 524320 | tf_op jit(solution)/shard_map/all_to_all | solution.py:205
  72.8 1.5 %shard_map.33 = bf16[512,512]{1,0:T(8,128)(2,1)} custom-call(bf16[512,1024]{1,0:T(8,128)(2,1)S(1)} %get-tuple-element.18.left_ref, bf16[512,512]{1,0:T(8,128)(2,1)S(1)} %shard_map.30.right_ref, bf16[512,512]{1,0:T(8,128)(2,1)S(1)} %shard_map.31.right_other_ref), custom_call_target="tpu_custom_call" | custom-call | flops 536870912 | bytes 2097152 | tf_op jit(solution)/shard_map/pallas_call | solution.py:220
  74.3 8.2 %all-to-all-start.2 = ((bf16[8,64,512]{2,1,0:T(8,128)(2,1)}), bf16[8,64,512]{2,1,0:T(8,128)(2,1)S(1)}, u32[]{:S(2)}, u32[]{:S(2)}) async-start(bf16[8,64,512]{2,1,0:T(8,128)(2,1)} %bitcast.9), calls=%async_computation.2 | async-start | bytes 1048576 | tf_op jit(solution)/shard_map/all_to_all | solution.py:227
  82.5 3.0 %collective-permute-start.3 = (bf16[4,64,512]{2,1,0:T(8,128)(2,1)S(1)}, bf16[4,64,512]{2,1,0:T(8,128)(2,1)S(1)}, u32[]{:S(2)}, u32[]{:S(2)}) collective-permute-start(bf16[4,64,512]{2,1,0:T(8,128)(2,1)S(1)} %constant_dynamic-slice_fusion.1), channel_id=1, source_target_pairs={{0,16},{16,0},{1,17},{17,1},{2,18},{18,2},{3,19},{19,3},{4,20},{20... | collective-permute-start | bytes 786440 | tf_op jit(solution)/shard_map/ppermute | solution.py:219
  85.4 1.1 %collective-permute-done.3.refs_1_ = bf16[4,64,512]{2,1,0:T(8,128)(2,1)S(1)} collective-permute-done((bf16[4,64,512]{2,1,0:T(8,128)(2,1)S(1)}, bf16[4,64,512]{2,1,0:T(8,128)(2,1)S(1)}, u32[]{:S(2)}, u32[]{:S(2)}) %collective-permute-start.3) | collective-permute-done | bytes 262176 | tf_op jit(solution)/shard_map/ppermute | solution.py:219
  86.6 0.8 shard_map.32.refs_1_
  87.4 13.0 %all-to-all-done.2.refs_0_ = bf16[8,64,512]{2,1,0:T(8,128)(2,1)S(1)} async-done(((bf16[8,64,512]{2,1,0:T(8,128)(2,1)}), bf16[8,64,512]{2,1,0:T(8,128)(2,1)S(1)}, u32[]{:S(2)}, u32[]{:S(2)}) %all-to-all-start.2) | async-done | bytes 524320 | tf_op jit(solution)/shard_map/all_to_all | solution.py:227
  100.4 2.4 %collective-permute-start.4 = (bf16[4,64,512]{2,1,0:T(8,128)(2,1)S(1)}, bf16[4,64,512]{2,1,0:T(8,128)(2,1)S(1)}, u32[]{:S(2)}, u32[]{:S(2)}) collective-permute-start(bf16[4,64,512]{2,1,0:T(8,128)(2,1)S(1)} %constant_dynamic-slice_fusion), channel_id=1, source_target_pairs={{0,16},{16,0},{1,17},{17,1},{2,18},{18,2},{3,19},{19,3},{4,20},{20... | collective-permute-start | bytes 786440 | tf_op jit(solution)/shard_map/ppermute | solution.py:230
  102.8 0.7 shard_map.34.refs_1_
  103.6 0.4 collective-permute-done.4.refs_0_
  104.0 0.7 shard_map.35
  (4 shorter events, 0.1 us)
Async XLA Ops:
  40.4 8.7 %collective-permute-start = (bf16[128,16,128]{2,1,0:T(8,128)(2,1)S(1)}, bf16[128,16,128]{2,1,0:T(8,128)(2,1)S(1)}, u32[]{:S(2)}, u32[]{:S(2)}) collective-permute-start(bf16[128,16,128]{2,1,0:T(8,128)(2,1)S(1)} %all_to_all.15), channel_id=1, source_target_pairs={{0,16},{16,0},{1,17},{17,1},{2,18},{18,2},{3,19},{19,3},{4,20},{20... | collective-permute-start | bytes 1572872 | tf_op jit(solution)/shard_map/ppermute | solution.py:189
  44.4 19.3 %collective-permute-start.1 = (bf16[64,16,128]{2,1,0:T(8,128)(2,1)S(1)}, bf16[64,16,128]{2,1,0:T(8,128)(2,1)S(1)}, u32[]{:S(2)}, u32[]{:S(2)}) collective-permute-start(bf16[64,16,128]{2,1,0:T(8,128)(2,1)S(1)} %constant_dynamic-slice_fusion.3), channel_id=1, source_target_pairs={{0,8},{8,0},{1,9},{9,1},{2,10},{10,2},{3,11},{11,3},{4,12},{12,4},... | collective-permute-start | bytes 786440 | tf_op jit(solution)/shard_map/ppermute | solution.py:188
  51.3 21.4 %all-to-all-start.1 = ((bf16[8,64,512]{2,1,0:T(8,128)(2,1)}), bf16[8,64,512]{2,1,0:T(8,128)(2,1)S(1)}, u32[]{:S(2)}, u32[]{:S(2)}) async-start(bf16[8,64,512]{2,1,0:T(8,128)(2,1)} %bitcast.6), calls=%async_computation.1 | async-start | bytes 1048576 | tf_op jit(solution)/shard_map/all_to_all | solution.py:205
  54.9 14.6 %collective-permute-start.2 = (bf16[64,16,128]{2,1,0:T(8,128)(2,1)S(1)}, bf16[64,16,128]{2,1,0:T(8,128)(2,1)S(1)}, u32[]{:S(2)}, u32[]{:S(2)}) collective-permute-start(bf16[64,16,128]{2,1,0:T(8,128)(2,1)S(1)} %constant_dynamic-slice_fusion.2), channel_id=1, source_target_pairs={{0,8},{8,0},{1,9},{9,1},{2,10},{10,2},{3,11},{11,3},{4,12},{12,4},... | collective-permute-start | bytes 786440 | tf_op jit(solution)/shard_map/ppermute | solution.py:204
  74.3 26.1 %all-to-all-start.2 = ((bf16[8,64,512]{2,1,0:T(8,128)(2,1)}), bf16[8,64,512]{2,1,0:T(8,128)(2,1)S(1)}, u32[]{:S(2)}, u32[]{:S(2)}) async-start(bf16[8,64,512]{2,1,0:T(8,128)(2,1)} %bitcast.9), calls=%async_computation.2 | async-start | bytes 1048576 | tf_op jit(solution)/shard_map/all_to_all | solution.py:227
  82.5 4.1 %collective-permute-start.3 = (bf16[4,64,512]{2,1,0:T(8,128)(2,1)S(1)}, bf16[4,64,512]{2,1,0:T(8,128)(2,1)S(1)}, u32[]{:S(2)}, u32[]{:S(2)}) collective-permute-start(bf16[4,64,512]{2,1,0:T(8,128)(2,1)S(1)} %constant_dynamic-slice_fusion.1), channel_id=1, source_target_pairs={{0,16},{16,0},{1,17},{17,1},{2,18},{18,2},{3,19},{19,3},{4,20},{20... | collective-permute-start | bytes 786440 | tf_op jit(solution)/shard_map/ppermute | solution.py:219
  100.4 3.6 %collective-permute-start.4 = (bf16[4,64,512]{2,1,0:T(8,128)(2,1)S(1)}, bf16[4,64,512]{2,1,0:T(8,128)(2,1)S(1)}, u32[]{:S(2)}, u32[]{:S(2)}) collective-permute-start(bf16[4,64,512]{2,1,0:T(8,128)(2,1)S(1)} %constant_dynamic-slice_fusion), channel_id=1, source_target_pairs={{0,16},{16,0},{1,17},{17,1},{2,18},{18,2},{3,19},{19,3},{4,20},{20... | collective-permute-start | bytes 786440 | tf_op jit(solution)/shard_map/ppermute | solution.py:230

commit v5 on v4

v5 whole, which is shorter than its diff:
```python
import functools

import jax
import jax.numpy as jnp
from jax import lax
from jax.experimental import pallas as pl
from jax.experimental.pallas import tpu as pltpu
from jax.sharding import Mesh, PartitionSpec as P

VMEM = pltpu.MemorySpace.VMEM
SMEM = pltpu.MemorySpace.SMEM
HBM = pltpu.MemorySpace.HBM
STEPS = 4
PARAMS = pltpu.CompilerParams(vmem_limit_bytes=32 * 1024 * 1024)


def vmem_call(body, out_shape, in_spaces, scratch=(), flops=0, nbytes=0, params=PARAMS):
    outs = out_shape if isinstance(out_shape, (list, tuple)) else (out_shape,)
    specs = [pl.BlockSpec(memory_space=VMEM) for _ in outs]
    return pl.pallas_call(
        body,
        out_shape=out_shape,
        in_specs=[pl.BlockSpec(memory_space=s) for s in in_spaces],
        out_specs=specs if isinstance(out_shape, (list, tuple)) else specs[0],
        scratch_shapes=list(scratch),
        compiler_params=params,
        cost_estimate=pl.CostEstimate(flops=flops, bytes_accessed=nbytes, transcendentals=0),
    )


def scale_kernel(weight_hbm, x_hbm, out_ref, weight_ref, x_ref, turned, sems):
    _, shots, chans, bins = x_ref.shape
    planes, depth = turned.shape[0], turned.shape[1]
    step = shots // STEPS
    weight_copy = pltpu.make_async_copy(weight_hbm, weight_ref, sems.at[STEPS])
    weight_copy.start()
    copies = []
    for i in range(STEPS):
        some = pl.ds(i * step, step)
        copies.append(pltpu.make_async_copy(x_hbm.at[:, some], x_ref.at[:, some], sems.at[i]))
        copies[-1].start()
    weight_copy.wait()
    for s in range(shots):
        if s % step == 0:
            copies[s // step].wait()
        block = x_ref[:, s].reshape(2 * chans, bins).astype(jnp.float32) * weight_ref[s]
        block = block.astype(jnp.bfloat16).astype(jnp.float32)
        turned[:, :, s, :] = block.T.reshape(planes, depth, 2 * chans)
    for z in range(depth):
        out_ref[z] = turned[:, z].astype(jnp.bfloat16)


def split_parts(first, second):
    half = first.shape[1] // 2
    p = jnp.concatenate([first[:, :half], second[:, :half]], axis=1)
    q = jnp.concatenate([first[:, half:], second[:, half:]], axis=1)
    return p, q


def fill_right(right, base, load, k_rows):
    width = right.shape[1] // 2
    for j in range(width // 128):
        p, q = load(j)
        cols = slice(j * 128, (j + 1) * 128)
        icols = slice(width + j * 128, width + (j + 1) * 128)
        right[base:base + k_rows, cols] = p
        right[base:base + k_rows, icols] = q
        right[base + k_rows:base + 2 * k_rows, cols] = q
        right[base + k_rows:base + 2 * k_rows, icols] = -p


def multiply(left_ref, rights, out_ref, factor):
    rows = left_ref.shape[0]
    step = 256
    for r in range(rows // step):
        at, acc = 0, None
        for right in rights:
            depth = right.shape[0]
            term = jnp.dot(
                left_ref[r * step:(r + 1) * step, at:at + depth],
                right[...],
                preferred_element_type=jnp.float32,
            )
            acc = term if acc is None else acc + term
            at += depth
        out_ref[r * step:(r + 1) * step, :] = (acc * factor).astype(jnp.bfloat16)


def left_kernel(a_ref, b_ref, left_ref):
    blocks, k_rows, _ = a_ref.shape
    for h, ref in enumerate((a_ref, b_ref)):
        base = 2 * h * k_rows
        for j in range(blocks // 2):
            p, q = split_parts(ref[2 * j], ref[2 * j + 1])
            rows = slice(j * 128, (j + 1) * 128)
            left_ref[rows, base:base + k_rows] = p.T
            left_ref[rows, base + k_rows:base + 2 * k_rows] = q.T


def gram_kernel(factor, zl_ref, left_ref, a_ref, b_ref, a_far_ref, b_far_ref, out_ref, right):
    k_rows = a_ref.shape[1]
    for zl in range(2):

        @pl.when(zl_ref[0] == zl)
        def _(zl=zl):
            for h, pair in enumerate(((a_ref, a_far_ref), (b_ref, b_far_ref))):

                def load(j, pair=pair):
                    return split_parts(pair[zl][j], pair[1 - zl][j])

                fill_right(right, 2 * h * k_rows, load, k_rows)

    multiply(left_ref, (right,), out_ref, factor)


def place_kernel(piece, core_ref, source, *refs):
    out_hbm, sems = refs[-2], refs[-1]
    core = core_ref[0]
    bins, width = out_hbm.shape[1], out_hbm.shape[3] // 2
    bins_at = core * bins if piece == 0 else 0
    column = pl.multiple_of((core + piece) % 2 * width, width)
    copies = []
    for part in range(2):
        copies.append(
            pltpu.make_async_copy(
                source.at[pl.ds(bins_at, bins), :, pl.ds(part * width, width)],
                out_hbm.at[part, :, :, pl.ds(column, width)],
                sems.at[part],
            )
        )
        copies[-1].start()
    for copy in copies:
        copy.wait()


def place(piece, core, source, shape, out=None):
    extra = [] if out is None else [out]
    return pl.pallas_call(
        functools.partial(place_kernel, piece),
        out_shape=jax.ShapeDtypeStruct(shape, jnp.bfloat16),
        in_specs=[pl.BlockSpec(memory_space=SMEM), pl.BlockSpec(memory_space=VMEM)]
        + [pl.BlockSpec(memory_space=HBM)] * len(extra),
        out_specs=pl.BlockSpec(memory_space=HBM),
        scratch_shapes=[pltpu.SemaphoreType.DMA((2,))],
        input_output_aliases={2: 0} if extra else {},
        compiler_params=PARAMS,
        cost_estimate=pl.CostEstimate(flops=0, bytes_accessed=2 ** 20, transcendentals=0),
    )(core, source, *extra)


SWAP = [(0, 1), (1, 0)]


def shards(spectra, shot_weight):
    _, shots, bins, chans = spectra.shape
    depth = lax.axis_size("yh") * lax.axis_size("zh")
    planes = lax.axis_size("y") * lax.axis_size("x")
    cores = lax.axis_size("c")
    factor = (shots * planes * cores) ** (-0.5)
    core = lax.axis_index("c").astype(jnp.int32).reshape(1)
    zl = lax.axis_index("zl").astype(jnp.int32).reshape(1)
    lanes = 2 * chans
    k_rows = planes * shots
    rows = depth * chans
    width = 2 * rows

    turned = jnp.swapaxes(spectra, 2, 3)
    scaled = vmem_call(
        scale_kernel,
        jax.ShapeDtypeStruct((depth, planes, shots, lanes), jnp.bfloat16),
        [HBM, HBM],
        [
            pltpu.SMEM((shots,), jnp.float32),
            pltpu.VMEM((2, shots, chans, bins), jnp.bfloat16),
            pltpu.VMEM((planes, depth, shots, lanes), jnp.float32),
            pltpu.SemaphoreType.DMA((STEPS + 1,)),
        ],
        nbytes=2 * spectra.size * 2,
        params=pltpu.CompilerParams(vmem_limit_bytes=56 * 1024 * 1024),
    )(shot_weight, turned)
    scaled = scaled.reshape(bins, shots, lanes)
    mine = lax.all_to_all(scaled, ("yh", "zh", "y", "x"), 0, 0, tiled=True)
    half = bins // cores
    first = lax.axis_index("c") * half
    near = lax.ppermute(mine, "c", SWAP)
    mine_part = lax.dynamic_slice_in_dim(mine, first, half)
    near_part = lax.dynamic_slice_in_dim(near, first, half)
    far = lax.ppermute(mine_part, "zl", SWAP)
    far_other = lax.ppermute(near_part, "zl", SWAP)

    left = vmem_call(
        left_kernel,
        jax.ShapeDtypeStruct((rows, 4 * k_rows), jnp.bfloat16),
        [VMEM, VMEM],
        nbytes=4 * rows * width,
    )(mine.reshape(depth, k_rows, lanes), near.reshape(depth, k_rows, lanes))
    parts = [x.reshape(depth // cores, k_rows, lanes) for x in (mine_part, near_part, far, far_other)]
    gram = vmem_call(
        functools.partial(gram_kernel, factor),
        jax.ShapeDtypeStruct((rows, width), jnp.bfloat16),
        [SMEM] + [VMEM] * 5,
        [pltpu.VMEM((4 * k_rows, width), jnp.bfloat16)],
        flops=2 * rows * 4 * k_rows * width,
        nbytes=4 * rows * width * 2,
    )(zl, left, *parts)
    gram = lax.all_to_all(gram.reshape(depth, chans, width), ("yh", "zh"), 0, 0, tiled=True)
    per = depth // cores
    theirs = (1 - lax.axis_index("c")) * per
    other = lax.ppermute(lax.dynamic_slice_in_dim(gram, theirs, per), "c", SWAP)
    shape = (2, per, chans, 2 * rows)
    return place(1, core, other, shape, place(0, core, gram, shape))


def solution(mesh):
    fine = Mesh(mesh.devices.reshape(4, 4, 2, 2, 4, 2), ("y", "x", "c", "yh", "zh", "zl"))
    shot, pair = ("y", "x", "c"), ("yh", "zh", "zl")
    return jax.shard_map(
        shards,
        mesh=fine,
        in_specs=(P(None, shot, None, pair), P(shot)),
        out_specs=P(None, shot, pair, None),
        check_vma=False,
    )
```

time: 105 us -> 112 us (1.067)
  the two profiles are of different devices: /device:TPU:1 before, /device:TPU:9 now
where the time goes in v5:
time: 112 us; the launch traced here: 111 us
  waiting for transfers between devices  44.4 us (40%)
  blocking collectives  40.6 us (36%)
  starting transfers between devices  18.3 us (16%)
  Pallas kernels  7.85 us (7%)
    all_to_all x1, blocking collectives, shards(): mine = lax.all_to_all(scaled, ('yh', 'zh', 'y', 'x'), 0, 0, tiled=True)  40.6 us
    all_to_all x1, waiting for transfers between devices, shards(): lax.all_to_all(gram.reshape(depth, chans, width), ('yh', 'zh'), 0, 0, til...  34.5 us
    ppermute x1, waiting for transfers between devices, shards(): far_other = lax.ppermute(near_part, 'zl', SWAP)  5.62 us
    ppermute x1, starting transfers between devices, shards(): other = lax.ppermute(lax.dynamic_slice_in_dim(gram, theirs, per), 'c', SWAP)  5.01 us
    ppermute x1, starting transfers between devices, shards(): near = lax.ppermute(mine, 'c', SWAP)  4.46 us
    all_to_all x1, starting transfers between devices, shards(): lax.all_to_all(gram.reshape(depth, chans, width), ('yh', 'zh'), 0, 0, til...  3.56 us
    ppermute x1, waiting for transfers between devices, shards(): far = lax.ppermute(mine_part, 'zl', SWAP)  3.55 us
    ppermute x1, starting transfers between devices, shards(): far = lax.ppermute(mine_part, 'zl', SWAP)  3.09 us
  transfers between devices with their start and end apart: 5, of which 4 were waited for; matrix products, arithmetic and copies ran while one was open for 0% of the time, Pallas kernels for 2%

profile of v5, /device:TPU:9, one launch (start us, length us, event | category | flops | bytes accessed | tf_op | source)
XLA Modules:
  0.0 111.3 jit_solution(13676184462913373001)
XLA Ops:
  0.0 2.7 %shard_map.28 = bf16[8,16,16,128]{3,2,1,0:T(8,128)(2,1)} custom-call(f32[16]{0:T(128)} %weight_hbm.1, bf16[2,16,64,128]{3,2,1,0:T(8,128)(2,1)} %bitcast.18), custom_call_target="tpu_custom_call" | custom-call | bytes 1048576 | tf_op jit(solution)/shard_map/pallas_call | solution.py:168
  2.7 40.6 %all_to_all.10 = bf16[128,16,128]{2,1,0:T(8,128)(2,1)S(1)} all-to-all(bf16[128,16,128]{2,1,0:T(8,128)(2,1)} %bitcast.17), channel_id=1, replica_groups=mesh['y'=4,'x'=4,'c'=2,'yh'=2,'zh'=4,'zl'=2] {'yh','zh','y','x'}, dimensions={0} | all-to-all | bytes 1048576 | tf_op jit(solution)/shard_map/all_to_all | solution.py:182
  43.3 4.5 %collective-permute-start = (bf16[128,16,128]{2,1,0:T(8,128)(2,1)S(1)}, bf16[128,16,128]{2,1,0:T(8,128)(2,1)S(1)}, u32[]{:S(2)}, u32[]{:S(2)}) collective-permute-start(bf16[128,16,128]{2,1,0:T(8,128)(2,1)S(1)} %all_to_all.10), channel_id=1, source_target_pairs={{0,16},{16,0},{1,17},{17,1},{2,18},{18,2},{3,19},{19,3},{4,20},{20... | collective-permute-start | bytes 1572872 | tf_op jit(solution)/shard_map/ppermute | solution.py:185
  47.8 3.1 %collective-permute-start.1 = (bf16[64,16,128]{2,1,0:T(8,128)(2,1)S(1)}, bf16[64,16,128]{2,1,0:T(8,128)(2,1)S(1)}, u32[]{:S(2)}, u32[]{:S(2)}) collective-permute-start(bf16[64,16,128]{2,1,0:T(8,128)(2,1)S(1)} %constant_dynamic-slice_fusion.2), channel_id=1, source_target_pairs={{0,1},{1,0},{2,3},{3,2},{4,5},{5,4},{6,7},{7,6},{8,9},{9,8},{10,11... | collective-permute-start | bytes 786440 | tf_op jit(solution)/shard_map/ppermute | solution.py:188
  50.9 0.0 collective-permute-done
  50.9 2.2 %collective-permute-start.2 = (bf16[64,16,128]{2,1,0:T(8,128)(2,1)S(1)}, bf16[64,16,128]{2,1,0:T(8,128)(2,1)S(1)}, u32[]{:S(2)}, u32[]{:S(2)}) collective-permute-start(bf16[64,16,128]{2,1,0:T(8,128)(2,1)S(1)} %constant_dynamic-slice_fusion.1), channel_id=1, source_target_pairs={{0,1},{1,0},{2,3},{3,2},{4,5},{5,4},{6,7},{7,6},{8,9},{9,8},{10,11... | collective-permute-start | bytes 786440 | tf_op jit(solution)/shard_map/ppermute | solution.py:189
  53.1 0.9 shard_map.29.left_ref
  54.1 3.5 %collective-permute-done.1 = bf16[64,16,128]{2,1,0:T(8,128)(2,1)S(1)} collective-permute-done((bf16[64,16,128]{2,1,0:T(8,128)(2,1)S(1)}, bf16[64,16,128]{2,1,0:T(8,128)(2,1)S(1)}, u32[]{:S(2)}, u32[]{:S(2)}) %collective-permute-start.1) | collective-permute-done | bytes 262176 | tf_op jit(solution)/shard_map/ppermute | solution.py:188
  57.6 5.6 %collective-permute-done.2 = bf16[64,16,128]{2,1,0:T(8,128)(2,1)S(1)} collective-permute-done((bf16[64,16,128]{2,1,0:T(8,128)(2,1)S(1)}, bf16[64,16,128]{2,1,0:T(8,128)(2,1)S(1)}, u32[]{:S(2)}, u32[]{:S(2)}) %collective-permute-start.2) | collective-permute-done | bytes 262176 | tf_op jit(solution)/shard_map/ppermute | solution.py:189
  63.2 2.6 %shard_map.30 = bf16[512,1024]{1,0:T(8,128)(2,1)} custom-call(s32[1]{0:T(128)} %bitcast.1.zl_ref, bf16[512,1024]{1,0:T(8,128)(2,1)S(1)} %shard_map.29.left_ref, bf16[4,256,128]{2,1,0:T(8,128)(2,1)S(1)} %bitcast.13, bf16[4,256,128]{2,1,0:T(8,128)(2,1)S(1)} %bitcast.14, bf16[4,256,128]{2,1,0:T(8,128)(2,1)S(1)} %bitcast.15, bf16[4,256,128]{2,1,0:T(8,128)(2,1)S(1)} %bitcast.16), custom_call_target="tpu_custom_call" | custom-call | flops 1073741824 | bytes 4194304 | tf_op jit(solution)/shard_map/pallas_call | solution.py:198
  65.8 3.6 %all-to-all-start.1 = ((bf16[8,64,1024]{2,1,0:T(8,128)(2,1)}), bf16[8,64,1024]{2,1,0:T(8,128)(2,1)S(1)}, u32[]{:S(2)}, u32[]{:S(2)}) async-start(bf16[8,64,1024]{2,1,0:T(8,128)(2,1)} %bitcast.10), calls=%async_computation.1 | async-start | bytes 2097152 | tf_op jit(solution)/shard_map/all_to_all | solution.py:206
  69.4 34.5 %all-to-all-done.1.source = bf16[8,64,1024]{2,1,0:T(8,128)(2,1)S(1)} async-done(((bf16[8,64,1024]{2,1,0:T(8,128)(2,1)}), bf16[8,64,1024]{2,1,0:T(8,128)(2,1)S(1)}, u32[]{:S(2)}, u32[]{:S(2)}) %all-to-all-start.1) | async-done | bytes 1048608 | tf_op jit(solution)/shard_map/all_to_all | solution.py:206
  104.0 5.0 %collective-permute-start.3 = (bf16[4,64,1024]{2,1,0:T(8,128)(2,1)S(1)}, bf16[4,64,1024]{2,1,0:T(8,128)(2,1)S(1)}, u32[]{:S(2)}, u32[]{:S(2)}) collective-permute-start(bf16[4,64,1024]{2,1,0:T(8,128)(2,1)S(1)} %constant_dynamic-slice_fusion), channel_id=1, source_target_pairs={{0,16},{16,0},{1,17},{17,1},{2,18},{18,2},{3,19},{19,3},{4,20},{20... | collective-permute-start | bytes 1572872 | tf_op jit(solution)/shard_map/ppermute | solution.py:209
  109.0 0.8 shard_map.31.refs_0_
  109.8 0.7 collective-permute-done.3.source
  110.5 0.8 shard_map.32
  (3 shorter events, 0.1 us)
Async XLA Ops:
  43.3 7.6 %collective-permute-start = (bf16[128,16,128]{2,1,0:T(8,128)(2,1)S(1)}, bf16[128,16,128]{2,1,0:T(8,128)(2,1)S(1)}, u32[]{:S(2)}, u32[]{:S(2)}) collective-permute-start(bf16[128,16,128]{2,1,0:T(8,128)(2,1)S(1)} %all_to_all.10), channel_id=1, source_target_pairs={{0,16},{16,0},{1,17},{17,1},{2,18},{18,2},{3,19},{19,3},{4,20},{20... | collective-permute-start | bytes 1572872 | tf_op jit(solution)/shard_map/ppermute | solution.py:185
  47.8 9.8 %collective-permute-start.1 = (bf16[64,16,128]{2,1,0:T(8,128)(2,1)S(1)}, bf16[64,16,128]{2,1,0:T(8,128)(2,1)S(1)}, u32[]{:S(2)}, u32[]{:S(2)}) collective-permute-start(bf16[64,16,128]{2,1,0:T(8,128)(2,1)S(1)} %constant_dynamic-slice_fusion.2), channel_id=1, source_target_pairs={{0,1},{1,0},{2,3},{3,2},{4,5},{5,4},{6,7},{7,6},{8,9},{9,8},{10,11... | collective-permute-start | bytes 786440 | tf_op jit(solution)/shard_map/ppermute | solution.py:188
  50.9 12.3 %collective-permute-start.2 = (bf16[64,16,128]{2,1,0:T(8,128)(2,1)S(1)}, bf16[64,16,128]{2,1,0:T(8,128)(2,1)S(1)}, u32[]{:S(2)}, u32[]{:S(2)}) collective-permute-start(bf16[64,16,128]{2,1,0:T(8,128)(2,1)S(1)} %constant_dynamic-slice_fusion.1), channel_id=1, source_target_pairs={{0,1},{1,0},{2,3},{3,2},{4,5},{5,4},{6,7},{7,6},{8,9},{9,8},{10,11... | collective-permute-start | bytes 786440 | tf_op jit(solution)/shard_map/ppermute | solution.py:189
  65.8 38.1 %all-to-all-start.1 = ((bf16[8,64,1024]{2,1,0:T(8,128)(2,1)}), bf16[8,64,1024]{2,1,0:T(8,128)(2,1)S(1)}, u32[]{:S(2)}, u32[]{:S(2)}) async-start(bf16[8,64,1024]{2,1,0:T(8,128)(2,1)} %bitcast.10), calls=%async_computation.1 | async-start | bytes 2097152 | tf_op jit(solution)/shard_map/all_to_all | solution.py:206
  104.0 6.5 %collective-permute-start.3 = (bf16[4,64,1024]{2,1,0:T(8,128)(2,1)S(1)}, bf16[4,64,1024]{2,1,0:T(8,128)(2,1)S(1)}, u32[]{:S(2)}, u32[]{:S(2)}) collective-permute-start(bf16[4,64,1024]{2,1,0:T(8,128)(2,1)S(1)} %constant_dynamic-slice_fusion), channel_id=1, source_target_pairs={{0,16},{16,0},{1,17},{17,1},{2,18},{18,2},{3,19},{19,3},{4,20},{20... | collective-permute-start | bytes 1572872 | tf_op jit(solution)/shard_map/ppermute | solution.py:209

commit v6 on v4

--- a/solution.py
+++ b/solution.py
@@ -106,12 +106,23 @@
     multiply(left_ref, (right,), out_ref, factor)
 
 
-def right_kernel(y_ref, right):
-    fill_right(right, 0, lambda j: split_parts(y_ref[2 * j], y_ref[2 * j + 1]), y_ref.shape[1])
-
-
-def cross_kernel(factor, left_ref, right_ref, right_other_ref, out_ref):
-    multiply(left_ref, (right_ref, right_other_ref), out_ref, factor)
+def first_kernel(left_ref, y_ref, out_ref, right):
+    k_rows = y_ref.shape[1]
+    fill_right(right, 0, lambda j: split_parts(y_ref[2 * j], y_ref[2 * j + 1]), k_rows)
+    out_ref[...] = jnp.dot(
+        left_ref[:, :2 * k_rows], right[...], preferred_element_type=jnp.float32
+    )
+
+
+def second_kernel(factor, left_ref, y_ref, first_ref, out_ref, right):
+    k_rows, step = y_ref.shape[1], 128
+    fill_right(right, 0, lambda j: split_parts(y_ref[2 * j], y_ref[2 * j + 1]), k_rows)
+    for r in range(left_ref.shape[0] // step):
+        rows = slice(r * step, (r + 1) * step)
+        acc = first_ref[rows] + jnp.dot(
+            left_ref[rows, 2 * k_rows:], right[...], preferred_element_type=jnp.float32
+        )
+        out_ref[rows] = (acc * factor).astype(jnp.bfloat16)
 
 
 def place_kernel(pieces, half, yh_ref, core_ref, *refs):
@@ -203,27 +214,28 @@
     own, near = lax.optimization_barrier((own, near))
     far_other = lax.ppermute(lax.dynamic_slice_in_dim(near, first, half), "yh", SWAP)
     own = lax.all_to_all(own.reshape(depth, chans, width), "z", 0, 0, tiled=True)
-    def right_of(part, weight):
-        return vmem_call(
-            right_kernel,
-            jax.ShapeDtypeStruct((2 * k_rows, width), jnp.bfloat16),
-            [VMEM],
-            flops=weight * flops,
-        )(part.reshape(depth // cores, k_rows, lanes))
-
-    right, right_other = right_of(far, 15), right_of(far_other, 0)
-    own, right, right_other = lax.optimization_barrier((own, right, right_other))
+    half_right = [pltpu.VMEM((2 * k_rows, width), jnp.bfloat16)]
+    part = (depth // cores, k_rows, lanes)
+    cross = vmem_call(
+        first_kernel,
+        jax.ShapeDtypeStruct((rows, width), jnp.float32),
+        [VMEM, VMEM],
+        half_right,
+        flops=15 * flops,
+    )(left, far.reshape(part))
+    own, cross, far_other = lax.optimization_barrier((own, cross, far_other))
     per = depth // cores
     shape = (2, per, chans, 2 * rows)
     theirs = (1 - lax.axis_index("c")) * per
     own_other = lax.ppermute(lax.dynamic_slice_in_dim(own, theirs, per), "c", SWAP)
     cross = vmem_call(
-        functools.partial(cross_kernel, factor),
+        functools.partial(second_kernel, factor),
         jax.ShapeDtypeStruct((rows, width), jnp.bfloat16),
         [VMEM, VMEM, VMEM],
+        half_right,
         flops=flops,
         nbytes=4 * rows * width * 2,
-    )(left, right, right_other)
+    )(left, far_other.reshape(part), cross)
     cross = lax.all_to_all(cross.reshape(depth, chans, width), "z", 0, 0, tiled=True)
     out = place((0, 1), 0, yh, core, (own, own_other), shape)
     out, cross = lax.optimization_barrier((out, cross))

time: 105 us -> 105 us (level)
  no operation moved by 1% of the time
where the time goes in v6:
time: 105 us; the launch traced here: 104 us
  blocking collectives  37.7 us (36%)
  starting transfers between devices  30 us (29%)
  waiting for transfers between devices  27.4 us (26%)
  Pallas kernels  9.11 us (9%)
    all_to_all x1, blocking collectives, shards(): mine = lax.all_to_all(scaled, ('z', 'y', 'x'), 0, 0, tiled=True)  37.7 us
    all_to_all x1, waiting for transfers between devices, shards(): lax.all_to_all(cross.reshape(depth, chans, width), 'z', 0, 0, tiled=True)  13 us
    all_to_all x1, starting transfers between devices, shards(): lax.all_to_all(cross.reshape(depth, chans, width), 'z', 0, 0, tiled=True)  8.01 us
    ppermute x1, waiting for transfers between devices, shards(): lax.ppermute(lax.dynamic_slice_in_dim(near, first, half), 'yh', SWAP)  5.22 us
    ppermute x1, starting transfers between devices, shards(): far = lax.ppermute(lax.dynamic_slice_in_dim(mine, first, half), 'yh', SWAP)  4.76 us
    ppermute x1, starting transfers between devices, shards(): lax.ppermute(lax.dynamic_slice_in_dim(near, first, half), 'yh', SWAP)  4.43 us
    ppermute x1, waiting for transfers between devices, shards(): far = lax.ppermute(lax.dynamic_slice_in_dim(mine, first, half), 'yh', SWAP)  4.4 us
    ppermute x1, starting transfers between devices, shards(): near = lax.ppermute(mine, 'c', SWAP)  3.92 us
  transfers between devices with their start and end apart: 7, of which 6 were waited for; matrix products, arithmetic and copies ran while one was open for 0% of the time, Pallas kernels for 4%

profile of v6, /device:TPU:1, one launch (start us, length us, event | category | flops | bytes accessed | tf_op | source)
XLA Modules:
  0.0 104.4 jit_solution(15279947918736593705)
XLA Ops:
  0.0 2.7 %shard_map.28 = bf16[8,16,16,128]{3,2,1,0:T(8,128)(2,1)} custom-call(f32[16]{0:T(128)} %weight_hbm.1, bf16[2,16,64,128]{3,2,1,0:T(8,128)(2,1)} %bitcast.15), custom_call_target="tpu_custom_call" | custom-call | bytes 1048576 | tf_op jit(solution)/shard_map/pallas_call | solution.py:182
  2.7 37.7 %all_to_all.15 = bf16[128,16,128]{2,1,0:T(8,128)(2,1)S(1)} all-to-all(bf16[128,16,128]{2,1,0:T(8,128)(2,1)} %bitcast.14), channel_id=1, replica_groups=mesh['y'=4,'x'=4,'c'=2,'yh'=2,'z'=8] {'z','y','x'}, dimensions={0} | all-to-all | bytes 1048576 | tf_op jit(solution)/shard_map/all_to_all | solution.py:196
  40.4 3.9 %collective-permute-start = (bf16[128,16,128]{2,1,0:T(8,128)(2,1)S(1)}, bf16[128,16,128]{2,1,0:T(8,128)(2,1)S(1)}, u32[]{:S(2)}, u32[]{:S(2)}) collective-permute-start(bf16[128,16,128]{2,1,0:T(8,128)(2,1)S(1)} %all_to_all.15), channel_id=1, source_target_pairs={{0,16},{16,0},{1,17},{17,1},{2,18},{18,2},{3,19},{19,3},{4,20},{20... | collective-permute-start | bytes 1572872 | tf_op jit(solution)/shard_map/ppermute | solution.py:200
  44.4 4.8 %collective-permute-start.1 = (bf16[64,16,128]{2,1,0:T(8,128)(2,1)S(1)}, bf16[64,16,128]{2,1,0:T(8,128)(2,1)S(1)}, u32[]{:S(2)}, u32[]{:S(2)}) collective-permute-start(bf16[64,16,128]{2,1,0:T(8,128)(2,1)S(1)} %constant_dynamic-slice_fusion.3), channel_id=1, source_target_pairs={{0,8},{8,0},{1,9},{9,1},{2,10},{10,2},{3,11},{11,3},{4,12},{12,4},... | collective-permute-start | bytes 786440 | tf_op jit(solution)/shard_map/ppermute | solution.py:199
  49.1 0.0 collective-permute-done
  49.1 2.2 %shard_map.29 = (bf16[512,512]{1,0:T(8,128)(2,1)}, bf16[512,1024]{1,0:T(8,128)(2,1)S(1)}) custom-call(s32[1]{0:T(128)} %bitcast.1.core_ref, bf16[8,256,128]{2,1,0:T(8,128)(2,1)S(1)} %bitcast.10, bf16[8,256,128]{2,1,0:T(8,128)(2,1)S(1)} %bitcast.12), custom_call_target="tpu_custom_call" | custom-call | flops 536870912 | bytes 2097152 | tf_op jit(solution)/shard_map/pallas_call | solution.py:203
  51.3 3.5 %all-to-all-start.1 = ((bf16[8,64,512]{2,1,0:T(8,128)(2,1)}), bf16[8,64,512]{2,1,0:T(8,128)(2,1)S(1)}, u32[]{:S(2)}, u32[]{:S(2)}) async-start(bf16[8,64,512]{2,1,0:T(8,128)(2,1)} %bitcast.6), calls=%async_computation.1 | async-start | bytes 1048576 | tf_op jit(solution)/shard_map/all_to_all | solution.py:216
  54.9 4.4 %collective-permute-start.2 = (bf16[64,16,128]{2,1,0:T(8,128)(2,1)S(1)}, bf16[64,16,128]{2,1,0:T(8,128)(2,1)S(1)}, u32[]{:S(2)}, u32[]{:S(2)}) collective-permute-start(bf16[64,16,128]{2,1,0:T(8,128)(2,1)S(1)} %constant_dynamic-slice_fusion.2), channel_id=1, source_target_pairs={{0,8},{8,0},{1,9},{9,1},{2,10},{10,2},{3,11},{11,3},{4,12},{12,4},... | collective-permute-start | bytes 786440 | tf_op jit(solution)/shard_map/ppermute | solution.py:215
  59.3 4.4 %collective-permute-done.1 = bf16[64,16,128]{2,1,0:T(8,128)(2,1)S(1)} collective-permute-done((bf16[64,16,128]{2,1,0:T(8,128)(2,1)S(1)}, bf16[64,16,128]{2,1,0:T(8,128)(2,1)S(1)}, u32[]{:S(2)}, u32[]{:S(2)}) %collective-permute-start.1) | collective-permute-done | bytes 262176 | tf_op jit(solution)/shard_map/ppermute | solution.py:199
  63.7 0.6 shard_map.30.first_ref
  64.3 5.2 %collective-permute-done.2 = bf16[64,16,128]{2,1,0:T(8,128)(2,1)S(1)} collective-permute-done((bf16[64,16,128]{2,1,0:T(8,128)(2,1)S(1)}, bf16[64,16,128]{2,1,0:T(8,128)(2,1)S(1)}, u32[]{:S(2)}, u32[]{:S(2)}) %collective-permute-start.2) | collective-permute-done | bytes 262176 | tf_op jit(solution)/shard_map/ppermute | solution.py:215
  69.5 3.3 %all-to-all-done.1.refs_0_ = bf16[8,64,512]{2,1,0:T(8,128)(2,1)S(1)} async-done(((bf16[8,64,512]{2,1,0:T(8,128)(2,1)}), bf16[8,64,512]{2,1,0:T(8,128)(2,1)S(1)}, u32[]{:S(2)}, u32[]{:S(2)}) %all-to-all-start.1) | async-done | bytes 524320 | tf_op jit(solution)/shard_map/all_to_all | solution.py:216
  72.8 1.4 %shard_map.32 = bf16[512,512]{1,0:T(8,128)(2,1)} custom-call(bf16[512,1024]{1,0:T(8,128)(2,1)S(1)} %get-tuple-element.16.left_ref, bf16[4,256,128]{2,1,0:T(8,128)(2,1)S(1)} %bitcast.11, f32[512,512]{1,0:T(8,128)S(1)} %shard_map.30.first_ref), custom_call_target="tpu_custom_call" | custom-call | flops 536870912 | bytes 2097152 | tf_op jit(solution)/shard_map/pallas_call | solution.py:231
  74.2 8.0 %all-to-all-start.2 = ((bf16[8,64,512]{2,1,0:T(8,128)(2,1)}), bf16[8,64,512]{2,1,0:T(8,128)(2,1)S(1)}, u32[]{:S(2)}, u32[]{:S(2)}) async-start(bf16[8,64,512]{2,1,0:T(8,128)(2,1)} %bitcast.9), calls=%async_computation.2 | async-start | bytes 1048576 | tf_op jit(solution)/shard_map/all_to_all | solution.py:239
  82.2 3.0 %collective-permute-start.3 = (bf16[4,64,512]{2,1,0:T(8,128)(2,1)S(1)}, bf16[4,64,512]{2,1,0:T(8,128)(2,1)S(1)}, u32[]{:S(2)}, u32[]{:S(2)}) collective-permute-start(bf16[4,64,512]{2,1,0:T(8,128)(2,1)S(1)} %constant_dynamic-slice_fusion.1), channel_id=1, source_target_pairs={{0,16},{16,0},{1,17},{17,1},{2,18},{18,2},{3,19},{19,3},{4,20},{20... | collective-permute-start | bytes 786440 | tf_op jit(solution)/shard_map/ppermute | solution.py:230
  85.2 1.1 %collective-permute-done.3.refs_1_ = bf16[4,64,512]{2,1,0:T(8,128)(2,1)S(1)} collective-permute-done((bf16[4,64,512]{2,1,0:T(8,128)(2,1)S(1)}, bf16[4,64,512]{2,1,0:T(8,128)(2,1)S(1)}, u32[]{:S(2)}, u32[]{:S(2)}) %collective-permute-start.3) | collective-permute-done | bytes 262176 | tf_op jit(solution)/shard_map/ppermute | solution.py:230
  86.3 0.8 shard_map.31.refs_1_
  87.1 13.0 %all-to-all-done.2.refs_0_ = bf16[8,64,512]{2,1,0:T(8,128)(2,1)S(1)} async-done(((bf16[8,64,512]{2,1,0:T(8,128)(2,1)}), bf16[8,64,512]{2,1,0:T(8,128)(2,1)S(1)}, u32[]{:S(2)}, u32[]{:S(2)}) %all-to-all-start.2) | async-done | bytes 524320 | tf_op jit(solution)/shard_map/all_to_all | solution.py:239
  100.1 2.4 %collective-permute-start.4 = (bf16[4,64,512]{2,1,0:T(8,128)(2,1)S(1)}, bf16[4,64,512]{2,1,0:T(8,128)(2,1)S(1)}, u32[]{:S(2)}, u32[]{:S(2)}) collective-permute-start(bf16[4,64,512]{2,1,0:T(8,128)(2,1)S(1)} %constant_dynamic-slice_fusion), channel_id=1, source_target_pairs={{0,16},{16,0},{1,17},{17,1},{2,18},{18,2},{3,19},{19,3},{4,20},{20... | collective-permute-start | bytes 786440 | tf_op jit(solution)/shard_map/ppermute | solution.py:242
  102.6 0.7 shard_map.33.refs_1_
  103.3 0.4 collective-permute-done.4.refs_0_
  103.7 0.7 shard_map.34
  (4 shorter events, 0.1 us)
Async XLA Ops:
  40.4 8.7 %collective-permute-start = (bf16[128,16,128]{2,1,0:T(8,128)(2,1)S(1)}, bf16[128,16,128]{2,1,0:T(8,128)(2,1)S(1)}, u32[]{:S(2)}, u32[]{:S(2)}) collective-permute-start(bf16[128,16,128]{2,1,0:T(8,128)(2,1)S(1)} %all_to_all.15), channel_id=1, source_target_pairs={{0,16},{16,0},{1,17},{17,1},{2,18},{18,2},{3,19},{19,3},{4,20},{20... | collective-permute-start | bytes 1572872 | tf_op jit(solution)/shard_map/ppermute | solution.py:200
  44.4 19.3 %collective-permute-start.1 = (bf16[64,16,128]{2,1,0:T(8,128)(2,1)S(1)}, bf16[64,16,128]{2,1,0:T(8,128)(2,1)S(1)}, u32[]{:S(2)}, u32[]{:S(2)}) collective-permute-start(bf16[64,16,128]{2,1,0:T(8,128)(2,1)S(1)} %constant_dynamic-slice_fusion.3), channel_id=1, source_target_pairs={{0,8},{8,0},{1,9},{9,1},{2,10},{10,2},{3,11},{11,3},{4,12},{12,4},... | collective-permute-start | bytes 786440 | tf_op jit(solution)/shard_map/ppermute | solution.py:199
  51.3 21.4 %all-to-all-start.1 = ((bf16[8,64,512]{2,1,0:T(8,128)(2,1)}), bf16[8,64,512]{2,1,0:T(8,128)(2,1)S(1)}, u32[]{:S(2)}, u32[]{:S(2)}) async-start(bf16[8,64,512]{2,1,0:T(8,128)(2,1)} %bitcast.6), calls=%async_computation.1 | async-start | bytes 1048576 | tf_op jit(solution)/shard_map/all_to_all | solution.py:216
  54.9 14.6 %collective-permute-start.2 = (bf16[64,16,128]{2,1,0:T(8,128)(2,1)S(1)}, bf16[64,16,128]{2,1,0:T(8,128)(2,1)S(1)}, u32[]{:S(2)}, u32[]{:S(2)}) collective-permute-start(bf16[64,16,128]{2,1,0:T(8,128)(2,1)S(1)} %constant_dynamic-slice_fusion.2), channel_id=1, source_target_pairs={{0,8},{8,0},{1,9},{9,1},{2,10},{10,2},{3,11},{11,3},{4,12},{12,4},... | collective-permute-start | bytes 786440 | tf_op jit(solution)/shard_map/ppermute | solution.py:215
  74.2 25.9 %all-to-all-start.2 = ((bf16[8,64,512]{2,1,0:T(8,128)(2,1)}), bf16[8,64,512]{2,1,0:T(8,128)(2,1)S(1)}, u32[]{:S(2)}, u32[]{:S(2)}) async-start(bf16[8,64,512]{2,1,0:T(8,128)(2,1)} %bitcast.9), calls=%async_computation.2 | async-start | bytes 1048576 | tf_op jit(solution)/shard_map/all_to_all | solution.py:239
  82.2 4.1 %collective-permute-start.3 = (bf16[4,64,512]{2,1,0:T(8,128)(2,1)S(1)}, bf16[4,64,512]{2,1,0:T(8,128)(2,1)S(1)}, u32[]{:S(2)}, u32[]{:S(2)}) collective-permute-start(bf16[4,64,512]{2,1,0:T(8,128)(2,1)S(1)} %constant_dynamic-slice_fusion.1), channel_id=1, source_target_pairs={{0,16},{16,0},{1,17},{17,1},{2,18},{18,2},{3,19},{19,3},{4,20},{20... | collective-permute-start | bytes 786440 | tf_op jit(solution)/shard_map/ppermute | solution.py:230
  100.1 3.6 %collective-permute-start.4 = (bf16[4,64,512]{2,1,0:T(8,128)(2,1)S(1)}, bf16[4,64,512]{2,1,0:T(8,128)(2,1)S(1)}, u32[]{:S(2)}, u32[]{:S(2)}) collective-permute-start(bf16[4,64,512]{2,1,0:T(8,128)(2,1)S(1)} %constant_dynamic-slice_fusion), channel_id=1, source_target_pairs={{0,16},{16,0},{1,17},{17,1},{2,18},{18,2},{3,19},{19,3},{4,20},{20... | collective-permute-start | bytes 786440 | tf_op jit(solution)/shard_map/ppermute | solution.py:242

commit v7 on v5

v7 whole, which is shorter than its diff:
```python
import functools

import jax
import jax.numpy as jnp
from jax import lax
from jax.experimental import pallas as pl
from jax.experimental.pallas import tpu as pltpu
from jax.sharding import Mesh, PartitionSpec as P

VMEM = pltpu.MemorySpace.VMEM
SMEM = pltpu.MemorySpace.SMEM
HBM = pltpu.MemorySpace.HBM
STEPS = 4
PARAMS = pltpu.CompilerParams(vmem_limit_bytes=32 * 1024 * 1024)


def vmem_call(body, out_shape, in_spaces, scratch=(), flops=0, nbytes=0, params=PARAMS):
    outs = out_shape if isinstance(out_shape, (list, tuple)) else (out_shape,)
    specs = [pl.BlockSpec(memory_space=VMEM) for _ in outs]
    return pl.pallas_call(
        body,
        out_shape=out_shape,
        in_specs=[pl.BlockSpec(memory_space=s) for s in in_spaces],
        out_specs=specs if isinstance(out_shape, (list, tuple)) else specs[0],
        scratch_shapes=list(scratch),
        compiler_params=params,
        cost_estimate=pl.CostEstimate(flops=flops, bytes_accessed=nbytes, transcendentals=0),
    )


def scale_kernel(weight_hbm, x_hbm, out_ref, weight_ref, x_ref, turned, sems):
    _, shots, chans, bins = x_ref.shape
    planes, cores, depth = turned.shape[:3]
    step = shots // STEPS
    weight_copy = pltpu.make_async_copy(weight_hbm, weight_ref, sems.at[STEPS])
    weight_copy.start()
    copies = []
    for i in range(STEPS):
        some = pl.ds(i * step, step)
        copies.append(pltpu.make_async_copy(x_hbm.at[:, some], x_ref.at[:, some], sems.at[i]))
        copies[-1].start()
    weight_copy.wait()
    for s in range(shots):
        if s % step == 0:
            copies[s // step].wait()
        block = x_ref[:, s].reshape(2 * chans, bins).astype(jnp.float32) * weight_ref[s]
        block = block.astype(jnp.bfloat16).astype(jnp.float32)
        turned[:, :, :, s, :] = block.T.reshape(planes, cores, depth, 2 * chans)
    for z in range(depth):
        out_ref[z] = turned[:, :, z].astype(jnp.bfloat16)


def split_parts(first, second):
    half = first.shape[1] // 2
    p = jnp.concatenate([first[:, :half], second[:, :half]], axis=1)
    q = jnp.concatenate([first[:, half:], second[:, half:]], axis=1)
    return p, q


def fill_right(right, pairs):
    width, k_rows = right.shape[1] // 2, right.shape[0] // 2
    for j, (first, second) in enumerate(pairs):
        p, q = split_parts(first, second)
        cols = slice(j * 128, (j + 1) * 128)
        icols = slice(width + j * 128, width + (j + 1) * 128)
        right[:k_rows, cols] = p
        right[:k_rows, icols] = q
        right[k_rows:, cols] = q
        right[k_rows:, icols] = -p


def multiply(left_ref, right, out_ref, factor):
    rows, step = left_ref.shape[0], 256
    for r in range(rows // step):
        some = slice(r * step, (r + 1) * step)
        acc = jnp.dot(left_ref[some, :], right[...], preferred_element_type=jnp.float32)
        out_ref[some, :] = (acc * factor).astype(jnp.bfloat16)


def own_kernel(factor, zl_ref, mine_ref, near_ref, out_ref, left_ref, right):
    blocks, k_rows, _ = mine_ref.shape
    for zl in range(2):

        @pl.when(zl_ref[0] == zl)
        def _(zl=zl):
            even, odd = (mine_ref, near_ref) if zl == 0 else (near_ref, mine_ref)
            for j in range(blocks):
                p, q = split_parts(even[j], odd[j])
                rows = slice(j * 128, (j + 1) * 128)
                left_ref[rows, :k_rows] = p.T
                left_ref[rows, k_rows:] = q.T
            half = blocks // 2
            fill_right(right, [(even[j], odd[j]) for j in range(zl * half, (zl + 1) * half)])

    multiply(left_ref, right, out_ref, factor)


def right_kernel(far_ref, right):
    fill_right(right, [(far_ref[j], far_ref[j + 1]) for j in range(0, far_ref.shape[0], 2)])


def cross_kernel(factor, left_ref, right, out_ref):
    multiply(left_ref, right, out_ref, factor)


def place_own_kernel(yh_ref, source, out_hbm, sems):
    width = out_hbm.shape[3] // 4
    copies = []
    for quarter in range(2):
        column = pl.multiple_of((2 * yh_ref[0] + quarter) * width, width)
        for part in range(2):
            copies.append(
                pltpu.make_async_copy(
                    source.at[:, quarter, :, pl.ds(part * width, width)],
                    out_hbm.at[part, :, :, pl.ds(column, width)],
                    sems.at[2 * quarter + part],
                )
            )
            copies[-1].start()
    for copy in copies:
        copy.wait()


def place_cross_kernel(yh_ref, source, _, out_hbm, turned, sems):
    bins, _, rows, wide = source.shape
    width = wide // 2
    column = pl.multiple_of((1 - yh_ref[0]) * 2 * width, 2 * width)
    copies = []
    for part in range(2):
        for b in range(bins):
            for j in range(width // 64):
                cols = slice(part * width + j * 64, part * width + (j + 1) * 64)
                turned[part, b, :, j * 128:(j + 1) * 128] = jnp.concatenate(
                    [source[b, 0, :, cols], source[b, 1, :, cols]], axis=1
                )
        copies.append(
            pltpu.make_async_copy(
                turned.at[part],
                out_hbm.at[part, :, :, pl.ds(column, 2 * width)],
                sems.at[part],
            )
        )
        copies[-1].start()
    for copy in copies:
        copy.wait()


def place(body, yh, source, shape, scratch, out=None):
    extra = [] if out is None else [out]
    return pl.pallas_call(
        body,
        out_shape=jax.ShapeDtypeStruct(shape, jnp.bfloat16),
        in_specs=[pl.BlockSpec(memory_space=SMEM), pl.BlockSpec(memory_space=VMEM)]
        + [pl.BlockSpec(memory_space=HBM)] * len(extra),
        out_specs=pl.BlockSpec(memory_space=HBM),
        scratch_shapes=scratch,
        input_output_aliases={2: 0} if extra else {},
        compiler_params=PARAMS,
        cost_estimate=pl.CostEstimate(flops=0, bytes_accessed=2 ** 20, transcendentals=0),
    )(yh, source, *extra)


SWAP = [(0, 1), (1, 0)]


def shards(spectra, shot_weight):
    _, shots, bins, chans = spectra.shape
    depth = lax.axis_size("zh")
    planes = lax.axis_size("y") * lax.axis_size("x")
    cores = lax.axis_size("c")
    k_rows = planes * cores * shots
    factor = k_rows ** (-0.5)
    yh = lax.axis_index("yh").astype(jnp.int32).reshape(1)
    zl = lax.axis_index("zl").astype(jnp.int32).reshape(1)
    lanes = 2 * chans
    rows = 2 * depth * chans
    width = rows
    blocks = (depth, k_rows, lanes)

    turned = jnp.swapaxes(spectra, 2, 3)
    scaled = vmem_call(
        scale_kernel,
        jax.ShapeDtypeStruct((depth, planes, cores, shots, lanes), jnp.bfloat16),
        [HBM, HBM],
        [
            pltpu.SMEM((shots,), jnp.float32),
            pltpu.VMEM((2, shots, chans, bins), jnp.bfloat16),
            pltpu.VMEM((planes, cores, depth, shots, lanes), jnp.float32),
            pltpu.SemaphoreType.DMA((STEPS + 1,)),
        ],
        nbytes=2 * spectra.size * 2,
        params=pltpu.CompilerParams(vmem_limit_bytes=56 * 1024 * 1024),
    )(shot_weight, turned)
    scaled = scaled.reshape(bins, shots, lanes)
    mine = lax.all_to_all(scaled, ("zh", "y", "x", "c"), 0, 0, tiled=True)
    near = lax.ppermute(mine, "zl", SWAP)
    far = lax.ppermute(mine, "yh", SWAP)

    flops = 2 * rows * 2 * k_rows * width
    own, left = vmem_call(
        functools.partial(own_kernel, factor),
        (
            jax.ShapeDtypeStruct((rows, width), jnp.bfloat16),
            jax.ShapeDtypeStruct((rows, 2 * k_rows), jnp.bfloat16),
        ),
        [SMEM, VMEM, VMEM],
        [pltpu.VMEM((2 * k_rows, width), jnp.bfloat16)],
        flops=flops,
        nbytes=4 * rows * width * 2,
    )(zl, mine.reshape(blocks), near.reshape(blocks))
    pieces = (2 * depth, chans, width)
    own = lax.all_to_all(own.reshape(pieces), ("zh", "zl"), 0, 0, tiled=True)

    right = vmem_call(
        right_kernel,
        jax.ShapeDtypeStruct((2 * k_rows, width), jnp.bfloat16),
        [VMEM],
        flops=40 * flops,
    )(far.reshape(blocks))
    own, right = lax.optimization_barrier((own, right))
    cross = vmem_call(
        functools.partial(cross_kernel, factor),
        jax.ShapeDtypeStruct((rows, width), jnp.bfloat16),
        [VMEM, VMEM],
        flops=flops,
        nbytes=4 * rows * width * 2,
    )(left, right)
    cross = lax.all_to_all(cross.reshape(pieces), ("zh", "zl"), 0, 0, tiled=True)

    shape = (2, depth, chans, 2 * rows)
    by_bin = (depth, 2, chans, width)
    out = place(place_own_kernel, yh, own.reshape(by_bin), shape, [pltpu.SemaphoreType.DMA((4,))])
    out, cross = lax.optimization_barrier((out, cross))
    scratch = [
        pltpu.VMEM((2, depth, chans, width), jnp.bfloat16),
        pltpu.SemaphoreType.DMA((2,)),
    ]
    return place(place_cross_kernel, yh, cross.reshape(by_bin), shape, scratch, out)


def solution(mesh):
    fine = Mesh(mesh.devices.reshape(4, 4, 2, 2, 4, 2), ("y", "x", "c", "yh", "zh", "zl"))
    shot, pair = ("y", "x", "c"), ("yh", "zh", "zl")
    return jax.shard_map(
        shards,
        mesh=fine,
        in_specs=(P(None, shot, None, pair), P(shot)),
        out_specs=P(None, shot, pair, None),
        check_vma=False,
    )
```

time: 112 us -> 103 us (0.920)
  the two profiles are of different devices: /device:TPU:9 before, /device:TPU:7 now
where the time goes in v7:
time: 103 us
  waiting for transfers between devices  42 us (41%)
  blocking collectives  37.3 us (36%)
  starting transfers between devices  14.8 us (14%)
  Pallas kernels  8.55 us (8%)
    all_to_all x1, blocking collectives, shards(): mine = lax.all_to_all(scaled, ('zh', 'y', 'x', 'c'), 0, 0, tiled=True)  37.3 us
    all_to_all x1, waiting for transfers between devices, shards(): lax.all_to_all(cross.reshape(pieces), ('zh', 'zl'), 0, 0, tiled=True)  17 us
    ppermute x1, waiting for transfers between devices, shards(): far = lax.ppermute(mine, 'yh', SWAP)  12.7 us
    ppermute x1, waiting for transfers between devices, shards(): near = lax.ppermute(mine, 'zl', SWAP)  7.35 us
    all_to_all x1, waiting for transfers between devices, shards(): own = lax.all_to_all(own.reshape(pieces), ('zh', 'zl'), 0, 0, tiled=True)  4.94 us
    ppermute x1, starting transfers between devices, shards(): far = lax.ppermute(mine, 'yh', SWAP)  4.76 us
    all_to_all x1, starting transfers between devices, shards(): own = lax.all_to_all(own.reshape(pieces), ('zh', 'zl'), 0, 0, tiled=True)  3.49 us
    all_to_all x1, starting transfers between devices, shards(): lax.all_to_all(cross.reshape(pieces), ('zh', 'zl'), 0, 0, tiled=True)  3.49 us
  transfers between devices with their start and end apart: 4, of which 4 were waited for; matrix products, arithmetic and copies ran while one was open for 0% of the time, Pallas kernels for 3%

profile of v7, /device:TPU:7, one launch (start us, length us, event | category | flops | bytes accessed | tf_op | source)
XLA Modules:
  0.0 102.7 jit_solution(14290375725351781813)
XLA Ops:
  0.0 2.7 %shard_map.28 = bf16[4,16,2,16,128]{4,3,2,1,0:T(8,128)(2,1)} custom-call(f32[16]{0:T(128)} %weight_hbm.1, bf16[2,16,64,128]{3,2,1,0:T(8,128)(2,1)} %bitcast.17), custom_call_target="tpu_custom_call" | custom-call | bytes 1048576 | tf_op jit(solution)/shard_map/pallas_call | solution.py:181
  2.7 37.3 %all_to_all.15 = bf16[128,16,128]{2,1,0:T(8,128)(2,1)S(1)} all-to-all(bf16[128,16,128]{2,1,0:T(8,128)(2,1)} %bitcast.16), channel_id=1, replica_groups=mesh['y'=4,'x'=4,'c'=2,'yh'=2,'zh'=4,'zl'=2] {'zh','y','x','c'}, dimensions={0} | all-to-all | bytes 1048576 | tf_op jit(solution)/shard_map/all_to_all | solution.py:195
  40.0 3.1 %collective-permute-start = (bf16[128,16,128]{2,1,0:T(8,128)(2,1)S(1)}, bf16[128,16,128]{2,1,0:T(8,128)(2,1)S(1)}, u32[]{:S(2)}, u32[]{:S(2)}) collective-permute-start(bf16[128,16,128]{2,1,0:T(8,128)(2,1)S(1)} %all_to_all.15), channel_id=1, source_target_pairs={{0,1},{1,0},{2,3},{3,2},{4,5},{5,4},{6,7},{7,6},{8,9},{9,8},{10,11... | collective-permute-start | bytes 1572872 | tf_op jit(solution)/shard_map/ppermute | solution.py:196
  43.1 4.8 %collective-permute-start.1 = (bf16[128,16,128]{2,1,0:T(8,128)(2,1)S(1)}, bf16[128,16,128]{2,1,0:T(8,128)(2,1)S(1)}, u32[]{:S(2)}, u32[]{:S(2)}) collective-permute-start(bf16[128,16,128]{2,1,0:T(8,128)(2,1)S(1)} %all_to_all.15), channel_id=1, source_target_pairs={{0,8},{8,0},{1,9},{9,1},{2,10},{10,2},{3,11},{11,3},{4,12},{12,4},... | collective-permute-start | bytes 1572872 | tf_op jit(solution)/shard_map/ppermute | solution.py:197
  47.8 7.4 %collective-permute-done = bf16[128,16,128]{2,1,0:T(8,128)(2,1)S(1)} collective-permute-done((bf16[128,16,128]{2,1,0:T(8,128)(2,1)S(1)}, bf16[128,16,128]{2,1,0:T(8,128)(2,1)S(1)}, u32[]{:S(2)}, u32[]{:S(2)}) %collective-permute-start) | collective-permute-done | bytes 524320 | tf_op jit(solution)/shard_map/ppermute | solution.py:196
  55.2 2.4 %shard_map.29 = (bf16[512,512]{1,0:T(8,128)(2,1)}, bf16[512,1024]{1,0:T(8,128)(2,1)S(1)}) custom-call(s32[1]{0:T(128)} %bitcast.1.zl_ref, bf16[4,512,128]{2,1,0:T(8,128)(2,1)S(1)} %bitcast.13, bf16[4,512,128]{2,1,0:T(8,128)(2,1)S(1)} %bitcast.15), custom_call_target="tpu_custom_call" | custom-call | flops 536870912 | bytes 2097152 | tf_op jit(solution)/shard_map/pallas_call | solution.py:200
  57.6 3.5 %all-to-all-start.1 = ((bf16[8,64,512]{2,1,0:T(8,128)(2,1)}), bf16[8,64,512]{2,1,0:T(8,128)(2,1)S(1)}, u32[]{:S(2)}, u32[]{:S(2)}) async-start(bf16[8,64,512]{2,1,0:T(8,128)(2,1)} %bitcast.6), calls=%async_computation.1 | async-start | bytes 1048576 | tf_op jit(solution)/shard_map/all_to_all | solution.py:212
  61.1 12.7 %collective-permute-done.1 = bf16[128,16,128]{2,1,0:T(8,128)(2,1)S(1)} collective-permute-done((bf16[128,16,128]{2,1,0:T(8,128)(2,1)S(1)}, bf16[128,16,128]{2,1,0:T(8,128)(2,1)S(1)}, u32[]{:S(2)}, u32[]{:S(2)}) %collective-permute-start.1) | collective-permute-done | bytes 524320 | tf_op jit(solution)/shard_map/ppermute | solution.py:197
  73.8 0.2 shard_map.30.right
  74.0 4.9 %all-to-all-done.1 = bf16[8,64,512]{2,1,0:T(8,128)(2,1)S(1)} async-done(((bf16[8,64,512]{2,1,0:T(8,128)(2,1)}), bf16[8,64,512]{2,1,0:T(8,128)(2,1)S(1)}, u32[]{:S(2)}, u32[]{:S(2)}) %all-to-all-start.1) | async-done | bytes 524320 | tf_op jit(solution)/shard_map/all_to_all | solution.py:212
  78.9 1.5 %shard_map.32 = bf16[512,512]{1,0:T(8,128)(2,1)} custom-call(bf16[512,1024]{1,0:T(8,128)(2,1)S(1)} %get-tuple-element.13.left_ref, bf16[1024,512]{1,0:T(8,128)(2,1)S(1)} %shard_map.30.right), custom_call_target="tpu_custom_call" | custom-call | flops 536870912 | bytes 2097152 | tf_op jit(solution)/shard_map/pallas_call | solution.py:221
  80.4 3.5 %all-to-all-start.2 = ((bf16[8,64,512]{2,1,0:T(8,128)(2,1)}), bf16[8,64,512]{2,1,0:T(8,128)(2,1)S(1)}, u32[]{:S(2)}, u32[]{:S(2)}) async-start(bf16[8,64,512]{2,1,0:T(8,128)(2,1)} %bitcast.9), calls=%async_computation.2 | async-start | bytes 1048576 | tf_op jit(solution)/shard_map/all_to_all | solution.py:228
  83.9 0.8 shard_map.31._
  84.8 17.0 %all-to-all-done.2 = bf16[8,64,512]{2,1,0:T(8,128)(2,1)S(1)} async-done(((bf16[8,64,512]{2,1,0:T(8,128)(2,1)}), bf16[8,64,512]{2,1,0:T(8,128)(2,1)S(1)}, u32[]{:S(2)}, u32[]{:S(2)}) %all-to-all-start.2) | async-done | bytes 524320 | tf_op jit(solution)/shard_map/all_to_all | solution.py:228
  101.8 0.9 shard_map.33
Async XLA Ops:
  40.0 15.2 %collective-permute-start = (bf16[128,16,128]{2,1,0:T(8,128)(2,1)S(1)}, bf16[128,16,128]{2,1,0:T(8,128)(2,1)S(1)}, u32[]{:S(2)}, u32[]{:S(2)}) collective-permute-start(bf16[128,16,128]{2,1,0:T(8,128)(2,1)S(1)} %all_to_all.15), channel_id=1, source_target_pairs={{0,1},{1,0},{2,3},{3,2},{4,5},{5,4},{6,7},{7,6},{8,9},{9,8},{10,11... | collective-permute-start | bytes 1572872 | tf_op jit(solution)/shard_map/ppermute | solution.py:196
  43.1 30.7 %collective-permute-start.1 = (bf16[128,16,128]{2,1,0:T(8,128)(2,1)S(1)}, bf16[128,16,128]{2,1,0:T(8,128)(2,1)S(1)}, u32[]{:S(2)}, u32[]{:S(2)}) collective-permute-start(bf16[128,16,128]{2,1,0:T(8,128)(2,1)S(1)} %all_to_all.15), channel_id=1, source_target_pairs={{0,8},{8,0},{1,9},{9,1},{2,10},{10,2},{3,11},{11,3},{4,12},{12,4},... | collective-permute-start | bytes 1572872 | tf_op jit(solution)/shard_map/ppermute | solution.py:197
  57.6 21.4 %all-to-all-start.1 = ((bf16[8,64,512]{2,1,0:T(8,128)(2,1)}), bf16[8,64,512]{2,1,0:T(8,128)(2,1)S(1)}, u32[]{:S(2)}, u32[]{:S(2)}) async-start(bf16[8,64,512]{2,1,0:T(8,128)(2,1)} %bitcast.6), calls=%async_computation.1 | async-start | bytes 1048576 | tf_op jit(solution)/shard_map/all_to_all | solution.py:212
  80.4 21.4 %all-to-all-start.2 = ((bf16[8,64,512]{2,1,0:T(8,128)(2,1)}), bf16[8,64,512]{2,1,0:T(8,128)(2,1)S(1)}, u32[]{:S(2)}, u32[]{:S(2)}) async-start(bf16[8,64,512]{2,1,0:T(8,128)(2,1)} %bitcast.9), calls=%async_computation.2 | async-start | bytes 1048576 | tf_op jit(solution)/shard_map/all_to_all | solution.py:228

commit v8 on v7

--- a/solution.py
+++ b/solution.py
@@ -69,62 +69,54 @@
         right[k_rows:, icols] = -p
 
 
-def multiply(left_ref, right, out_ref, factor):
-    rows, step = left_ref.shape[0], 256
-    for r in range(rows // step):
-        some = slice(r * step, (r + 1) * step)
-        acc = jnp.dot(left_ref[some, :], right[...], preferred_element_type=jnp.float32)
-        out_ref[some, :] = (acc * factor).astype(jnp.bfloat16)
-
-
-def own_kernel(factor, zl_ref, mine_ref, near_ref, out_ref, left_ref, right):
-    blocks, k_rows, _ = mine_ref.shape
-    for zl in range(2):
-
-        @pl.when(zl_ref[0] == zl)
-        def _(zl=zl):
-            even, odd = (mine_ref, near_ref) if zl == 0 else (near_ref, mine_ref)
-            for j in range(blocks):
-                p, q = split_parts(even[j], odd[j])
-                rows = slice(j * 128, (j + 1) * 128)
-                left_ref[rows, :k_rows] = p.T
-                left_ref[rows, k_rows:] = q.T
-            half = blocks // 2
-            fill_right(right, [(even[j], odd[j]) for j in range(zl * half, (zl + 1) * half)])
-
-    multiply(left_ref, right, out_ref, factor)
-
-
-def right_kernel(far_ref, right):
-    fill_right(right, [(far_ref[j], far_ref[j + 1]) for j in range(0, far_ref.shape[0], 2)])
-
-
-def cross_kernel(factor, left_ref, right, out_ref):
-    multiply(left_ref, right, out_ref, factor)
-
-
-def place_own_kernel(yh_ref, source, out_hbm, sems):
-    width = out_hbm.shape[3] // 4
-    copies = []
-    for quarter in range(2):
-        column = pl.multiple_of((2 * yh_ref[0] + quarter) * width, width)
-        for part in range(2):
-            copies.append(
-                pltpu.make_async_copy(
-                    source.at[:, quarter, :, pl.ds(part * width, width)],
-                    out_hbm.at[part, :, :, pl.ds(column, width)],
-                    sems.at[2 * quarter + part],
-                )
-            )
-            copies[-1].start()
-    for copy in copies:
-        copy.wait()
-
-
-def place_cross_kernel(yh_ref, source, _, out_hbm, turned, sems):
+def block_pairs(ref):
+    return [(ref[j], ref[j + 1]) for j in range(0, ref.shape[0], 2)]
+
+
+def fill_left(left_ref, ref):
+    k_rows = ref.shape[1]
+    for j, (first, second) in enumerate(block_pairs(ref)):
+        p, q = split_parts(first, second)
+        rows = slice(j * 128, (j + 1) * 128)
+        left_ref[rows, :k_rows] = p.T
+        left_ref[rows, k_rows:] = q.T
+
+
+def rows_of(left_ref, right_ref, factor):
+    acc = jnp.dot(left_ref[...], right_ref[...], preferred_element_type=jnp.float32)
+    return (acc * factor).astype(jnp.bfloat16)
+
+
+def begin_kernel(factor, mine_ref, out_ref, left_ref, right_ref):
+    fill_left(left_ref, mine_ref)
+    fill_right(right_ref, block_pairs(mine_ref))
+    out_ref[...] = rows_of(left_ref, right_ref, factor).reshape(out_ref.shape)
+
+
+def own_kernel(factor, zl_ref, near_ref, right_ref, begun_ref, out_ref, left_ref):
+    zl = zl_ref[0]
+    fill_left(left_ref, near_ref)
+    theirs = rows_of(left_ref, right_ref, factor).reshape(begun_ref.shape)
+    for j in range(begun_ref.shape[0]):
+        out_ref[2 * j + zl] = begun_ref[j]
+        out_ref[2 * j + 1 - zl] = theirs[j]
+
+
+def cross_kernel(factor, zl_ref, left_ref, left_near_ref, far_ref, out_ref, right):
+    zl = zl_ref[0]
+    fill_right(right, block_pairs(far_ref))
+    half = (out_ref.shape[0] // 2,) + out_ref.shape[1:]
+    for ref, parity in ((left_ref, zl), (left_near_ref, 1 - zl)):
+        block = rows_of(ref, right, factor).reshape(half)
+        for j in range(half[0]):
+            out_ref[2 * j + parity] = block[j]
+
+
+def place_kernel(half, yh_ref, source, *refs):
+    out_hbm, turned, sems = refs[-3:]
     bins, _, rows, wide = source.shape
     width = wide // 2
-    column = pl.multiple_of((1 - yh_ref[0]) * 2 * width, 2 * width)
+    column = pl.multiple_of((yh_ref[0] + half) % 2 * 2 * width, 2 * width)
     copies = []
     for part in range(2):
         for b in range(bins):
@@ -145,10 +137,10 @@
         copy.wait()
 
 
-def place(body, yh, source, shape, scratch, out=None):
+def place(half, yh, source, shape, scratch, out=None):
     extra = [] if out is None else [out]
     return pl.pallas_call(
-        body,
+        functools.partial(place_kernel, half),
         out_shape=jax.ShapeDtypeStruct(shape, jnp.bfloat16),
         in_specs=[pl.BlockSpec(memory_space=SMEM), pl.BlockSpec(memory_space=VMEM)]
         + [pl.BlockSpec(memory_space=HBM)] * len(extra),
@@ -197,45 +189,43 @@
     far = lax.ppermute(mine, "yh", SWAP)
 
     flops = 2 * rows * 2 * k_rows * width
-    own, left = vmem_call(
+    left_shape = jax.ShapeDtypeStruct((rows // 2, 2 * k_rows), jnp.bfloat16)
+    right_shape = jax.ShapeDtypeStruct((2 * k_rows, width), jnp.bfloat16)
+    begun, left, right = vmem_call(
+        functools.partial(begin_kernel, factor),
+        (jax.ShapeDtypeStruct((depth, chans, width), jnp.bfloat16), left_shape, right_shape),
+        [VMEM],
+        flops=flops // 2,
+    )(mine.reshape(blocks))
+    pieces = (2 * depth, chans, width)
+    own, left_near = vmem_call(
         functools.partial(own_kernel, factor),
-        (
-            jax.ShapeDtypeStruct((rows, width), jnp.bfloat16),
-            jax.ShapeDtypeStruct((rows, 2 * k_rows), jnp.bfloat16),
-        ),
-        [SMEM, VMEM, VMEM],
-        [pltpu.VMEM((2 * k_rows, width), jnp.bfloat16)],
-        flops=flops,
-        nbytes=4 * rows * width * 2,
-    )(zl, mine.reshape(blocks), near.reshape(blocks))
-    pieces = (2 * depth, chans, width)
-    own = lax.all_to_all(own.reshape(pieces), ("zh", "zl"), 0, 0, tiled=True)
-
-    right = vmem_call(
-        right_kernel,
-        jax.ShapeDtypeStruct((2 * k_rows, width), jnp.bfloat16),
-        [VMEM],
-        flops=40 * flops,
-    )(far.reshape(blocks))
-    own, right = lax.optimization_barrier((own, right))
+        (jax.ShapeDtypeStruct(pieces, jnp.bfloat16), left_shape),
+        [SMEM, VMEM, VMEM, VMEM],
+        flops=flops // 2,
+    )(zl, near.reshape(blocks), right, begun)
+    own = lax.all_to_all(own, ("zh", "zl"), 0, 0, tiled=True)
+
     cross = vmem_call(
         functools.partial(cross_kernel, factor),
-        jax.ShapeDtypeStruct((rows, width), jnp.bfloat16),
-        [VMEM, VMEM],
-        flops=flops,
+        jax.ShapeDtypeStruct(pieces, jnp.bfloat16),
+        [SMEM, VMEM, VMEM, VMEM],
+        [pltpu.VMEM((2 * k_rows, width), jnp.bfloat16)],
+        flops=40 * flops,
         nbytes=4 * rows * width * 2,
-    )(left, right)
-    cross = lax.all_to_all(cross.reshape(pieces), ("zh", "zl"), 0, 0, tiled=True)
+    )(zl, left, left_near, far.reshape(blocks))
+    own, cross = lax.optimization_barrier((own, cross))
+    cross = lax.all_to_all(cross, ("zh", "zl"), 0, 0, tiled=True)
 
     shape = (2, depth, chans, 2 * rows)
     by_bin = (depth, 2, chans, width)
-    out = place(place_own_kernel, yh, own.reshape(by_bin), shape, [pltpu.SemaphoreType.DMA((4,))])
-    out, cross = lax.optimization_barrier((out, cross))
     scratch = [
         pltpu.VMEM((2, depth, chans, width), jnp.bfloat16),
         pltpu.SemaphoreType.DMA((2,)),
     ]
-    return place(place_cross_kernel, yh, cross.reshape(by_bin), shape, scratch, out)
+    out = place(0, yh, own.reshape(by_bin), shape, scratch)
+    out, cross = lax.optimization_barrier((out, cross))
+    return place(1, yh, cross.reshape(by_bin), shape, scratch, out)
 
 
 def solution(mesh):

time: 103 us -> 101 us (0.981)
  waiting for transfers between devices: 42 us -> 39.6 us
    all_to_all x2, waiting for transfers between devices: 22 us -> 19.6 us  [the longest x1 16.9 us: shards(): cross = lax.all_to_all(cross, ('zh', 'zl'), 0, 0, tiled=True)]
  transfers between devices with their start and end apart: 4 -> 4, of which waited for: 4 -> 4; matrix products, arithmetic and copies ran while one was open for 0% -> 0% of each run, Pallas kernels for 3% -> 5%
where the time goes in v8:
time: 101 us; the launch traced here: 100 us
  waiting for transfers between devices  39.6 us (39%)
  blocking collectives  37.3 us (37%)
  starting transfers between devices  14.8 us (15%)
  Pallas kernels  8.65 us (9%)
    all_to_all x1, blocking collectives, shards(): mine = lax.all_to_all(scaled, ('zh', 'y', 'x', 'c'), 0, 0, tiled=True)  37.3 us
    all_to_all x1, waiting for transfers between devices, shards(): cross = lax.all_to_all(cross, ('zh', 'zl'), 0, 0, tiled=True)  16.9 us
    ppermute x1, waiting for transfers between devices, shards(): far = lax.ppermute(mine, 'yh', SWAP)  13.6 us
    ppermute x1, waiting for transfers between devices, shards(): near = lax.ppermute(mine, 'zl', SWAP)  6.45 us
    ppermute x1, starting transfers between devices, shards(): far = lax.ppermute(mine, 'yh', SWAP)  4.76 us
    all_to_all x1, starting transfers between devices, shards(): own = lax.all_to_all(own, ('zh', 'zl'), 0, 0, tiled=True)  3.49 us
    all_to_all x1, starting transfers between devices, shards(): cross = lax.all_to_all(cross, ('zh', 'zl'), 0, 0, tiled=True)  3.49 us
    ppermute x1, starting transfers between devices, shards(): near = lax.ppermute(mine, 'zl', SWAP)  3.09 us
  transfers between devices with their start and end apart: 4, of which 4 were waited for; matrix products, arithmetic and copies ran while one was open for 0% of the time, Pallas kernels for 5%

profile of v8, /device:TPU:7, one launch (start us, length us, event | category | flops | bytes accessed | tf_op | source)
XLA Modules:
  0.0 100.4 jit_solution(4928741068068547213)
XLA Ops:
  0.0 2.7 %shard_map.28 = bf16[4,16,2,16,128]{4,3,2,1,0:T(8,128)(2,1)} custom-call(f32[16]{0:T(128)} %weight_hbm.1, bf16[2,16,64,128]{3,2,1,0:T(8,128)(2,1)} %bitcast.15), custom_call_target="tpu_custom_call" | custom-call | bytes 1048576 | tf_op jit(solution)/shard_map/pallas_call | solution.py:173
  2.7 37.3 %all_to_all.15 = bf16[128,16,128]{2,1,0:T(8,128)(2,1)S(1)} all-to-all(bf16[128,16,128]{2,1,0:T(8,128)(2,1)} %bitcast.14), channel_id=1, replica_groups=mesh['y'=4,'x'=4,'c'=2,'yh'=2,'zh'=4,'zl'=2] {'zh','y','x','c'}, dimensions={0} | all-to-all | bytes 1048576 | tf_op jit(solution)/shard_map/all_to_all | solution.py:187
  40.0 3.1 %collective-permute-start = (bf16[128,16,128]{2,1,0:T(8,128)(2,1)S(1)}, bf16[128,16,128]{2,1,0:T(8,128)(2,1)S(1)}, u32[]{:S(2)}, u32[]{:S(2)}) collective-permute-start(bf16[128,16,128]{2,1,0:T(8,128)(2,1)S(1)} %all_to_all.15), channel_id=1, source_target_pairs={{0,1},{1,0},{2,3},{3,2},{4,5},{5,4},{6,7},{7,6},{8,9},{9,8},{10,11... | collective-permute-start | bytes 1572872 | tf_op jit(solution)/shard_map/ppermute | solution.py:188
  43.1 4.8 %collective-permute-start.1 = (bf16[128,16,128]{2,1,0:T(8,128)(2,1)S(1)}, bf16[128,16,128]{2,1,0:T(8,128)(2,1)S(1)}, u32[]{:S(2)}, u32[]{:S(2)}) collective-permute-start(bf16[128,16,128]{2,1,0:T(8,128)(2,1)S(1)} %all_to_all.15), channel_id=1, source_target_pairs={{0,8},{8,0},{1,9},{9,1},{2,10},{10,2},{3,11},{11,3},{4,12},{12,4},... | collective-permute-start | bytes 1572872 | tf_op jit(solution)/shard_map/ppermute | solution.py:189
  47.8 0.9 shard_map.29
  48.7 6.5 %collective-permute-done = bf16[128,16,128]{2,1,0:T(8,128)(2,1)S(1)} collective-permute-done((bf16[128,16,128]{2,1,0:T(8,128)(2,1)S(1)}, bf16[128,16,128]{2,1,0:T(8,128)(2,1)S(1)}, u32[]{:S(2)}, u32[]{:S(2)}) %collective-permute-start) | collective-permute-done | bytes 524320 | tf_op jit(solution)/shard_map/ppermute | solution.py:188
  55.2 1.5 %shard_map.30 = (bf16[8,64,512]{2,1,0:T(8,128)(2,1)}, bf16[256,1024]{1,0:T(8,128)(2,1)S(1)}) custom-call(s32[1]{0:T(128)} %bitcast.1.zl_ref, bf16[4,512,128]{2,1,0:T(8,128)(2,1)S(1)} %bitcast.12, bf16[1024,512]{1,0:T(8,128)(2,1)S(1)} %get-tuple-element.14.right_ref, bf16[4,64,512]{2,1,0:T(8,128)(2,1)S(1)} %get-tuple-element.15.begun_ref), custom_call_target="tpu_custom_call" | custom-call | flops 268435456 | tf_op jit(solution)/shard_map/pallas_call | solution.py:201
  56.7 3.5 %all-to-all-start.1 = ((bf16[8,64,512]{2,1,0:T(8,128)(2,1)}), bf16[8,64,512]{2,1,0:T(8,128)(2,1)S(1)}, u32[]{:S(2)}, u32[]{:S(2)}) async-start(bf16[8,64,512]{2,1,0:T(8,128)(2,1)} %get-tuple-element.16), calls=%async_computation.1 | async-start | bytes 1048576 | tf_op jit(solution)/shard_map/all_to_all | solution.py:207
  60.2 13.6 %collective-permute-done.1 = bf16[128,16,128]{2,1,0:T(8,128)(2,1)S(1)} collective-permute-done((bf16[128,16,128]{2,1,0:T(8,128)(2,1)S(1)}, bf16[128,16,128]{2,1,0:T(8,128)(2,1)S(1)}, u32[]{:S(2)}, u32[]{:S(2)}) %collective-permute-start.1) | collective-permute-done | bytes 524320 | tf_op jit(solution)/shard_map/ppermute | solution.py:189
  73.8 1.7 %shard_map.31 = bf16[8,64,512]{2,1,0:T(8,128)(2,1)} custom-call(s32[1]{0:T(128)} %bitcast.1.zl_ref, bf16[256,1024]{1,0:T(8,128)(2,1)S(1)} %get-tuple-element.17.left_ref, bf16[256,1024]{1,0:T(8,128)(2,1)S(1)} %get-tuple-element.18.left_near_ref, bf16[4,512,128]{2,1,0:T(8,128)(2,1)S(1)} %bitcast.13), custom_call_target="tpu_custom_call" | custom-call | flops 21474836480 | bytes 2097152 | tf_op jit(solution)/shard_map/pallas_call | solution.py:209
  75.4 2.6 %all-to-all-done.1 = bf16[8,64,512]{2,1,0:T(8,128)(2,1)S(1)} async-done(((bf16[8,64,512]{2,1,0:T(8,128)(2,1)}), bf16[8,64,512]{2,1,0:T(8,128)(2,1)S(1)}, u32[]{:S(2)}, u32[]{:S(2)}) %all-to-all-start.1) | async-done | bytes 524320 | tf_op jit(solution)/shard_map/all_to_all | solution.py:207
  78.1 3.5 %all-to-all-start.2 = ((bf16[8,64,512]{2,1,0:T(8,128)(2,1)}), bf16[8,64,512]{2,1,0:T(8,128)(2,1)S(1)}, u32[]{:S(2)}, u32[]{:S(2)}) async-start(bf16[8,64,512]{2,1,0:T(8,128)(2,1)} %shard_map.31), calls=%async_computation.2 | async-start | bytes 1048576 | tf_op jit(solution)/shard_map/all_to_all | solution.py:218
  81.6 0.9 shard_map.32.refs_0_
  82.5 16.9 %all-to-all-done.2 = bf16[8,64,512]{2,1,0:T(8,128)(2,1)S(1)} async-done(((bf16[8,64,512]{2,1,0:T(8,128)(2,1)}), bf16[8,64,512]{2,1,0:T(8,128)(2,1)S(1)}, u32[]{:S(2)}, u32[]{:S(2)}) %all-to-all-start.2) | async-done | bytes 524320 | tf_op jit(solution)/shard_map/all_to_all | solution.py:218
  99.5 0.9 shard_map.33
Async XLA Ops:
  40.0 15.2 %collective-permute-start = (bf16[128,16,128]{2,1,0:T(8,128)(2,1)S(1)}, bf16[128,16,128]{2,1,0:T(8,128)(2,1)S(1)}, u32[]{:S(2)}, u32[]{:S(2)}) collective-permute-start(bf16[128,16,128]{2,1,0:T(8,128)(2,1)S(1)} %all_to_all.15), channel_id=1, source_target_pairs={{0,1},{1,0},{2,3},{3,2},{4,5},{5,4},{6,7},{7,6},{8,9},{9,8},{10,11... | collective-permute-start | bytes 1572872 | tf_op jit(solution)/shard_map/ppermute | solution.py:188
  43.1 30.7 %collective-permute-start.1 = (bf16[128,16,128]{2,1,0:T(8,128)(2,1)S(1)}, bf16[128,16,128]{2,1,0:T(8,128)(2,1)S(1)}, u32[]{:S(2)}, u32[]{:S(2)}) collective-permute-start(bf16[128,16,128]{2,1,0:T(8,128)(2,1)S(1)} %all_to_all.15), channel_id=1, source_target_pairs={{0,8},{8,0},{1,9},{9,1},{2,10},{10,2},{3,11},{11,3},{4,12},{12,4},... | collective-permute-start | bytes 1572872 | tf_op jit(solution)/shard_map/ppermute | solution.py:189
  56.7 21.4 %all-to-all-start.1 = ((bf16[8,64,512]{2,1,0:T(8,128)(2,1)}), bf16[8,64,512]{2,1,0:T(8,128)(2,1)S(1)}, u32[]{:S(2)}, u32[]{:S(2)}) async-start(bf16[8,64,512]{2,1,0:T(8,128)(2,1)} %get-tuple-element.16), calls=%async_computation.1 | async-start | bytes 1048576 | tf_op jit(solution)/shard_map/all_to_all | solution.py:207
  78.1 21.4 %all-to-all-start.2 = ((bf16[8,64,512]{2,1,0:T(8,128)(2,1)}), bf16[8,64,512]{2,1,0:T(8,128)(2,1)S(1)}, u32[]{:S(2)}, u32[]{:S(2)}) async-start(bf16[8,64,512]{2,1,0:T(8,128)(2,1)} %shard_map.31), calls=%async_computation.2 | async-start | bytes 1048576 | tf_op jit(solution)/shard_map/all_to_all | solution.py:218

commit v9 on v8

--- a/solution.py
+++ b/solution.py
@@ -44,10 +44,11 @@
         if s % step == 0:
             copies[s // step].wait()
         block = x_ref[:, s].reshape(2 * chans, bins).astype(jnp.float32) * weight_ref[s]
-        block = block.astype(jnp.bfloat16).astype(jnp.float32)
-        turned[:, :, :, s, :] = block.T.reshape(planes, cores, depth, 2 * chans)
+        block = block.astype(jnp.bfloat16).T.astype(jnp.float32)
+        turned[:, :, :, s, :] = block.reshape(planes, cores, depth, 2 * chans)
     for z in range(depth):
-        out_ref[z] = turned[:, :, z].astype(jnp.bfloat16)
+        for core in range(cores):
+            out_ref[z, core] = turned[:, core, z].astype(jnp.bfloat16)
 
 
 def split_parts(first, second):
@@ -125,14 +126,14 @@
                 turned[part, b, :, j * 128:(j + 1) * 128] = jnp.concatenate(
                     [source[b, 0, :, cols], source[b, 1, :, cols]], axis=1
                 )
-        copies.append(
-            pltpu.make_async_copy(
-                turned.at[part],
-                out_hbm.at[part, :, :, pl.ds(column, 2 * width)],
-                sems.at[part],
+            copies.append(
+                pltpu.make_async_copy(
+                    turned.at[part, b],
+                    out_hbm.at[part, b, :, pl.ds(column, 2 * width)],
+                    sems.at[part * bins + b],
+                )
             )
-        )
-        copies[-1].start()
+            copies[-1].start()
     for copy in copies:
         copy.wait()
 
@@ -172,7 +173,7 @@
     turned = jnp.swapaxes(spectra, 2, 3)
     scaled = vmem_call(
         scale_kernel,
-        jax.ShapeDtypeStruct((depth, planes, cores, shots, lanes), jnp.bfloat16),
+        jax.ShapeDtypeStruct((depth, cores, planes, shots, lanes), jnp.bfloat16),
         [HBM, HBM],
         [
             pltpu.SMEM((shots,), jnp.float32),
@@ -184,7 +185,7 @@
         params=pltpu.CompilerParams(vmem_limit_bytes=56 * 1024 * 1024),
     )(shot_weight, turned)
     scaled = scaled.reshape(bins, shots, lanes)
-    mine = lax.all_to_all(scaled, ("zh", "y", "x", "c"), 0, 0, tiled=True)
+    mine = lax.all_to_all(scaled, ("zh", "c", "y", "x"), 0, 0, tiled=True)
     near = lax.ppermute(mine, "zl", SWAP)
     far = lax.ppermute(mine, "yh", SWAP)
 
@@ -221,7 +222,7 @@
     by_bin = (depth, 2, chans, width)
     scratch = [
         pltpu.VMEM((2, depth, chans, width), jnp.bfloat16),
-        pltpu.SemaphoreType.DMA((2,)),
+        pltpu.SemaphoreType.DMA((2 * depth,)),
     ]
     out = place(0, yh, own.reshape(by_bin), shape, scratch)
     out, cross = lax.optimization_barrier((out, cross))

time: 101 us -> 100 us (0.990)
  the two profiles are of different devices: /device:TPU:7 before, /device:TPU:15 now
where the time goes in v9:
time: 100 us; the launch traced here: 99.7 us
  waiting for transfers between devices  39.9 us (40%)
  blocking collectives  36.4 us (36%)
  starting transfers between devices  14.7 us (15%)
  Pallas kernels  8.57 us (9%)
    all_to_all x1, blocking collectives, shards(): mine = lax.all_to_all(scaled, ('zh', 'c', 'y', 'x'), 0, 0, tiled=True)  36.4 us
    all_to_all x1, waiting for transfers between devices, shards(): cross = lax.all_to_all(cross, ('zh', 'zl'), 0, 0, tiled=True)  16.9 us
    ppermute x1, waiting for transfers between devices, shards(): far = lax.ppermute(mine, 'yh', SWAP)  13.2 us
    ppermute x1, waiting for transfers between devices, shards(): near = lax.ppermute(mine, 'zl', SWAP)  6.72 us
    ppermute x1, starting transfers between devices, shards(): far = lax.ppermute(mine, 'yh', SWAP)  4.76 us
    all_to_all x1, starting transfers between devices, shards(): own = lax.all_to_all(own, ('zh', 'zl'), 0, 0, tiled=True)  3.49 us
    all_to_all x1, starting transfers between devices, shards(): cross = lax.all_to_all(cross, ('zh', 'zl'), 0, 0, tiled=True)  3.49 us
    all_to_all x1, waiting for transfers between devices, shards(): own = lax.all_to_all(own, ('zh', 'zl'), 0, 0, tiled=True)  3.11 us
  transfers between devices with their start and end apart: 4, of which 4 were waited for; matrix products, arithmetic and copies ran while one was open for 0% of the time, Pallas kernels for 5%

profile of v9, /device:TPU:15, one launch (start us, length us, event | category | flops | bytes accessed | tf_op | source)
XLA Modules:
  0.0 99.7 jit_solution(2551117655306969295)
XLA Ops:
  0.0 2.6 %shard_map.28 = bf16[4,2,16,16,128]{4,3,2,1,0:T(8,128)(2,1)} custom-call(f32[16]{0:T(128)} %weight_hbm.1, bf16[2,16,64,128]{3,2,1,0:T(8,128)(2,1)} %bitcast.15), custom_call_target="tpu_custom_call" | custom-call | bytes 1048576 | tf_op jit(solution)/shard_map/pallas_call | solution.py:174
  2.6 36.4 %all_to_all.15 = bf16[128,16,128]{2,1,0:T(8,128)(2,1)S(1)} all-to-all(bf16[128,16,128]{2,1,0:T(8,128)(2,1)} %bitcast.14), channel_id=1, replica_groups=mesh['y'=4,'x'=4,'c'=2,'yh'=2,'zh'=4,'zl'=2] {'zh','c','y','x'}, dimensions={0} | all-to-all | bytes 1048576 | tf_op jit(solution)/shard_map/all_to_all | solution.py:188
  39.0 3.0 %collective-permute-start = (bf16[128,16,128]{2,1,0:T(8,128)(2,1)S(1)}, bf16[128,16,128]{2,1,0:T(8,128)(2,1)S(1)}, u32[]{:S(2)}, u32[]{:S(2)}) collective-permute-start(bf16[128,16,128]{2,1,0:T(8,128)(2,1)S(1)} %all_to_all.15), channel_id=1, source_target_pairs={{0,1},{1,0},{2,3},{3,2},{4,5},{5,4},{6,7},{7,6},{8,9},{9,8},{10,11... | collective-permute-start | bytes 1572872 | tf_op jit(solution)/shard_map/ppermute | solution.py:189
  42.0 4.8 %collective-permute-start.1 = (bf16[128,16,128]{2,1,0:T(8,128)(2,1)S(1)}, bf16[128,16,128]{2,1,0:T(8,128)(2,1)S(1)}, u32[]{:S(2)}, u32[]{:S(2)}) collective-permute-start(bf16[128,16,128]{2,1,0:T(8,128)(2,1)S(1)} %all_to_all.15), channel_id=1, source_target_pairs={{0,8},{8,0},{1,9},{9,1},{2,10},{10,2},{3,11},{11,3},{4,12},{12,4},... | collective-permute-start | bytes 1572872 | tf_op jit(solution)/shard_map/ppermute | solution.py:190
  46.8 0.9 shard_map.29
  47.7 6.7 %collective-permute-done = bf16[128,16,128]{2,1,0:T(8,128)(2,1)S(1)} collective-permute-done((bf16[128,16,128]{2,1,0:T(8,128)(2,1)S(1)}, bf16[128,16,128]{2,1,0:T(8,128)(2,1)S(1)}, u32[]{:S(2)}, u32[]{:S(2)}) %collective-permute-start) | collective-permute-done | bytes 524320 | tf_op jit(solution)/shard_map/ppermute | solution.py:189
  54.4 1.5 %shard_map.30 = (bf16[8,64,512]{2,1,0:T(8,128)(2,1)}, bf16[256,1024]{1,0:T(8,128)(2,1)S(1)}) custom-call(s32[1]{0:T(128)} %bitcast.1.zl_ref, bf16[4,512,128]{2,1,0:T(8,128)(2,1)S(1)} %bitcast.12, bf16[1024,512]{1,0:T(8,128)(2,1)S(1)} %get-tuple-element.14.right_ref, bf16[4,64,512]{2,1,0:T(8,128)(2,1)S(1)} %get-tuple-element.15.begun_ref), custom_call_target="tpu_custom_call" | custom-call | flops 268435456 | tf_op jit(solution)/shard_map/pallas_call | solution.py:202
  55.9 3.5 %all-to-all-start.1 = ((bf16[8,64,512]{2,1,0:T(8,128)(2,1)}), bf16[8,64,512]{2,1,0:T(8,128)(2,1)S(1)}, u32[]{:S(2)}, u32[]{:S(2)}) async-start(bf16[8,64,512]{2,1,0:T(8,128)(2,1)} %get-tuple-element.16), calls=%async_computation.1 | async-start | bytes 1048576 | tf_op jit(solution)/shard_map/all_to_all | solution.py:208
  59.4 13.2 %collective-permute-done.1 = bf16[128,16,128]{2,1,0:T(8,128)(2,1)S(1)} collective-permute-done((bf16[128,16,128]{2,1,0:T(8,128)(2,1)S(1)}, bf16[128,16,128]{2,1,0:T(8,128)(2,1)S(1)}, u32[]{:S(2)}, u32[]{:S(2)}) %collective-permute-start.1) | collective-permute-done | bytes 524320 | tf_op jit(solution)/shard_map/ppermute | solution.py:190
  72.6 1.7 %shard_map.31 = bf16[8,64,512]{2,1,0:T(8,128)(2,1)} custom-call(s32[1]{0:T(128)} %bitcast.1.zl_ref, bf16[256,1024]{1,0:T(8,128)(2,1)S(1)} %get-tuple-element.17.left_ref, bf16[256,1024]{1,0:T(8,128)(2,1)S(1)} %get-tuple-element.18.left_near_ref, bf16[4,512,128]{2,1,0:T(8,128)(2,1)S(1)} %bitcast.13), custom_call_target="tpu_custom_call" | custom-call | flops 21474836480 | bytes 2097152 | tf_op jit(solution)/shard_map/pallas_call | solution.py:210
  74.3 3.1 %all-to-all-done.1 = bf16[8,64,512]{2,1,0:T(8,128)(2,1)S(1)} async-done(((bf16[8,64,512]{2,1,0:T(8,128)(2,1)}), bf16[8,64,512]{2,1,0:T(8,128)(2,1)S(1)}, u32[]{:S(2)}, u32[]{:S(2)}) %all-to-all-start.1) | async-done | bytes 524320 | tf_op jit(solution)/shard_map/all_to_all | solution.py:208
  77.4 3.5 %all-to-all-start.2 = ((bf16[8,64,512]{2,1,0:T(8,128)(2,1)}), bf16[8,64,512]{2,1,0:T(8,128)(2,1)S(1)}, u32[]{:S(2)}, u32[]{:S(2)}) async-start(bf16[8,64,512]{2,1,0:T(8,128)(2,1)} %shard_map.31), calls=%async_computation.2 | async-start | bytes 1048576 | tf_op jit(solution)/shard_map/all_to_all | solution.py:219
  80.9 0.9 shard_map.32.refs_0_
  81.8 16.9 %all-to-all-done.2 = bf16[8,64,512]{2,1,0:T(8,128)(2,1)S(1)} async-done(((bf16[8,64,512]{2,1,0:T(8,128)(2,1)}), bf16[8,64,512]{2,1,0:T(8,128)(2,1)S(1)}, u32[]{:S(2)}, u32[]{:S(2)}) %all-to-all-start.2) | async-done | bytes 524320 | tf_op jit(solution)/shard_map/all_to_all | solution.py:219
  98.8 0.9 shard_map.33
Async XLA Ops:
  39.0 15.4 %collective-permute-start = (bf16[128,16,128]{2,1,0:T(8,128)(2,1)S(1)}, bf16[128,16,128]{2,1,0:T(8,128)(2,1)S(1)}, u32[]{:S(2)}, u32[]{:S(2)}) collective-permute-start(bf16[128,16,128]{2,1,0:T(8,128)(2,1)S(1)} %all_to_all.15), channel_id=1, source_target_pairs={{0,1},{1,0},{2,3},{3,2},{4,5},{5,4},{6,7},{7,6},{8,9},{9,8},{10,11... | collective-permute-start | bytes 1572872 | tf_op jit(solution)/shard_map/ppermute | solution.py:189
  42.0 30.6 %collective-permute-start.1 = (bf16[128,16,128]{2,1,0:T(8,128)(2,1)S(1)}, bf16[128,16,128]{2,1,0:T(8,128)(2,1)S(1)}, u32[]{:S(2)}, u32[]{:S(2)}) collective-permute-start(bf16[128,16,128]{2,1,0:T(8,128)(2,1)S(1)} %all_to_all.15), channel_id=1, source_target_pairs={{0,8},{8,0},{1,9},{9,1},{2,10},{10,2},{3,11},{11,3},{4,12},{12,4},... | collective-permute-start | bytes 1572872 | tf_op jit(solution)/shard_map/ppermute | solution.py:190
  55.9 21.4 %all-to-all-start.1 = ((bf16[8,64,512]{2,1,0:T(8,128)(2,1)}), bf16[8,64,512]{2,1,0:T(8,128)(2,1)S(1)}, u32[]{:S(2)}, u32[]{:S(2)}) async-start(bf16[8,64,512]{2,1,0:T(8,128)(2,1)} %get-tuple-element.16), calls=%async_computation.1 | async-start | bytes 1048576 | tf_op jit(solution)/shard_map/all_to_all | solution.py:208
  77.4 21.4 %all-to-all-start.2 = ((bf16[8,64,512]{2,1,0:T(8,128)(2,1)}), bf16[8,64,512]{2,1,0:T(8,128)(2,1)S(1)}, u32[]{:S(2)}, u32[]{:S(2)}) async-start(bf16[8,64,512]{2,1,0:T(8,128)(2,1)} %shard_map.31), calls=%async_computation.2 | async-start | bytes 1048576 | tf_op jit(solution)/shard_map/all_to_all | solution.py:219

commit v10 on v9

--- a/solution.py
+++ b/solution.py
@@ -10,7 +10,7 @@
 VMEM = pltpu.MemorySpace.VMEM
 SMEM = pltpu.MemorySpace.SMEM
 HBM = pltpu.MemorySpace.HBM
-STEPS = 4
+STEPS = 8
 PARAMS = pltpu.CompilerParams(vmem_limit_bytes=32 * 1024 * 1024)
 
 

time: 100 us -> 100 us (level)
  no operation moved by 1% of the time
where the time goes in v10:
time: 100 us; the launch traced here: 99.9 us
  waiting for transfers between devices  39.9 us (40%)
  blocking collectives  36.4 us (36%)
  starting transfers between devices  14.7 us (15%)
  Pallas kernels  8.79 us (9%)
    all_to_all x1, blocking collectives, shards(): mine = lax.all_to_all(scaled, ('zh', 'c', 'y', 'x'), 0, 0, tiled=True)  36.4 us
    all_to_all x1, waiting for transfers between devices, shards(): cross = lax.all_to_all(cross, ('zh', 'zl'), 0, 0, tiled=True)  16.9 us
    ppermute x1, waiting for transfers between devices, shards(): far = lax.ppermute(mine, 'yh', SWAP)  13.2 us
    ppermute x1, waiting for transfers between devices, shards(): near = lax.ppermute(mine, 'zl', SWAP)  6.72 us
    ppermute x1, starting transfers between devices, shards(): far = lax.ppermute(mine, 'yh', SWAP)  4.76 us
    all_to_all x1, starting transfers between devices, shards(): own = lax.all_to_all(own, ('zh', 'zl'), 0, 0, tiled=True)  3.49 us
    all_to_all x1, starting transfers between devices, shards(): cross = lax.all_to_all(cross, ('zh', 'zl'), 0, 0, tiled=True)  3.49 us
    all_to_all x1, waiting for transfers between devices, shards(): own = lax.all_to_all(own, ('zh', 'zl'), 0, 0, tiled=True)  3.11 us
  transfers between devices with their start and end apart: 4, of which 4 were waited for; matrix products, arithmetic and copies ran while one was open for 0% of the time, Pallas kernels for 5%

profile of v10, /device:TPU:15, one launch (start us, length us, event | category | flops | bytes accessed | tf_op | source)
XLA Modules:
  0.0 99.9 jit_solution(18388820461986699926)
XLA Ops:
  0.0 2.9 %shard_map.28 = bf16[4,2,16,16,128]{4,3,2,1,0:T(8,128)(2,1)} custom-call(f32[16]{0:T(128)} %weight_hbm.1, bf16[2,16,64,128]{3,2,1,0:T(8,128)(2,1)} %bitcast.15), custom_call_target="tpu_custom_call" | custom-call | bytes 1048576 | tf_op jit(solution)/shard_map/pallas_call | solution.py:174
  2.9 36.4 %all_to_all.15 = bf16[128,16,128]{2,1,0:T(8,128)(2,1)S(1)} all-to-all(bf16[128,16,128]{2,1,0:T(8,128)(2,1)} %bitcast.14), channel_id=1, replica_groups=mesh['y'=4,'x'=4,'c'=2,'yh'=2,'zh'=4,'zl'=2] {'zh','c','y','x'}, dimensions={0} | all-to-all | bytes 1048576 | tf_op jit(solution)/shard_map/all_to_all | solution.py:188
  39.2 3.0 %collective-permute-start = (bf16[128,16,128]{2,1,0:T(8,128)(2,1)S(1)}, bf16[128,16,128]{2,1,0:T(8,128)(2,1)S(1)}, u32[]{:S(2)}, u32[]{:S(2)}) collective-permute-start(bf16[128,16,128]{2,1,0:T(8,128)(2,1)S(1)} %all_to_all.15), channel_id=1, source_target_pairs={{0,1},{1,0},{2,3},{3,2},{4,5},{5,4},{6,7},{7,6},{8,9},{9,8},{10,11... | collective-permute-start | bytes 1572872 | tf_op jit(solution)/shard_map/ppermute | solution.py:189
  42.3 4.8 %collective-permute-start.1 = (bf16[128,16,128]{2,1,0:T(8,128)(2,1)S(1)}, bf16[128,16,128]{2,1,0:T(8,128)(2,1)S(1)}, u32[]{:S(2)}, u32[]{:S(2)}) collective-permute-start(bf16[128,16,128]{2,1,0:T(8,128)(2,1)S(1)} %all_to_all.15), channel_id=1, source_target_pairs={{0,8},{8,0},{1,9},{9,1},{2,10},{10,2},{3,11},{11,3},{4,12},{12,4},... | collective-permute-start | bytes 1572872 | tf_op jit(solution)/shard_map/ppermute | solution.py:190
  47.0 0.9 shard_map.29
  47.9 6.7 %collective-permute-done = bf16[128,16,128]{2,1,0:T(8,128)(2,1)S(1)} collective-permute-done((bf16[128,16,128]{2,1,0:T(8,128)(2,1)S(1)}, bf16[128,16,128]{2,1,0:T(8,128)(2,1)S(1)}, u32[]{:S(2)}, u32[]{:S(2)}) %collective-permute-start) | collective-permute-done | bytes 524320 | tf_op jit(solution)/shard_map/ppermute | solution.py:189
  54.6 1.5 %shard_map.30 = (bf16[8,64,512]{2,1,0:T(8,128)(2,1)}, bf16[256,1024]{1,0:T(8,128)(2,1)S(1)}) custom-call(s32[1]{0:T(128)} %bitcast.1.zl_ref, bf16[4,512,128]{2,1,0:T(8,128)(2,1)S(1)} %bitcast.12, bf16[1024,512]{1,0:T(8,128)(2,1)S(1)} %get-tuple-element.14.right_ref, bf16[4,64,512]{2,1,0:T(8,128)(2,1)S(1)} %get-tuple-element.15.begun_ref), custom_call_target="tpu_custom_call" | custom-call | flops 268435456 | tf_op jit(solution)/shard_map/pallas_call | solution.py:202
  56.2 3.5 %all-to-all-start.1 = ((bf16[8,64,512]{2,1,0:T(8,128)(2,1)}), bf16[8,64,512]{2,1,0:T(8,128)(2,1)S(1)}, u32[]{:S(2)}, u32[]{:S(2)}) async-start(bf16[8,64,512]{2,1,0:T(8,128)(2,1)} %get-tuple-element.16), calls=%async_computation.1 | async-start | bytes 1048576 | tf_op jit(solution)/shard_map/all_to_all | solution.py:208
  59.7 13.2 %collective-permute-done.1 = bf16[128,16,128]{2,1,0:T(8,128)(2,1)S(1)} collective-permute-done((bf16[128,16,128]{2,1,0:T(8,128)(2,1)S(1)}, bf16[128,16,128]{2,1,0:T(8,128)(2,1)S(1)}, u32[]{:S(2)}, u32[]{:S(2)}) %collective-permute-start.1) | collective-permute-done | bytes 524320 | tf_op jit(solution)/shard_map/ppermute | solution.py:190
  72.8 1.7 %shard_map.31 = bf16[8,64,512]{2,1,0:T(8,128)(2,1)} custom-call(s32[1]{0:T(128)} %bitcast.1.zl_ref, bf16[256,1024]{1,0:T(8,128)(2,1)S(1)} %get-tuple-element.17.left_ref, bf16[256,1024]{1,0:T(8,128)(2,1)S(1)} %get-tuple-element.18.left_near_ref, bf16[4,512,128]{2,1,0:T(8,128)(2,1)S(1)} %bitcast.13), custom_call_target="tpu_custom_call" | custom-call | flops 21474836480 | bytes 2097152 | tf_op jit(solution)/shard_map/pallas_call | solution.py:210
  74.5 3.1 %all-to-all-done.1 = bf16[8,64,512]{2,1,0:T(8,128)(2,1)S(1)} async-done(((bf16[8,64,512]{2,1,0:T(8,128)(2,1)}), bf16[8,64,512]{2,1,0:T(8,128)(2,1)S(1)}, u32[]{:S(2)}, u32[]{:S(2)}) %all-to-all-start.1) | async-done | bytes 524320 | tf_op jit(solution)/shard_map/all_to_all | solution.py:208
  77.6 3.5 %all-to-all-start.2 = ((bf16[8,64,512]{2,1,0:T(8,128)(2,1)}), bf16[8,64,512]{2,1,0:T(8,128)(2,1)S(1)}, u32[]{:S(2)}, u32[]{:S(2)}) async-start(bf16[8,64,512]{2,1,0:T(8,128)(2,1)} %shard_map.31), calls=%async_computation.2 | async-start | bytes 1048576 | tf_op jit(solution)/shard_map/all_to_all | solution.py:219
  81.1 0.9 shard_map.32.refs_0_
  82.1 16.9 %all-to-all-done.2 = bf16[8,64,512]{2,1,0:T(8,128)(2,1)S(1)} async-done(((bf16[8,64,512]{2,1,0:T(8,128)(2,1)}), bf16[8,64,512]{2,1,0:T(8,128)(2,1)S(1)}, u32[]{:S(2)}, u32[]{:S(2)}) %all-to-all-start.2) | async-done | bytes 524320 | tf_op jit(solution)/shard_map/all_to_all | solution.py:219
  99.0 0.9 shard_map.33
Async XLA Ops:
  39.2 15.4 %collective-permute-start = (bf16[128,16,128]{2,1,0:T(8,128)(2,1)S(1)}, bf16[128,16,128]{2,1,0:T(8,128)(2,1)S(1)}, u32[]{:S(2)}, u32[]{:S(2)}) collective-permute-start(bf16[128,16,128]{2,1,0:T(8,128)(2,1)S(1)} %all_to_all.15), channel_id=1, source_target_pairs={{0,1},{1,0},{2,3},{3,2},{4,5},{5,4},{6,7},{7,6},{8,9},{9,8},{10,11... | collective-permute-start | bytes 1572872 | tf_op jit(solution)/shard_map/ppermute | solution.py:189
  42.3 30.6 %collective-permute-start.1 = (bf16[128,16,128]{2,1,0:T(8,128)(2,1)S(1)}, bf16[128,16,128]{2,1,0:T(8,128)(2,1)S(1)}, u32[]{:S(2)}, u32[]{:S(2)}) collective-permute-start(bf16[128,16,128]{2,1,0:T(8,128)(2,1)S(1)} %all_to_all.15), channel_id=1, source_target_pairs={{0,8},{8,0},{1,9},{9,1},{2,10},{10,2},{3,11},{11,3},{4,12},{12,4},... | collective-permute-start | bytes 1572872 | tf_op jit(solution)/shard_map/ppermute | solution.py:190
  56.2 21.4 %all-to-all-start.1 = ((bf16[8,64,512]{2,1,0:T(8,128)(2,1)}), bf16[8,64,512]{2,1,0:T(8,128)(2,1)S(1)}, u32[]{:S(2)}, u32[]{:S(2)}) async-start(bf16[8,64,512]{2,1,0:T(8,128)(2,1)} %get-tuple-element.16), calls=%async_computation.1 | async-start | bytes 1048576 | tf_op jit(solution)/shard_map/all_to_all | solution.py:208
  77.6 21.4 %all-to-all-start.2 = ((bf16[8,64,512]{2,1,0:T(8,128)(2,1)}), bf16[8,64,512]{2,1,0:T(8,128)(2,1)S(1)}, u32[]{:S(2)}, u32[]{:S(2)}) async-start(bf16[8,64,512]{2,1,0:T(8,128)(2,1)} %shard_map.31), calls=%async_computation.2 | async-start | bytes 1048576 | tf_op jit(solution)/shard_map/all_to_all | solution.py:219
